TPU v7x, 256 devices: a whole 4x4x8 slice. The times are simulated.
256 devices in a mesh: dp: 64 (over x, z_hi, y, core), group: 4 (over z_lo).
Axes of the slice: x: 4, y: 4, z: 8 (z_hi: 2, z_lo: 4; z = z_hi * 4 + z_lo), core: 2. Of those that a mesh axis runs over, the one named last changes fastest.
Arguments:
- activations: bfloat16 [65536, 4096], P('dp', 'group'), may hold values from -36 to 36
- output_grads: bfloat16 [65536, 8192], P(('dp', 'group')), may hold values from -36 to 36
- token_counts: int32 [64], replicated, may hold values from 513 to 1024, as said below
- owner_blocks: int32 [64], replicated, may hold values from 0 to 63, each once
- basis_in: bfloat16 [4, 1024, 1024], P('group', 'dp'), may hold values from -0.1875 to 0.1875
- basis_out: bfloat16 [64, 128, 128], P('dp'), may hold values from -0.5 to 0.5
- values_in: float32 [4096], P('group'), may hold values from 0.1 to 1
- values_out: float32 [8192], P('dp'), may hold values from 0.1 to 1
- gradient: bfloat16 [4096, 8192], P('group', 'dp'), may hold values from -3500 to 3500
- learning_rate: float32 [1], replicated, may hold values from 3e-06 to 1.2e-05
Outputs:
- cov_in: float32 [4, 1024, 1024], P('group', 'dp')
- cov_out: float32 [64, 128, 128], P('dp', 'group')
- update: float32 [4096, 8192], P('group', 'dp')
Inputs may be any that keep to these rules, and one draw needn't show every extreme that they name: `token_counts`: each shard counts at least half of its 1024 tokens; some shard counts all of them and some shard exactly 513. `owner_blocks`: each block number appears once.
All inputs are finite; a program needn't handle non-finite values.
Results may differ from a plain program's by a relative error of at most 0.0026.
The roundings to bfloat16 on the way count: a program that leaves them out, or rounds other values in their place, can miss the bound.
Values may be sent and summed in bfloat16 or wider, within the bound.
No kernel may reach another device: no remote copies, remote signals or barrier semaphores. Data moves between devices by JAX's collectives and lax.ppermute only.
A program may use at most 64 MiB of HBM per device.

v0:
```python
import jax
import jax.numpy as jnp
from jax import lax
from jax.sharding import PartitionSpec as P

damping = 0.03
kl_clip = 0.001


def finish_rotation(scaled, q_out, full_basis):
    back_rot = lax.dot_general(
        scaled, q_out, (((1,), (1,)), ((), ())), preferred_element_type=jnp.float32
    ).astype(jnp.bfloat16)
    return jnp.dot(full_basis, back_rot, preferred_element_type=jnp.float32)


def local(
    activations,
    output_grads,
    token_counts,
    owner_blocks,
    basis_in,
    basis_out,
    values_in,
    values_out,
    gradient,
    learning_rate,
):
    dp_index = lax.axis_index("dp")
    group_index = lax.axis_index("group")
    token_total = jnp.sum(token_counts).astype(jnp.float32)
    own_count = lax.dynamic_slice_in_dim(token_counts, dp_index, 1)[0]
    tok_rows, block_in = activations.shape
    live_rows = jnp.arange(tok_rows, dtype=jnp.int32) < own_count
    in_masked = jnp.where(live_rows[:, None], activations, jnp.zeros((), jnp.bfloat16))
    in_share = lax.psum_scatter(
        lax.dot_general(
            in_masked, in_masked, (((0,), (0,)), ((), ())), preferred_element_type=jnp.float32
        ),
        "dp",
        scatter_dimension=0,
        tiled=True,
    )
    cov_in = (in_share / token_total)[None]
    quarter, width_out = output_grads.shape
    block_out = basis_out.shape[1]
    first_token = group_index * quarter
    live_out = first_token + jnp.arange(quarter, dtype=jnp.int32) < own_count
    out_masked = jnp.where(live_out[:, None], output_grads, jnp.zeros((), jnp.bfloat16))
    blocked = out_masked.reshape(quarter, width_out // block_out, block_out)
    ordered = jnp.take(blocked, owner_blocks, axis=1)
    partial_value = jnp.einsum("tbi,tbj->bij", ordered, ordered, preferred_element_type=jnp.float32)
    row_share = lax.psum_scatter(
        partial_value.reshape(-1, block_out), ("dp", "group"), scatter_dimension=0, tiled=True
    )
    cov_out = (row_share / token_total)[None]
    full_basis = lax.all_gather(basis_in, "dp", axis=1, tiled=True)[0]
    q_out = basis_out[0]
    rotated = lax.dot_general(
        full_basis, gradient, (((0,), (0,)), ((), ())), preferred_element_type=jnp.float32
    ).astype(jnp.bfloat16)
    spectral = jnp.dot(rotated, q_out, preferred_element_type=jnp.float32)
    scaled = (spectral / (values_in[:, None] * values_out[None, :] + damping)).astype(jnp.bfloat16)
    precond = finish_rotation(scaled, q_out, full_basis)
    inner = lax.psum(jnp.sum(precond * gradient.astype(jnp.float32)), ("dp", "group"))
    clip_factor = jnp.minimum(
        1.0, jnp.sqrt(kl_clip / (learning_rate[0] * learning_rate[0] * inner))
    )
    update = clip_factor * precond
    return (cov_in, cov_out, update)


def solution(mesh):
    placed = (
        P("dp", "group"),
        P(("dp", "group"), None),
        P(),
        P(),
        P("group", "dp", None),
        P("dp", None, None),
        P("group"),
        P("dp"),
        P("group", "dp"),
        P(),
    )
    return jax.shard_map(
        local,
        mesh=mesh,
        in_specs=placed,
        out_specs=(P("group", "dp", None), P("dp", "group", None), P("group", "dp")),
        check_vma=False,
    )
```

profile of v0, /device:TPU:1, one launch (start us, length us, event | category | flops | bytes accessed | tf_op | source)
XLA Modules:
  0.0 1740.0 jit_solution(11156140195017795612)
XLA Ops:
  8.1 0.7 all-gather.2.cloned.1.call-update
  8.7 0.0 reduce-scatter.5.cloned.1.call-start
  8.8 6.4 copy.19
  15.2 0.6 dynamic_slice.3
  15.8 0.7 add_compare_fusion
  16.5 4.4 broadcast_select_fusion
  20.9 6.4 copy.20
  27.3 5.3 gather_fusion
  32.6 7.0 fusion
  39.6 0.0 reduce-scatter.3.cloned.1.call-start
  39.7 0.8 iota_compare_fusion
  40.5 0.7 copy-done.3
  41.2 4.5 fusion.9
  45.7 0.6 reduce_sum.18
  47.0 0.1 copy.22
  47.8 51.9 %all-gather.2.cloned.1.call-done = bf16[1,1024,1024]{2,1,0:T(8,128)(2,1)} async-done(((bf16[1,16,1024]{2,1,0:T(8,128)(2,1)}), bf16[1,1024,1024]{2,1,0:T(8,128)(2,1)}) %all-gather.2.cloned.1.call-update) | async-done | bytes 2097168 | tf_op jit(solution)/shard_map/all_gather | solution.py:57
  99.7 2.6 fusion.15
  102.3 1.6 multiply_reduce_fusion
  103.9 74.5 %psum.7 = f32[]{:T(128)} all-reduce(f32[]{:T(128)} %get-tuple-element.12), channel_id=1, replica_groups=mesh['dp'=64,'group'=4] {'dp','group'}, use_global_device_ids=true, to_apply=%region_4.5 | all-reduce | flops 1 | bytes 8 | tf_op jit(solution)/shard_map/psum | solution.py:65
  179.2 1.0 copy.23
  180.2 1134.9 %reduce-scatter.5.cloned.1.call-done = f32[32,128]{1,0:T(8,128)} async-done(((f32[8192,128]{1,0:T(8,128)}), f32[32,128]{1,0:T(8,128)}) %reduce-scatter.5.cloned.1.call-update) | async-done | bytes 16400 | tf_op jit(solution)/shard_map/reduce_scatter | solution.py:53
  1315.1 1.3 divide_bitcast_fusion.1
  1316.4 414.7 %reduce-scatter.3.cloned.1.call-done = f32[16,1024]{1,0:T(8,128)} async-done(((f32[1024,1024]{1,0:T(8,128)}), f32[16,1024]{1,0:T(8,128)}) %reduce-scatter.3.cloned.1.call-update) | async-done | bytes 65552 | tf_op jit(solution)/shard_map/reduce_scatter | solution.py:36
  1731.1 1.5 divide_bitcast_fusion
  (22 shorter events, 0.2 us)
Async XLA Ops:
  8.0 91.7 %copy-start = (bf16[1,128,128]{2,1,0:T(8,128)(2,1)S(1)}, bf16[1,128,128]{2,1,0:T(8,128)(2,1)}, u32[]{:S(2)}) copy-start(bf16[1,128,128]{2,1,0:T(8,128)(2,1)} %param.15) | copy-start | bytes 98308
  8.0 91.6 %all-gather.2.cloned.1.call-start = ((), (), s32[]{:S(2)}) async-start(), calls=%async_computation.4 | async-start | bytes 2129920 | tf_op jit(solution)/shard_map/all_gather | solution.py:57
  8.7 1306.3 %reduce-scatter.5.cloned.1.call-start = ((), (), s32[]{:S(2)}) async-start(), calls=%async_computation.3 | async-start | bytes 4210688 | tf_op jit(solution)/shard_map/reduce_scatter | solution.py:53
  8.8 6.4 copy-start.6
  20.9 6.4 copy-start.5
  39.6 1.6 copy-start.3
  39.6 1691.5 %reduce-scatter.3.cloned.1.call-start = ((), (), s32[]{:S(2)}) async-start(), calls=%async_computation.2 | async-start | bytes 4259840 | tf_op jit(solution)/shard_map/reduce_scatter | solution.py:36
  45.7 1.3 copy-start.2
  45.7 54.0 %copy-start.4 = (f32[1024]{0:T(1024)S(1)}, f32[1024]{0:T(1024)}, u32[]{:S(2)}) copy-start(f32[1024]{0:T(1024)} %param.16) | copy-start | bytes 12292
  45.7 54.0 %copy-start.7 = (f32[128]{0:T(128)S(1)}, f32[128]{0:T(128)}, u32[]{:S(2)}) copy-start(f32[128]{0:T(128)} %param.17) | copy-start | bytes 1540
  99.7 2.7 copy-start.1
Sparse Core Ops, SparseCore 0:
  12.4 87.1 all-gather.1
Sparse Core Ops, SparseCore 1:
  39.7 1275.3 reduce-scatter.4
  1317.6 413.4 reduce-scatter.2
where the time goes:
time: 1750 us; the launch traced here: 1740 us
  waiting for transfers between devices  1600 us (91%)
  blocking collectives  74.5 us (4%)
  local copies, waits for them, and re-layouts  20.5 us (1%)
  between operations  17.6 us (1%)
    reduce_scatter x1, waiting for transfers between devices, local(): lax.psum_scatter(partial_value.reshape(-1, block_out), ('dp', 'group'), s...  1130 us
    reduce_scatter x1, waiting for transfers between devices, local(): lax.psum_scatter(lax.dot_general(in_masked, in_masked, (((0,), (0,)), (()...  415 us
    psum x1, blocking collectives, local(): lax.psum(jnp.sum(precond * gradient.astype(jnp.float32)), ('dp', 'group'))  74.5 us
    all_gather x1, waiting for transfers between devices, local(): full_basis = lax.all_gather(basis_in, 'dp', axis=1, tiled=True)[0]  51.9 us
  transfers between devices with their start and end apart: 3, of which 3 were waited for; matrix products, arithmetic and copies ran while one was open for 2% of the time, Pallas kernels for 0%

commit v1 on v0

v1 whole, which is shorter than its diff:
```python
import jax
import jax.numpy as jnp
from jax import lax
from jax.experimental import pallas as pl
from jax.experimental.pallas import tpu as pltpu
from jax.sharding import Mesh, PartitionSpec as P

damping = 0.03
kl_clip = 0.001
f32 = jnp.float32
bf16 = jnp.bfloat16

AXES = ("x", "zh", "y", "core", "zl")
SIZES = (4, 2, 4, 2, 4)
DP = ("x", "zh", "y", "core")
PLANE = ("x", "y")
COLUMN = ("zh", "zl")
VMEM = 40 << 20

ROWS_IN = 256
ROWS_OUT = 128
ROWS_EXTRA = 16
ROWS = ROWS_IN + ROWS_OUT + ROWS_EXTRA


def dot(a, b, ca, cb):
    return lax.dot_general(a, b, (((ca,), (cb,)), ((), ())), preferred_element_type=f32)


def cov_out_kernel(owners, meta, *refs):
    blocks, (send, keep) = refs[:8], refs[8:]
    live = meta[1]
    rows = lax.broadcasted_iota(jnp.int32, blocks[0].shape, 0) < live
    for y in range(4):
        for src, dst in ((blocks[y], keep), (blocks[4 + y], send)):
            full = src[...]
            masked = jnp.where(rows, full, jnp.zeros((), bf16))
            dst[y] = dot(masked, full, 0, 0)


def cov_out_partial(output_grads, owners, meta):
    quarter = output_grads.shape[0]

    def at(y, other):
        def index(s, owners, meta):
            core = 1 - meta[0] if other else meta[0]
            return (0, owners[(s * 4 + y) * 2 + core])

        return pl.BlockSpec((quarter, 128), index)

    out = pl.BlockSpec((4, 128, 128), lambda s, owners, meta: (s, 0, 0))
    return pl.pallas_call(
        cov_out_kernel,
        grid_spec=pltpu.PrefetchScalarGridSpec(
            num_scalar_prefetch=2,
            grid=(8,),
            in_specs=[at(y, False) for y in range(4)] + [at(y, True) for y in range(4)],
            out_specs=[out, out],
        ),
        out_shape=[jax.ShapeDtypeStruct((32, 128, 128), f32)] * 2,
        compiler_params=pltpu.CompilerParams(vmem_limit_bytes=VMEM),
        cost_estimate=pl.CostEstimate(
            flops=2 * quarter * 8192 * 128, bytes_accessed=quarter * 8192 * 2 + (4 << 20), transcendentals=0
        ),
        name="cov_out_partial",
    )(owners, meta, *([output_grads] * 8))


def cov_in_kernel(meta, lhs, rhs, send, keep):
    first = meta[0] == 0
    rows = lax.broadcasted_iota(jnp.int32, lhs.shape, 0) < meta[2]
    masked = jnp.where(rows, lhs[...], jnp.zeros((), bf16))
    part = dot(masked, rhs[...], 0, 0).reshape(8, 2, 16, 1024)
    keep[...] = jnp.where(first, part[:, 0], part[:, 1])
    send[...] = jnp.where(first, part[:, 1], part[:, 0])


def cov_in_partial(activations, meta):
    tok = activations.shape[0]
    out = pl.BlockSpec((8, 16, 1024), lambda s, meta: (s, 0, 0))
    return pl.pallas_call(
        cov_in_kernel,
        grid_spec=pltpu.PrefetchScalarGridSpec(
            num_scalar_prefetch=1,
            grid=(4,),
            in_specs=[
                pl.BlockSpec((tok, 256), lambda s, meta: (0, s)),
                pl.BlockSpec((tok, 1024), lambda s, meta: (0, 0)),
            ],
            out_specs=[out, out],
        ),
        out_shape=[jax.ShapeDtypeStruct((32, 16, 1024), f32)] * 2,
        compiler_params=pltpu.CompilerParams(vmem_limit_bytes=VMEM),
        cost_estimate=pl.CostEstimate(
            flops=2 * tok * 1024 * 1024, bytes_accessed=tok * 4096 + (4 << 20), transcendentals=0
        ),
        name="cov_in_partial",
    )(meta, activations, activations)


def pack_kernel(keep_out, recv_out, keep_in, recv_in, msg):
    row = lax.broadcasted_iota(jnp.int32, (128, 128), 0)
    col = lax.broadcasted_iota(jnp.int32, (128, 128), 1)
    for y in range(4):
        first = keep_out[0, y] + recv_out[0, y]
        second = keep_out[1, y] + recv_out[1, y]
        msg[y, ROWS_IN : ROWS_IN + ROWS_OUT] = jnp.where(row <= col, first, second).astype(bf16)
        diag = jnp.sum(jnp.where(row == col, second, 0.0), axis=0, keepdims=True)
        top = lax.broadcasted_iota(jnp.int32, (ROWS_EXTRA, 128), 0) == 0
        msg[y, ROWS_IN + ROWS_OUT :] = jnp.where(top, diag, 0.0).astype(bf16)
        for zh in range(2):
            rows = (keep_in[zh, y] + recv_in[zh, y]).astype(bf16)
            for c in range(8):
                msg[y, c * 32 + zh * 16 : c * 32 + zh * 16 + 16] = rows[:, c * 128 : c * 128 + 128]


def pack(keep_out, recv_out, keep_in, recv_in):
    outs = pl.BlockSpec((2, 4, 128, 128), lambda x: (x, 0, 0, 0))
    ins = pl.BlockSpec((2, 4, 16, 1024), lambda x: (x, 0, 0, 0))
    return pl.pallas_call(
        pack_kernel,
        grid=(4,),
        in_specs=[outs, outs, ins, ins],
        out_specs=pl.BlockSpec((4, ROWS, 128), lambda x: (x, 0, 0)),
        out_shape=jax.ShapeDtypeStruct((16, ROWS, 128), bf16),
        compiler_params=pltpu.CompilerParams(vmem_limit_bytes=VMEM),
        cost_estimate=pl.CostEstimate(flops=4 << 20, bytes_accessed=10 << 20, transcendentals=0),
        name="pack",
    )(
        keep_out.reshape(8, 4, 128, 128),
        recv_out.reshape(8, 4, 128, 128),
        keep_in.reshape(8, 4, 16, 1024),
        recv_in.reshape(8, 4, 16, 1024),
    )


def precond_kernel(meta, q_own, q_other, grad, q_out, values_in, values_out, precond, parts, full):
    core, zh = meta[0], meta[3]
    for x in range(4):
        for y in range(4):
            for p in range(2):
                z = zh if p == 0 else 1 - zh
                slab = ((x * 2 + z) * 4 + y) * 2
                for src, c in ((q_own, core), (q_other, 1 - core)):
                    at = pl.multiple_of((slab + c) * 16, 16)
                    full[pl.ds(at, 16), :] = src[x * 4 + y, p * 16 : p * 16 + 16, :]
    basis = full[...]
    g = grad[...]
    q = q_out[...]
    rotated = dot(g, basis, 0, 0).astype(bf16)
    spectral = dot(q, rotated, 0, 0)
    scaled = (spectral / (values_in[...] * values_out[...] + damping)).astype(bf16)
    back_rot = dot(q, scaled, 1, 0).astype(bf16)
    result = dot(basis, back_rot, 1, 1)
    precond[...] = result
    inner = jnp.sum(jnp.sum(result * g.astype(f32), axis=0, keepdims=True), axis=1, keepdims=True)
    high = inner.astype(bf16).astype(f32)
    rest = inner - high
    middle = rest.astype(bf16).astype(f32)
    low = rest - middle
    row = lax.broadcasted_iota(jnp.int32, (16, 128), 0)
    parts[...] = jnp.where(
        row == 1, high, jnp.where(row == 2, middle, jnp.where(row == 3, low, 0.0))
    ).astype(bf16)


def precondition(meta, q_own, q_other, grad, q_out, values_in, values_out):
    whole = pl.BlockSpec(memory_space=pltpu.VMEM)
    return pl.pallas_call(
        precond_kernel,
        in_specs=[pl.BlockSpec(memory_space=pltpu.SMEM)] + [whole] * 6,
        out_specs=[whole, whole],
        out_shape=[jax.ShapeDtypeStruct((1024, 128), f32), jax.ShapeDtypeStruct((16, 128), bf16)],
        scratch_shapes=[pltpu.VMEM((1024, 1024), bf16)],
        compiler_params=pltpu.CompilerParams(vmem_limit_bytes=VMEM),
        cost_estimate=pl.CostEstimate(flops=600 << 20, bytes_accessed=3 << 20, transcendentals=0),
        name="precondition",
    )(meta, q_own, q_other, grad, q_out, values_in, values_out)


def unpack_kernel(meta, msg, column, keep_in, send_in):
    first = meta[3] == 0

    def total(at, rows):
        out = msg[0, at : at + rows].astype(f32)
        for s in range(1, 16):
            out = out + msg[s, at : at + rows].astype(f32)
        return out

    for c in range(8):
        pair = total(c * 32, 32)
        lo, hi = pair[:16], pair[16:]
        keep_in[:, c * 128 : c * 128 + 128] = jnp.where(first, lo, hi)
        send_in[:, c * 128 : c * 128 + 128] = jnp.where(first, hi, lo)
    folded = total(ROWS_IN, ROWS_OUT)
    extra = total(ROWS_IN + ROWS_OUT, ROWS_EXTRA)
    turned = folded.T
    row = lax.broadcasted_iota(jnp.int32, (128, 128), 0)
    col = lax.broadcasted_iota(jnp.int32, (128, 128), 1)
    one = jnp.where(row <= col, folded, turned)
    two = jnp.where(row > col, folded, jnp.where(row == col, extra[0:1], turned))
    inner = jnp.broadcast_to(extra[1:2] + extra[2:3] + extra[3:4], (8, 128))
    for z in range(4):
        column[z, 0:32] = one[z * 32 : z * 32 + 32]
        column[4 + z, 0:32] = two[z * 32 : z * 32 + 32]
        column[z, 32:40] = inner
        column[4 + z, 32:40] = inner


def unpack(meta, msg):
    whole = pl.BlockSpec(memory_space=pltpu.VMEM)
    return pl.pallas_call(
        unpack_kernel,
        in_specs=[pl.BlockSpec(memory_space=pltpu.SMEM), whole],
        out_specs=[whole] * 3,
        out_shape=[
            jax.ShapeDtypeStruct((8, 40, 128), f32),
            jax.ShapeDtypeStruct((16, 1024), f32),
            jax.ShapeDtypeStruct((16, 1024), f32),
        ],
        compiler_params=pltpu.CompilerParams(vmem_limit_bytes=VMEM),
        cost_estimate=pl.CostEstimate(flops=2 << 20, bytes_accessed=2 << 20, transcendentals=0),
        name="unpack",
    )(meta, msg)


def swap(array, axis):
    return lax.ppermute(array, axis, [(0, 1), (1, 0)])


def local(
    activations,
    output_grads,
    token_counts,
    owner_blocks,
    basis_in,
    basis_out,
    values_in,
    values_out,
    gradient,
    learning_rate,
):
    core = lax.axis_index("core").astype(jnp.int32)
    zh = lax.axis_index("zh").astype(jnp.int32)
    zl = lax.axis_index("zl").astype(jnp.int32)
    own_count = lax.dynamic_slice_in_dim(token_counts, lax.axis_index(DP), 1)[0]
    token_total = jnp.sum(token_counts).astype(f32)
    quarter = output_grads.shape[0]
    meta = jnp.stack([core, own_count - zl * quarter, own_count, zh])

    mine = basis_in[0]
    slabs = jnp.concatenate([mine, swap(mine, "zh")], axis=0)

    send_out, keep_out = cov_out_partial(output_grads, owner_blocks, meta)
    recv_out = swap(send_out, "core")
    send_in, keep_in = cov_in_partial(activations, meta)
    recv_in = swap(send_in, "core")

    q_own = lax.all_to_all(
        jnp.broadcast_to(slabs[None], (16,) + slabs.shape), PLANE, 0, 0, tiled=True
    )
    q_other = swap(q_own, "core")
    msg = pack(keep_out, recv_out, keep_in, recv_in)
    precond, parts = precondition(
        meta, q_own, q_other, gradient, basis_out[0], values_in[None, :], values_out[:, None]
    )
    at = ROWS_IN + ROWS_OUT + 1
    msg = lax.dynamic_update_slice(
        msg, jnp.broadcast_to(parts[None, 1:4], (16, 3, 128)), (0, at, 0)
    )
    msg = lax.all_to_all(msg, PLANE, 0, 0, tiled=True)
    column, keep_slab, send_slab = unpack(meta, msg)
    recv_slab = swap(send_slab, "zh")
    column = lax.all_to_all(column, COLUMN, 0, 0, tiled=True)
    cov_in = ((keep_slab + recv_slab) / token_total)[None]
    cov_out = (jnp.sum(column[:, :32], axis=0) / token_total)[None]
    inner = jnp.sum(column[:, 32, :1], axis=0)
    inner = (inner + swap(inner, "core"))[0]
    clip_factor = jnp.minimum(
        1.0, jnp.sqrt(kl_clip / (learning_rate[0] * learning_rate[0] * inner))
    )
    update = clip_factor * precond
    return (cov_in, cov_out, update)


def solution(mesh):
    fine = Mesh(mesh.devices.reshape(SIZES), AXES)
    placed = (
        P(DP, "zl"),
        P(AXES, None),
        P(),
        P(),
        P("zl", DP, None),
        P(DP, None, None),
        P("zl"),
        P(DP),
        P("zl", DP),
        P(),
    )
    return jax.shard_map(
        local,
        mesh=fine,
        in_specs=placed,
        out_specs=(P("zl", DP, None), P(DP, "zl", None), P("zl", DP)),
        check_vma=False,
    )
```

time: 1750 us -> 116 us (0.07)
  waiting for transfers between devices: 1600 us -> 9.17 us
  blocking collectives: 74.5 us -> 48.2 us
  starting transfers between devices: 0.13 us -> 21.2 us
  Pallas kernels: 0 us -> 18.1 us
    reduce_scatter x2 -> x0, waiting for transfers between devices: 1550 us -> none  [the longest x1 1130 us: local(): lax.psum_scatter(partial_value.reshape(-1, block_out), ('dp', 'group'), s...]
    psum x1 -> x0, blocking collectives: 74.5 us -> none  [local(): lax.psum(jnp.sum(precond * gradient.astype(jnp.float32)), ('dp', 'group'))]
    all_gather x1 -> x0, waiting for transfers between devices: 51.9 us -> none  [local(): full_basis = lax.all_gather(basis_in, 'dp', axis=1, tiled=True)[0]]
    all_to_all x0 -> x2, blocking collectives: none -> 48.2 us  [the longest x1 25.8 us: local(): msg = lax.all_to_all(msg, PLANE, 0, 0, tiled=True)]
    pallas_call x0 -> x5, Pallas kernels: none -> 18.1 us  [the longest x1 6.41 us: cov_out_partial(): pl.pallas_call(cov_out_kernel, grid_spec=pltpu.PrefetchScalarGridSpec(num...]
  transfers between devices with their start and end apart: 3 -> 7, of which waited for: 3 -> 3; matrix products, arithmetic and copies ran while one was open for 2% -> 1% of each run, Pallas kernels for 0% -> 7%
where the time goes in v1:
time: 116 us
  blocking collectives  48.2 us (42%)
  starting transfers between devices  21.2 us (18%)
  Pallas kernels  18.1 us (16%)
  local copies, waits for them, and re-layouts  11.2 us (10%)
  waiting for transfers between devices  9.17 us (8%)
  other arithmetic  4.07 us (4%)
  between operations  3.98 us (3%)
    all_to_all x1, blocking collectives, local(): msg = lax.all_to_all(msg, PLANE, 0, 0, tiled=True)  25.8 us
    all_to_all x1, blocking collectives, local(): lax.all_to_all(jnp.broadcast_to(slabs[None], (16,) + slabs.shape), PLANE,...  22.4 us
    ppermute x6, starting transfers between devices, swap(): return lax.ppermute(array, axis, [(0, 1), (1, 0)])  14.6 us
    unnamed x34, local copies, waits for them, and re-layouts  9.6 us
    all_to_all x1, starting transfers between devices, local(): column = lax.all_to_all(column, COLUMN, 0, 0, tiled=True)  6.57 us
    pallas_call x1, Pallas kernels, cov_out_partial(): pl.pallas_call(cov_out_kernel, grid_spec=pltpu.PrefetchScalarGridSpec(num...  6.41 us
    all_to_all x1, waiting for transfers between devices, local(): column = lax.all_to_all(column, COLUMN, 0, 0, tiled=True)  5.7 us
    pallas_call x1, Pallas kernels, cov_in_partial(): pl.pallas_call(cov_in_kernel, grid_spec=pltpu.PrefetchScalarGridSpec(num_...  4.74 us
  transfers between devices with their start and end apart: 7, of which 3 were waited for; matrix products, arithmetic and copies ran while one was open for 1% of the time, Pallas kernels for 7%

profile of v1, /device:TPU:1, one launch (start us, length us, event | category | flops | bytes accessed | tf_op | source)
XLA Modules:
  0.0 115.9 jit_solution(204031428068357466)
XLA Ops:
  0.6 1.2 %dynamic_slice.3 = s32[1]{0:T(128)} dynamic-slice(s32[64]{0:T(128)} %param.12, s32[]{:T(128)S(6)} %select_n.3), dynamic_slice_sizes={1} | dynamic-slice | bytes 12 | tf_op jit(solution)/shard_map/dynamic_slice | solution.py:246
  2.5 0.7 pad_add_fusion.meta
  3.3 2.2 %copy-done = bf16[256,8192]{1,0:T(8,128)(2,1)S(1)} copy-done((bf16[256,8192]{1,0:T(8,128)(2,1)S(1)}, bf16[256,8192]{1,0:T(8,128)(2,1)}, u32[]{:S(2)}) %copy-start) | copy-done | bytes 4194328
  6.1 6.4 %cov_out_partial.1 = (f32[32,128,128]{2,1,0:T(8,128)}, f32[32,128,128]{2,1,0:T(8,128)S(1)}) custom-call(s32[64]{0:T(128)S(1)} %copy-done.12, s32[4]{0:T(128)S(1)} %pad_add_fusion.meta, bf16[256,8192]{1,0:T(8,128)(2,1)S(1)} %copy-done, bf16[256,8192]{1,0:T(8,128)(2,1)S(1)} %copy-done, bf16[256,8192]{1,0:T(8,128)(2,1)S(1)} %copy-done, ...), custom_call_target="tpu_custom_call" | custom-call | flops 536870912 | bytes 8388608 | tf_op jit(solution)/shard_map/cov_out_partial/pallas_call | solution.py:52
  12.5 3.2 %collective-permute-start = (f32[32,128,128]{2,1,0:T(8,128)}, f32[32,128,128]{2,1,0:T(8,128)S(1)}, u32[]{:S(2)}, u32[]{:S(2)}) collective-permute-start(f32[32,128,128]{2,1,0:T(8,128)} %get-tuple-element.13), channel_id=1, source_target_pairs={{0,4},{4,0},{1,5},{5,1},{2,6},{6,2},{3,7},{7,3},{8,12},{12,8},{9,1... | collective-permute-start | bytes 6291464 | tf_op jit(solution)/shard_map/ppermute | solution.py:228
  15.8 5.2 %collective-permute-start.2 = (bf16[16,1024]{1,0:T(8,128)(2,1)S(1)}, bf16[16,1024]{1,0:T(8,128)(2,1)S(1)}, u32[]{:S(2)}, u32[]{:S(2)}) collective-permute-start(bf16[16,1024]{1,0:T(8,128)(2,1)S(1)} %bitcast.23), channel_id=1, source_target_pairs={{0,32},{32,0},{1,33},{33,1},{2,34},{34,2},{3,35},{35,3},{4,36},{36... | collective-permute-start | bytes 98312 | tf_op jit(solution)/shard_map/ppermute | solution.py:228
  21.0 4.7 %cov_in_partial.1 = (f32[32,16,1024]{2,1,0:T(8,128)}, f32[32,16,1024]{2,1,0:T(8,128)S(1)}) custom-call(s32[4]{0:T(128)S(1)} %pad_add_fusion.meta, bf16[1024,1024]{1,0:T(8,128)(2,1)S(1)} %copy-done.13, bf16[1024,1024]{1,0:T(8,128)(2,1)S(1)} %copy-done.13), custom_call_target="tpu_custom_call" | custom-call | flops 2147483648 | bytes 8388608 | tf_op jit(solution)/shard_map/cov_in_partial/pallas_call | solution.py:81
  25.7 1.4 %copy-done.5 = f32[32,16,1024]{2,1,0:T(8,128)} copy-done((f32[32,16,1024]{2,1,0:T(8,128)}, f32[32,16,1024]{2,1,0:T(8,128)S(1)}, u32[]{:S(2)}) %copy-start.5) | copy-done | bytes 2097176
  27.7 22.4 %all_to_all.15.q_own = bf16[16,32,1024]{2,1,0:T(8,128)(2,1)S(1)} all-to-all(bf16[16,32,1024]{2,1,0:T(8,128)(2,1)S(1)} %broadcast_in_dim.10), channel_id=1, replica_groups=mesh['x'=4,'zh'=2,'y'=4,'core'=2,'zl'=4] {'x','y'}, dimensions={0} | all-to-all | bytes 2097152 | tf_op jit(solution)/shard_map/all_to_all | solution.py:259
  50.0 2.3 %collective-permute-start.3 = (bf16[16,32,1024]{2,1,0:T(8,128)(2,1)S(1)}, bf16[16,32,1024]{2,1,0:T(8,128)(2,1)}, u32[]{:S(2)}, u32[]{:S(2)}) collective-permute-start(bf16[16,32,1024]{2,1,0:T(8,128)(2,1)S(1)} %all_to_all.15.q_own), channel_id=1, source_target_pairs={{0,4},{4,0},{1,5},{5,1},{2,6},{6,2},{3,7},{7,3},{8,12},{12,8},{9,1... | collective-permute-start | bytes 3145736 | tf_op jit(solution)/shard_map/ppermute | solution.py:228
  52.4 2.3 %collective-permute-done.3.q_other = bf16[16,32,1024]{2,1,0:T(8,128)(2,1)} collective-permute-done((bf16[16,32,1024]{2,1,0:T(8,128)(2,1)S(1)}, bf16[16,32,1024]{2,1,0:T(8,128)(2,1)}, u32[]{:S(2)}, u32[]{:S(2)}) %collective-permute-start.3) | collective-permute-done | bytes 1048608 | tf_op jit(solution)/shard_map/ppermute | solution.py:228
  54.7 2.9 %precondition.1 = (f32[1024,128]{1,0:T(8,128)S(1)}, bf16[16,128]{1,0:T(8,128)(2,1)S(1)}) custom-call(s32[4]{0:T(128)S(1)} %pad_add_fusion.meta, bf16[16,32,1024]{2,1,0:T(8,128)(2,1)S(1)} %all_to_all.15.q_own, bf16[16,32,1024]{2,1,0:T(8,128)(2,1)} %collective-permute-done.3.q_other, bf16[1024,128]{1,0:T(8,128)(2,1)S(1)} %copy-done.9, ...), custom_call_target="tpu_custom_call" | custom-call | flops 629145600 | bytes 3145728 | tf_op jit(solution)/shard_map/precondition/pallas_call | solution.py:169
  57.7 0.8 copy-done.7
  58.5 1.4 %copy-done.3 = f32[32,128,128]{2,1,0:T(8,128)} copy-done((f32[32,128,128]{2,1,0:T(8,128)}, f32[32,128,128]{2,1,0:T(8,128)S(1)}, u32[]{:S(2)}) %copy-start.3) | copy-done | bytes 2097176
  59.8 1.6 %copy-done.2 = f32[32,128,128]{2,1,0:T(8,128)S(1)} copy-done((f32[32,128,128]{2,1,0:T(8,128)S(1)}, f32[32,128,128]{2,1,0:T(8,128)}, u32[]{:S(2)}) %copy-start.2) | copy-done | bytes 2097176
  61.4 1.6 %copy-done.4 = f32[32,128,128]{2,1,0:T(8,128)S(1)} copy-done((f32[32,128,128]{2,1,0:T(8,128)S(1)}, f32[32,128,128]{2,1,0:T(8,128)}, u32[]{:S(2)}) %copy-start.4) | copy-done | bytes 2097176
  63.0 2.5 %pack.1 = bf16[16,400,128]{2,1,0:T(8,128)(2,1)S(1)} custom-call(f32[8,4,128,128]{3,2,1,0:T(8,128)S(1)} %bitcast.18, f32[8,4,128,128]{3,2,1,0:T(8,128)S(1)} %bitcast.19, f32[8,4,16,1024]{3,2,1,0:T(8,128)S(1)} %bitcast.20, f32[8,4,16,1024]{3,2,1,0:T(8,128)} %bitcast.7.recv_in), custom_call_target="tpu_custom_call" | custom-call | flops 4194304 | bytes 10485760 | tf_op jit(solution)/shard_map/pack/pallas_call | solution.py:120
  65.7 25.8 %all_to_all.16.msg = bf16[16,400,128]{2,1,0:T(8,128)(2,1)S(1)} all-to-all(bf16[16,400,128]{2,1,0:T(8,128)(2,1)S(1)} %dynamic_update_slice.3), channel_id=1, replica_groups=mesh['x'=4,'zh'=2,'y'=4,'core'=2,'zl'=4] {'x','y'}, dimensions={0} | all-to-all | bytes 3276800 | tf_op jit(solution)/shard_map/all_to_all | solution.py:271
  91.6 1.5 %unpack.1 = (f32[8,40,128]{2,1,0:T(8,128)}, f32[16,1024]{1,0:T(8,128)S(1)}, f32[16,1024]{1,0:T(8,128)S(1)}) custom-call(s32[4]{0:T(128)S(1)} %pad_add_fusion.meta, bf16[16,400,128]{2,1,0:T(8,128)(2,1)S(1)} %all_to_all.16.msg), custom_call_target="tpu_custom_call" | custom-call | flops 2097152 | bytes 2097152 | tf_op jit(solution)/shard_map/unpack/pallas_call | solution.py:212
  93.1 6.6 %all-to-all-start.2 = ((f32[8,40,128]{2,1,0:T(8,128)}), f32[8,40,128]{2,1,0:T(8,128)S(1)}, u32[]{:S(2)}, u32[]{:S(2)}) async-start(f32[8,40,128]{2,1,0:T(8,128)} %get-tuple-element.19), calls=%async_computation.2 | async-start | bytes 327680 | tf_op jit(solution)/shard_map/all_to_all | solution.py:274
  102.3 5.7 %all-to-all-done.2 = f32[8,40,128]{2,1,0:T(8,128)S(1)} async-done(((f32[8,40,128]{2,1,0:T(8,128)}), f32[8,40,128]{2,1,0:T(8,128)S(1)}, u32[]{:S(2)}, u32[]{:S(2)}) %all-to-all-start.2) | async-done | bytes 163872 | tf_op jit(solution)/shard_map/all_to_all | solution.py:274
  109.2 3.4 %collective-permute-start.5 = (f32[1]{0:T(128)}, f32[1]{0:T(128)}, u32[]{:S(2)}, u32[]{:S(2)}) collective-permute-start(f32[1]{0:T(128)} %bitcast.14), channel_id=1, source_target_pairs={{0,4},{4,0},{1,5},{5,1},{2,6},{6,2},{3,7},{7,3},{8,12},{12,8},{9,1... | collective-permute-start | bytes 20 | tf_op jit(solution)/shard_map/ppermute | solution.py:228
  112.6 1.2 %collective-permute-done.5 = f32[1]{0:T(128)} collective-permute-done((f32[1]{0:T(128)}, f32[1]{0:T(128)}, u32[]{:S(2)}, u32[]{:S(2)}) %collective-permute-start.5) | collective-permute-done | bytes 36 | tf_op jit(solution)/shard_map/ppermute | solution.py:228
  115.1 0.8 broadcast_multiply_fusion
  (45 shorter events, 4.2 us)
Async XLA Ops:
  3.3 2.2 %copy-start = (bf16[256,8192]{1,0:T(8,128)(2,1)S(1)}, bf16[256,8192]{1,0:T(8,128)(2,1)}, u32[]{:S(2)}) copy-start(bf16[256,8192]{1,0:T(8,128)(2,1)} %refs_7_.1) | copy-start | bytes 12582916
  5.5 0.7 copy-start.12
  6.1 9.7 %copy-start.14 = (bf16[1,16,1024]{2,1,0:T(8,128)(2,1)S(1)}, bf16[1,16,1024]{2,1,0:T(8,128)(2,1)}, u32[]{:S(2)}) copy-start(bf16[1,16,1024]{2,1,0:T(8,128)(2,1)} %param.14) | copy-start | bytes 98308
  6.1 14.9 %copy-start.13 = (bf16[1024,1024]{1,0:T(8,128)(2,1)S(1)}, bf16[1024,1024]{1,0:T(8,128)(2,1)}, u32[]{:S(2)}) copy-start(bf16[1024,1024]{1,0:T(8,128)(2,1)} %rhs.1) | copy-start | bytes 6291460
  12.5 13.2 %copy-start.1 = (f32[32,128,128]{2,1,0:T(8,128)}, f32[32,128,128]{2,1,0:T(8,128)S(1)}, u32[]{:S(2)}) copy-start(f32[32,128,128]{2,1,0:T(8,128)S(1)} %get-tuple-element.12) | copy-start | bytes 6291460
  12.5 45.9 %collective-permute-start = (f32[32,128,128]{2,1,0:T(8,128)}, f32[32,128,128]{2,1,0:T(8,128)S(1)}, u32[]{:S(2)}, u32[]{:S(2)}) collective-permute-start(f32[32,128,128]{2,1,0:T(8,128)} %get-tuple-element.13), channel_id=1, source_target_pairs={{0,4},{4,0},{1,5},{5,1},{2,6},{6,2},{3,7},{7,3},{8,12},{12,8},{9,1... | collective-permute-start | bytes 6291464 | tf_op jit(solution)/shard_map/ppermute | solution.py:228
  15.8 11.8 %collective-permute-start.2 = (bf16[16,1024]{1,0:T(8,128)(2,1)S(1)}, bf16[16,1024]{1,0:T(8,128)(2,1)S(1)}, u32[]{:S(2)}, u32[]{:S(2)}) collective-permute-start(bf16[16,1024]{1,0:T(8,128)(2,1)S(1)} %bitcast.23), channel_id=1, source_target_pairs={{0,32},{32,0},{1,33},{33,1},{2,34},{34,2},{3,35},{35,3},{4,36},{36... | collective-permute-start | bytes 98312 | tf_op jit(solution)/shard_map/ppermute | solution.py:228
  25.7 1.4 %copy-start.5 = (f32[32,16,1024]{2,1,0:T(8,128)}, f32[32,16,1024]{2,1,0:T(8,128)S(1)}, u32[]{:S(2)}) copy-start(f32[32,16,1024]{2,1,0:T(8,128)S(1)} %get-tuple-element.14) | copy-start | bytes 6291460
  27.1 25.2 %copy-start.15 = (f32[128]{0:T(128)S(1)}, f32[128]{0:T(128)}, u32[]{:S(2)}) copy-start(f32[128]{0:T(128)} %param.17) | copy-start | bytes 1540
  27.1 27.6 %copy-start.9 = (bf16[1024,128]{1,0:T(8,128)(2,1)S(1)}, bf16[1024,128]{1,0:T(8,128)(2,1)}, u32[]{:S(2)}) copy-start(bf16[1024,128]{1,0:T(8,128)(2,1)} %grad.1) | copy-start | bytes 786436
  27.1 27.6 %copy-start.10 = (bf16[1,128,128]{2,1,0:T(8,128)(2,1)S(1)}, bf16[1,128,128]{2,1,0:T(8,128)(2,1)}, u32[]{:S(2)}) copy-start(bf16[1,128,128]{2,1,0:T(8,128)(2,1)} %param.15) | copy-start | bytes 98308
  27.1 27.6 %copy-start.11 = (f32[1024]{0:T(1024)S(1)}, f32[1024]{0:T(1024)}, u32[]{:S(2)}) copy-start(f32[1024]{0:T(1024)} %param.16) | copy-start | bytes 12292
  27.1 32.7 %collective-permute-start.1 = (f32[32,16,1024]{2,1,0:T(8,128)}, f32[32,16,1024]{2,1,0:T(8,128)}, u32[]{:S(2)}, u32[]{:S(2)}) collective-permute-start(f32[32,16,1024]{2,1,0:T(8,128)} %get-tuple-element.15), channel_id=1, source_target_pairs={{0,4},{4,0},{1,5},{5,1},{2,6},{6,2},{3,7},{7,3},{8,12},{12,8},{9,1... | collective-permute-start | bytes 6291464 | tf_op jit(solution)/shard_map/ppermute | solution.py:228
  50.0 4.7 %collective-permute-start.3 = (bf16[16,32,1024]{2,1,0:T(8,128)(2,1)S(1)}, bf16[16,32,1024]{2,1,0:T(8,128)(2,1)}, u32[]{:S(2)}, u32[]{:S(2)}) collective-permute-start(bf16[16,32,1024]{2,1,0:T(8,128)(2,1)S(1)} %all_to_all.15.q_own), channel_id=1, source_target_pairs={{0,4},{4,0},{1,5},{5,1},{2,6},{6,2},{3,7},{7,3},{8,12},{12,8},{9,1... | collective-permute-start | bytes 3145736 | tf_op jit(solution)/shard_map/ppermute | solution.py:228
  52.4 7.4 %copy-start.6 = (f32[32,16,1024]{2,1,0:T(8,128)S(1)}, f32[32,16,1024]{2,1,0:T(8,128)}, u32[]{:S(2)}) copy-start(f32[32,16,1024]{2,1,0:T(8,128)} %copy-done.5) | copy-start | bytes 6291460
  57.7 0.8 copy-start.7
  58.5 1.4 %copy-start.3 = (f32[32,128,128]{2,1,0:T(8,128)}, f32[32,128,128]{2,1,0:T(8,128)S(1)}, u32[]{:S(2)}) copy-start(f32[32,128,128]{2,1,0:T(8,128)S(1)} %collective-permute-done) | copy-start | bytes 6291460
  59.8 1.6 %copy-start.2 = (f32[32,128,128]{2,1,0:T(8,128)S(1)}, f32[32,128,128]{2,1,0:T(8,128)}, u32[]{:S(2)}) copy-start(f32[32,128,128]{2,1,0:T(8,128)} %copy-done.1) | copy-start | bytes 6291460
  61.4 1.6 %copy-start.4 = (f32[32,128,128]{2,1,0:T(8,128)S(1)}, f32[32,128,128]{2,1,0:T(8,128)}, u32[]{:S(2)}) copy-start(f32[32,128,128]{2,1,0:T(8,128)} %copy-done.3) | copy-start | bytes 6291460
  65.7 34.0 %copy-start.16 = (s32[64]{0:T(128)S(1)}, s32[64]{0:T(128)}, u32[]{:S(2)}) copy-start(s32[64]{0:T(128)} %param.12) | copy-start | bytes 772
  65.7 49.3 %copy-start.8 = (f32[1024,128]{1,0:T(8,128)S(1)}, f32[1024,128]{1,0:T(8,128)}, u32[]{:S(2)}) copy-start(f32[1024,128]{1,0:T(8,128)} %copy-done.7) | copy-start | bytes 1572868
  93.1 8.6 %collective-permute-start.4 = (f32[16,1024]{1,0:T(8,128)S(1)}, f32[16,1024]{1,0:T(8,128)S(1)}, u32[]{:S(2)}, u32[]{:S(2)}) collective-permute-start(f32[16,1024]{1,0:T(8,128)S(1)} %get-tuple-element.18), channel_id=1, source_target_pairs={{0,32},{32,0},{1,33},{33,1},{2,34},{34,2},{3,35},{35,3},{4,36},{36... | collective-permute-start | bytes 196616 | tf_op jit(solution)/shard_map/ppermute | solution.py:228
  93.1 14.9 %all-to-all-start.2 = ((f32[8,40,128]{2,1,0:T(8,128)}), f32[8,40,128]{2,1,0:T(8,128)S(1)}, u32[]{:S(2)}, u32[]{:S(2)}) async-start(f32[8,40,128]{2,1,0:T(8,128)} %get-tuple-element.19), calls=%async_computation.2 | async-start | bytes 327680 | tf_op jit(solution)/shard_map/all_to_all | solution.py:274
  109.2 4.5 %collective-permute-start.5 = (f32[1]{0:T(128)}, f32[1]{0:T(128)}, u32[]{:S(2)}, u32[]{:S(2)}) collective-permute-start(f32[1]{0:T(128)} %bitcast.14), channel_id=1, source_target_pairs={{0,4},{4,0},{1,5},{5,1},{2,6},{6,2},{3,7},{7,3},{8,12},{12,8},{9,1... | collective-permute-start | bytes 20 | tf_op jit(solution)/shard_map/ppermute | solution.py:228

commit v2 on v1

v2 whole, which is shorter than its diff:
```python
import jax
import jax.numpy as jnp
from jax import lax
from jax.experimental import pallas as pl
from jax.experimental.pallas import tpu as pltpu
from jax.sharding import Mesh, PartitionSpec as P

damping = 0.03
kl_clip = 0.001
f32 = jnp.float32
bf16 = jnp.bfloat16

AXES = ("x", "zh", "y", "core", "zl")
SIZES = (4, 2, 4, 2, 4)
DP = ("x", "zh", "y", "core")
PLANE = ("x", "y")
COLUMN = ("zh", "zl")
VMEM = 20 << 20

ROWS_IN = 256
ROWS_OUT = 128
ROWS_EXTRA = 16
ROWS = ROWS_IN + ROWS_OUT + ROWS_EXTRA


def dot(a, b, ca, cb):
    return lax.dot_general(a, b, (((ca,), (cb,)), ((), ())), preferred_element_type=f32)


def counted():
    core = lax.axis_index("core")
    dp = ((lax.axis_index("x") * 2 + lax.axis_index("zh")) * 4 + lax.axis_index("y")) * 2 + core
    return dp, core, lax.axis_index("zl")


def cov_out_kernel(owners, counts, core, *refs):
    blocks, (send, keep) = refs[:8], refs[8:]
    dp, _, zl = counted()
    quarter = blocks[0].shape[0]
    live = counts[dp] - zl * quarter
    rows = lax.broadcasted_iota(jnp.int32, blocks[0].shape, 0) < live
    for y in range(4):
        for src, dst in ((blocks[y], keep), (blocks[4 + y], send)):
            full = src[...]
            masked = jnp.where(rows, full, jnp.zeros((), bf16))
            dst[y] = dot(masked, full, 0, 0)


def cov_out_partial(output_grads, owners, counts, core):
    quarter = output_grads.shape[0]

    def at(y, other):
        def index(s, owners, counts, core):
            c = 1 - core[0] if other else core[0]
            return (0, owners[(s * 4 + y) * 2 + c])

        return pl.BlockSpec((quarter, 128), index)

    out = pl.BlockSpec((4, 128, 128), lambda s, *_: (s, 0, 0))
    return pl.pallas_call(
        cov_out_kernel,
        grid_spec=pltpu.PrefetchScalarGridSpec(
            num_scalar_prefetch=3,
            grid=(8,),
            in_specs=[at(y, False) for y in range(4)] + [at(y, True) for y in range(4)],
            out_specs=[out, out],
        ),
        out_shape=[jax.ShapeDtypeStruct((32, 128, 128), f32)] * 2,
        compiler_params=pltpu.CompilerParams(vmem_limit_bytes=VMEM),
        cost_estimate=pl.CostEstimate(
            flops=2 * quarter * 8192 * 128, bytes_accessed=quarter * 8192 * 2 + (4 << 20), transcendentals=0
        ),
        name="cov_out_partial",
    )(owners, counts, core, *([output_grads] * 8))


def cov_in_kernel(counts, lhs, rhs, send, keep):
    dp, core, _ = counted()
    first = core == 0
    rows = lax.broadcasted_iota(jnp.int32, lhs.shape, 0) < counts[dp]
    masked = jnp.where(rows, lhs[...], jnp.zeros((), bf16))
    part = dot(masked, rhs[...], 0, 0).reshape(8, 2, 16, 1024)
    keep[...] = jnp.where(first, part[:, 0], part[:, 1])
    send[...] = jnp.where(first, part[:, 1], part[:, 0])


def cov_in_partial(activations, counts):
    tok = activations.shape[0]
    out = pl.BlockSpec((8, 16, 1024), lambda s, *_: (s, 0, 0))
    return pl.pallas_call(
        cov_in_kernel,
        grid_spec=pltpu.PrefetchScalarGridSpec(
            num_scalar_prefetch=1,
            grid=(4,),
            in_specs=[
                pl.BlockSpec((tok, 256), lambda s, *_: (0, s)),
                pl.BlockSpec((tok, 1024), lambda s, *_: (0, 0)),
            ],
            out_specs=[out, out],
        ),
        out_shape=[jax.ShapeDtypeStruct((32, 16, 1024), f32)] * 2,
        compiler_params=pltpu.CompilerParams(vmem_limit_bytes=VMEM),
        cost_estimate=pl.CostEstimate(
            flops=2 * tok * 1024 * 1024, bytes_accessed=tok * 4096 + (4 << 20), transcendentals=0
        ),
        name="cov_in_partial",
    )(counts, activations, activations)


def pack_kernel(keep_out, recv_out, keep_in, recv_in, msg):
    row = lax.broadcasted_iota(jnp.int32, (128, 128), 0)
    col = lax.broadcasted_iota(jnp.int32, (128, 128), 1)
    for y in range(4):
        first = keep_out[0, y] + recv_out[0, y]
        second = keep_out[1, y] + recv_out[1, y]
        msg[y, ROWS_IN : ROWS_IN + ROWS_OUT] = jnp.where(row <= col, first, second).astype(bf16)
        diag = jnp.sum(jnp.where(row == col, second, 0.0), axis=0, keepdims=True)
        top = lax.broadcasted_iota(jnp.int32, (ROWS_EXTRA, 128), 0) == 0
        msg[y, ROWS_IN + ROWS_OUT :] = jnp.where(top, diag, 0.0).astype(bf16)
        for zh in range(2):
            rows = (keep_in[zh, y] + recv_in[zh, y]).astype(bf16)
            for c in range(8):
                msg[y, c * 32 + zh * 16 : c * 32 + zh * 16 + 16] = rows[:, c * 128 : c * 128 + 128]


def pack(keep_out, recv_out, keep_in, recv_in):
    outs = pl.BlockSpec((2, 4, 128, 128), lambda x: (x, 0, 0, 0))
    ins = pl.BlockSpec((2, 4, 16, 1024), lambda x: (x, 0, 0, 0))
    return pl.pallas_call(
        pack_kernel,
        grid=(4,),
        in_specs=[outs, outs, ins, ins],
        out_specs=pl.BlockSpec((4, ROWS, 128), lambda x: (x, 0, 0)),
        out_shape=jax.ShapeDtypeStruct((16, ROWS, 128), bf16),
        compiler_params=pltpu.CompilerParams(vmem_limit_bytes=VMEM),
        cost_estimate=pl.CostEstimate(flops=4 << 20, bytes_accessed=10 << 20, transcendentals=0),
        name="pack",
    )(
        keep_out.reshape(8, 4, 128, 128),
        recv_out.reshape(8, 4, 128, 128),
        keep_in.reshape(8, 4, 16, 1024),
        recv_in.reshape(8, 4, 16, 1024),
    )


def dot_slabs(left, slabs, core):
    picked = jnp.concatenate(
        [left[pl.ds(pl.multiple_of((2 * s + core) * 16, 16), 16), :] for s in range(32)], axis=0
    )
    return dot(picked, slabs[...].reshape(512, 1024), 0, 0)


def rotate_kernel(slabs, grad, rotated):
    rotated[...] = dot_slabs(grad, slabs, lax.axis_index("core"))


def scale_kernel(slabs, grad, partial, q_out, values_in, values_out, back, parts):
    total = partial[...] + dot_slabs(grad, slabs, 1 - lax.axis_index("core"))
    q = q_out[...]
    spectral = dot(q, total.astype(bf16), 0, 0)
    scaled = (spectral / (values_in[...] * values_out[...] + damping)).astype(bf16)
    back_rot = dot(q, scaled, 1, 0).astype(bf16)
    back[...] = back_rot
    inner = jnp.sum(
        jnp.sum(back_rot.astype(f32) * total, axis=0, keepdims=True), axis=1, keepdims=True
    )
    high = inner.astype(bf16).astype(f32)
    rest = inner - high
    middle = rest.astype(bf16).astype(f32)
    low = rest - middle
    row = lax.broadcasted_iota(jnp.int32, (16, 128), 0)
    parts[...] = jnp.where(
        row == 1, high, jnp.where(row == 2, middle, jnp.where(row == 3, low, 0.0))
    ).astype(bf16)


def finish_kernel(q_own, q_other, back, precond):
    core = lax.axis_index("core")
    for src, c in ((q_own, core), (q_other, 1 - core)):
        result = dot(src[...].reshape(512, 1024), back[...], 1, 1)
        for s in range(32):
            at = pl.multiple_of((2 * s + c) * 16, 16)
            precond[pl.ds(at, 16), :] = result[s * 16 : s * 16 + 16]


def on_chip(kernel, outs, flops, *args):
    whole = pl.BlockSpec(memory_space=pltpu.VMEM)
    size = sum(a.size * a.dtype.itemsize for a in args)
    return pl.pallas_call(
        kernel,
        in_specs=[whole] * len(args),
        out_specs=[whole] * len(outs),
        out_shape=outs,
        compiler_params=pltpu.CompilerParams(vmem_limit_bytes=VMEM),
        cost_estimate=pl.CostEstimate(flops=flops, bytes_accessed=size, transcendentals=0),
        name=kernel.__name__[:-7],
    )(*args)


def unpack_kernel(msg, column, keep_in, send_in):
    first = lax.axis_index("zh") == 0

    def total(at, rows):
        out = msg[0, at : at + rows].astype(f32)
        for s in range(1, 16):
            out = out + msg[s, at : at + rows].astype(f32)
        return out

    for c in range(8):
        pair = total(c * 32, 32)
        lo, hi = pair[:16], pair[16:]
        keep_in[:, c * 128 : c * 128 + 128] = jnp.where(first, lo, hi)
        send_in[:, c * 128 : c * 128 + 128] = jnp.where(first, hi, lo)
    folded = total(ROWS_IN, ROWS_OUT)
    extra = total(ROWS_IN + ROWS_OUT, ROWS_EXTRA)
    turned = folded.T
    row = lax.broadcasted_iota(jnp.int32, (128, 128), 0)
    col = lax.broadcasted_iota(jnp.int32, (128, 128), 1)
    one = jnp.where(row <= col, folded, turned)
    two = jnp.where(row > col, folded, jnp.where(row == col, extra[0:1], turned))
    row = lax.broadcasted_iota(jnp.int32, extra.shape, 0)
    inner = jnp.sum(jnp.where((row >= 1) & (row < 7), extra, 0.0), axis=0, keepdims=True)
    inner = jnp.broadcast_to(inner, (8, 128))
    for z in range(4):
        column[z, 0:32] = one[z * 32 : z * 32 + 32]
        column[4 + z, 0:32] = two[z * 32 : z * 32 + 32]
        column[z, 32:40] = inner
        column[4 + z, 32:40] = inner


def swap(array, axis):
    return lax.ppermute(array, axis, [(0, 1), (1, 0)])


def local(
    activations,
    output_grads,
    token_counts,
    owner_blocks,
    basis_in,
    basis_out,
    values_in,
    values_out,
    gradient,
    learning_rate,
):
    token_total = jnp.sum(token_counts).astype(f32)
    shape = jax.ShapeDtypeStruct
    slabs = jnp.broadcast_to(basis_in, (32,) + basis_in.shape[1:])
    q_own = lax.all_to_all(slabs, ("x", "zh", "y"), 0, 0, tiled=True)

    core = lax.axis_index("core").astype(jnp.int32)[None]
    send_out, keep_out = cov_out_partial(output_grads, owner_blocks, token_counts, core)
    recv_out = swap(send_out, "core")
    send_in, keep_in = cov_in_partial(activations, token_counts)
    recv_in = swap(send_in, "core")
    msg = pack(keep_out, recv_out, keep_in, recv_in)

    q_other = swap(q_own, "core")
    (partial,) = on_chip(rotate_kernel, [shape((128, 1024), f32)], 128 << 20, q_own, gradient)
    back, parts = on_chip(
        scale_kernel,
        [shape((128, 1024), bf16), shape((16, 128), bf16)],
        256 << 20,
        q_other,
        gradient,
        partial,
        basis_out[0],
        values_in[None, :],
        values_out[:, None],
    )
    parts = jnp.concatenate([parts[1:4], swap(parts, "core")[1:4]], axis=0)
    (precond,) = on_chip(finish_kernel, [shape((1024, 128), f32)], 256 << 20, q_own, q_other, back)
    at = ROWS_IN + ROWS_OUT + 1
    msg = lax.dynamic_update_slice(
        msg, jnp.broadcast_to(parts[None], (16, 6, 128)), (0, at, 0)
    )
    msg = lax.all_to_all(msg, PLANE, 0, 0, tiled=True)
    column, keep_slab, send_slab = on_chip(
        unpack_kernel,
        [shape((8, 40, 128), f32), shape((16, 1024), f32), shape((16, 1024), f32)],
        2 << 20,
        msg,
    )
    recv_slab = swap(send_slab, "zh")
    column = lax.all_to_all(column, COLUMN, 0, 0, tiled=True)
    cov_in = ((keep_slab + recv_slab) / token_total)[None]
    cov_out = (jnp.sum(column[:, :32], axis=0) / token_total)[None]
    inner = jnp.sum(column[:, 32, 0], axis=0)
    clip_factor = jnp.minimum(
        1.0, jnp.sqrt(kl_clip / (learning_rate[0] * learning_rate[0] * inner))
    )
    update = clip_factor * precond
    return (cov_in, cov_out, update)


def solution(mesh):
    fine = Mesh(mesh.devices.reshape(SIZES), AXES)
    placed = (
        P(DP, "zl"),
        P(AXES, None),
        P(),
        P(),
        P("zl", DP, None),
        P(DP, None, None),
        P("zl"),
        P(DP),
        P("zl", DP),
        P(),
    )
    return jax.shard_map(
        local,
        mesh=fine,
        in_specs=placed,
        out_specs=(P("zl", DP, None), P(DP, "zl", None), P("zl", DP)),
        check_vma=False,
    )
```

time: 116 us -> 104 us (0.90)
  blocking collectives: 48.2 us -> 32.1 us
  starting transfers between devices: 21.2 us -> 27.7 us
  local copies, waits for them, and re-layouts: 11.2 us -> 7.42 us
  waiting for transfers between devices: 9.17 us -> 12.7 us
    all_to_all x1 -> x0, blocking collectives: 22.4 us -> none  [local(): lax.all_to_all(jnp.broadcast_to(slabs[None], (16,) + slabs.shape), PLANE,...]
    all_to_all x0 -> x1, starting transfers between devices: none -> 14.5 us  [local(): q_own = lax.all_to_all(slabs, ('x', 'zh', 'y'), 0, 0, tiled=True)]
    ppermute x6 -> x5, starting transfers between devices: 14.6 us -> 3.38 us  [swap(): return lax.ppermute(array, axis, [(0, 1), (1, 0)])]
    all_to_all x1, blocking collectives: 25.8 us -> 32.1 us  [local(): msg = lax.all_to_all(msg, PLANE, 0, 0, tiled=True)]
    all_to_all x0 -> x1, waiting for transfers between devices: none -> 5.86 us  [local(): q_own = lax.all_to_all(slabs, ('x', 'zh', 'y'), 0, 0, tiled=True)]
    unnamed x34 -> x28, local copies, waits for them, and re-layouts: 9.6 us -> 5.2 us
    all_to_all x1, starting transfers between devices: 6.57 us -> 9.85 us  [local(): column = lax.all_to_all(column, COLUMN, 0, 0, tiled=True)]
    broadcast_in_dim x2, local copies, waits for them, and re-layouts: 0.12 us -> 1.93 us  [the longest x1 1.93 us: local(): slabs = jnp.broadcast_to(basis_in, (32,) + basis_in.shape[1:])]
  transfers between devices with their start and end apart: 7 -> 7, of which waited for: 3 -> 3; matrix products, arithmetic and copies ran while one was open for 1% -> 1% of each run, Pallas kernels for 7% -> 16%
where the time goes in v2:
time: 104 us; the launch traced here: 103 us
  blocking collectives  32.1 us (31%)
  starting transfers between devices  27.7 us (27%)
  Pallas kernels  17.1 us (16%)
  waiting for transfers between devices  12.7 us (12%)
  local copies, waits for them, and re-layouts  7.42 us (7%)
  other arithmetic  3.36 us (3%)
  between operations  2.86 us (3%)
    all_to_all x1, blocking collectives, local(): msg = lax.all_to_all(msg, PLANE, 0, 0, tiled=True)  32.1 us
    all_to_all x1, starting transfers between devices, local(): q_own = lax.all_to_all(slabs, ('x', 'zh', 'y'), 0, 0, tiled=True)  14.5 us
    all_to_all x1, starting transfers between devices, local(): column = lax.all_to_all(column, COLUMN, 0, 0, tiled=True)  9.85 us
    pallas_call x1, Pallas kernels, cov_out_partial(): pl.pallas_call(cov_out_kernel, grid_spec=pltpu.PrefetchScalarGridSpec(num...  6.53 us
    all_to_all x1, waiting for transfers between devices, local(): q_own = lax.all_to_all(slabs, ('x', 'zh', 'y'), 0, 0, tiled=True)  5.86 us
    unnamed x28, local copies, waits for them, and re-layouts  5.2 us
    all_to_all x1, waiting for transfers between devices, local(): column = lax.all_to_all(column, COLUMN, 0, 0, tiled=True)  4.98 us
    pallas_call x1, Pallas kernels, cov_in_partial(): pl.pallas_call(cov_in_kernel, grid_spec=pltpu.PrefetchScalarGridSpec(num_...  4.77 us
  transfers between devices with their start and end apart: 7, of which 3 were waited for; matrix products, arithmetic and copies ran while one was open for 1% of the time, Pallas kernels for 16%

profile of v2, /device:TPU:1, one launch (start us, length us, event | category | flops | bytes accessed | tf_op | source)
XLA Modules:
  0.0 103.2 jit_solution(7600408287991059155)
XLA Ops:
  0.7 1.9 %broadcast_in_dim.28 = bf16[32,16,1024]{2,1,0:T(8,128)(2,1)} broadcast(bf16[16,1024]{1,0:T(8,128)(2,1)} %bitcast.18), dimensions={1,2} | broadcast | bytes 1081344 | tf_op jit(solution)/shard_map/broadcast_in_dim | solution.py:249
  2.6 14.5 %all-to-all-start = ((bf16[32,16,1024]{2,1,0:T(8,128)(2,1)}), bf16[32,16,1024]{2,1,0:T(8,128)(2,1)S(1)}, u32[]{:S(2)}, u32[]{:S(2)}) async-start(bf16[32,16,1024]{2,1,0:T(8,128)(2,1)} %broadcast_in_dim.28), calls=%async_computation | async-start | bytes 2097152 | tf_op jit(solution)/shard_map/all_to_all | solution.py:250
  17.1 2.2 %copy-done = bf16[256,8192]{1,0:T(8,128)(2,1)S(1)} copy-done((bf16[256,8192]{1,0:T(8,128)(2,1)S(1)}, bf16[256,8192]{1,0:T(8,128)(2,1)}, u32[]{:S(2)}) %copy-start) | copy-done | bytes 4194328
  19.3 6.5 %cov_out_partial.1 = (f32[32,128,128]{2,1,0:T(8,128)}, f32[32,128,128]{2,1,0:T(8,128)S(1)}) custom-call(s32[64]{0:T(128)S(1)} %copy-done.10, s32[64]{0:T(128)S(1)} %copy-done.11, s32[1]{0:T(128)} %bitcast.core, bf16[256,8192]{1,0:T(8,128)(2,1)S(1)} %copy-done, bf16[256,8192]{1,0:T(8,128)(2,1)S(1)} %copy-done, bf16[256,8192]{1,0:T(8,128)(2,1)S(1)} %copy-done, ...), custom_call_target="tpu_custom_call" | custom-call | flops 536870912 | bytes 8388608 | tf_op jit(solution)/shard_map/cov_out_partial/pallas_call | solution.py:60
  25.9 1.0 %collective-permute-start = (f32[32,128,128]{2,1,0:T(8,128)}, f32[32,128,128]{2,1,0:T(8,128)}, u32[]{:S(2)}, u32[]{:S(2)}) collective-permute-start(f32[32,128,128]{2,1,0:T(8,128)} %get-tuple-element.13), channel_id=1, source_target_pairs={{0,4},{4,0},{1,5},{5,1},{2,6},{6,2},{3,7},{7,3},{8,12},{12,8},{9,1... | collective-permute-start | bytes 6291464 | tf_op jit(solution)/shard_map/ppermute | solution.py:232
  26.9 4.8 %cov_in_partial.1 = (f32[32,16,1024]{2,1,0:T(8,128)}, f32[32,16,1024]{2,1,0:T(8,128)S(1)}) custom-call(s32[64]{0:T(128)S(1)} %copy-done.11, bf16[1024,1024]{1,0:T(8,128)(2,1)S(1)} %copy-done.12, bf16[1024,1024]{1,0:T(8,128)(2,1)S(1)} %copy-done.12), custom_call_target="tpu_custom_call" | custom-call | flops 2147483648 | bytes 8388608 | tf_op jit(solution)/shard_map/cov_in_partial/pallas_call | solution.py:90
  31.7 1.4 %copy-done.5 = f32[32,16,1024]{2,1,0:T(8,128)} copy-done((f32[32,16,1024]{2,1,0:T(8,128)}, f32[32,16,1024]{2,1,0:T(8,128)S(1)}, u32[]{:S(2)}) %copy-start.5) | copy-done | bytes 2097176
  33.1 5.9 %all-to-all-done.slabs.q_own = bf16[32,16,1024]{2,1,0:T(8,128)(2,1)S(1)} async-done(((bf16[32,16,1024]{2,1,0:T(8,128)(2,1)}), bf16[32,16,1024]{2,1,0:T(8,128)(2,1)S(1)}, u32[]{:S(2)}, u32[]{:S(2)}) %all-to-all-start) | async-done | bytes 1048608 | tf_op jit(solution)/shard_map/all_to_all | solution.py:250
  38.9 1.9 %collective-permute-start.2 = (bf16[32,16,1024]{2,1,0:T(8,128)(2,1)S(1)}, bf16[32,16,1024]{2,1,0:T(8,128)(2,1)S(1)}, u32[]{:S(2)}, u32[]{:S(2)}) collective-permute-start(bf16[32,16,1024]{2,1,0:T(8,128)(2,1)S(1)} %all-to-all-done.slabs.q_own), channel_id=1, source_target_pairs={{0,4},{4,0},{1,5},{5,1},{2,6},{6,2},{3,7},{7,3},{8,12},{12,8},{9,1... | collective-permute-start | bytes 3145736 | tf_op jit(solution)/shard_map/ppermute | solution.py:232
  41.4 1.8 %collective-permute-done.2.slabs.q_other = bf16[32,16,1024]{2,1,0:T(8,128)(2,1)S(1)} collective-permute-done((bf16[32,16,1024]{2,1,0:T(8,128)(2,1)S(1)}, bf16[32,16,1024]{2,1,0:T(8,128)(2,1)S(1)}, u32[]{:S(2)}, u32[]{:S(2)}) %collective-permute-start.2) | collective-permute-done | bytes 1048608 | tf_op jit(solution)/shard_map/ppermute | solution.py:232
  43.2 0.8 scale.1
  44.0 0.4 collective-permute-start.3
  44.4 1.6 %copy-done.6 = f32[32,16,1024]{2,1,0:T(8,128)S(1)} copy-done((f32[32,16,1024]{2,1,0:T(8,128)S(1)}, f32[32,16,1024]{2,1,0:T(8,128)}, u32[]{:S(2)}) %copy-start.6) | copy-done | bytes 2097176
  46.0 3.0 %pack.1 = bf16[16,400,128]{2,1,0:T(8,128)(2,1)S(1)} custom-call(f32[8,4,128,128]{3,2,1,0:T(8,128)S(1)} %bitcast.14, f32[8,4,128,128]{3,2,1,0:T(8,128)} %bitcast.2.recv_out, f32[8,4,16,1024]{3,2,1,0:T(8,128)S(1)} %bitcast.15, f32[8,4,16,1024]{3,2,1,0:T(8,128)} %bitcast.4.recv_in), custom_call_target="tpu_custom_call" | custom-call | flops 4194304 | bytes 10485760 | tf_op jit(solution)/shard_map/pack/pallas_call | solution.py:129
  49.2 32.1 %all_to_all.15.msg = bf16[16,400,128]{2,1,0:T(8,128)(2,1)S(1)} all-to-all(bf16[16,400,128]{2,1,0:T(8,128)(2,1)S(1)} %dynamic_update_slice.3), channel_id=1, replica_groups=mesh['x'=4,'zh'=2,'y'=4,'core'=2,'zl'=4] {'x','y'}, dimensions={0} | all-to-all | bytes 3276800 | tf_op jit(solution)/shard_map/all_to_all | solution.py:278
  81.3 1.0 unpack.1
  82.3 9.9 %all-to-all-start.2 = ((f32[8,40,128]{2,1,0:T(8,128)}), f32[8,40,128]{2,1,0:T(8,128)S(1)}, u32[]{:S(2)}, u32[]{:S(2)}) async-start(f32[8,40,128]{2,1,0:T(8,128)} %get-tuple-element.19), calls=%async_computation.2 | async-start | bytes 327680 | tf_op jit(solution)/shard_map/all_to_all | solution.py:286
  92.1 0.6 reduce_sum.27
  94.0 0.7 finish.1
  94.8 0.6 divide_bitcast_fusion
  95.4 5.0 %all-to-all-done.2 = f32[8,40,128]{2,1,0:T(8,128)S(1)} async-done(((f32[8,40,128]{2,1,0:T(8,128)}), f32[8,40,128]{2,1,0:T(8,128)S(1)}, u32[]{:S(2)}, u32[]{:S(2)}) %all-to-all-start.2) | async-done | bytes 163872 | tf_op jit(solution)/shard_map/all_to_all | solution.py:286
  100.4 0.6 divide_bitcast_fusion.1
  101.0 0.6 slice_reduce_fusion.1
  102.4 0.8 broadcast_multiply_fusion
  (39 shorter events, 0.7 us)
Async XLA Ops:
  0.6 16.5 %copy-start.10 = (s32[64]{0:T(128)S(1)}, s32[64]{0:T(128)}, u32[]{:S(2)}) copy-start(s32[64]{0:T(128)} %owners.1) | copy-start | bytes 772
  0.6 16.5 %copy-start.11 = (s32[64]{0:T(128)S(1)}, s32[64]{0:T(128)}, u32[]{:S(2)}) copy-start(s32[64]{0:T(128)} %counts.3) | copy-start | bytes 772
  2.6 36.4 %all-to-all-start = ((bf16[32,16,1024]{2,1,0:T(8,128)(2,1)}), bf16[32,16,1024]{2,1,0:T(8,128)(2,1)S(1)}, u32[]{:S(2)}, u32[]{:S(2)}) async-start(bf16[32,16,1024]{2,1,0:T(8,128)(2,1)} %broadcast_in_dim.28), calls=%async_computation | async-start | bytes 2097152 | tf_op jit(solution)/shard_map/all_to_all | solution.py:250
  17.1 2.2 %copy-start = (bf16[256,8192]{1,0:T(8,128)(2,1)S(1)}, bf16[256,8192]{1,0:T(8,128)(2,1)}, u32[]{:S(2)}) copy-start(bf16[256,8192]{1,0:T(8,128)(2,1)} %refs_7_.1) | copy-start | bytes 12582916
  19.3 7.6 %copy-start.12 = (bf16[1024,1024]{1,0:T(8,128)(2,1)S(1)}, bf16[1024,1024]{1,0:T(8,128)(2,1)}, u32[]{:S(2)}) copy-start(bf16[1024,1024]{1,0:T(8,128)(2,1)} %rhs.1) | copy-start | bytes 6291460
  25.8 5.8 %copy-start.3 = (f32[32,128,128]{2,1,0:T(8,128)}, f32[32,128,128]{2,1,0:T(8,128)S(1)}, u32[]{:S(2)}) copy-start(f32[32,128,128]{2,1,0:T(8,128)S(1)} %get-tuple-element.12) | copy-start | bytes 6291460
  25.8 15.0 %copy-start.13 = (f32[128]{0:T(128)S(1)}, f32[128]{0:T(128)}, u32[]{:S(2)}) copy-start(f32[128]{0:T(128)} %param.17) | copy-start | bytes 1540
  25.8 15.2 %copy-start.7 = (bf16[1024,128]{1,0:T(8,128)(2,1)S(1)}, bf16[1024,128]{1,0:T(8,128)(2,1)}, u32[]{:S(2)}) copy-start(bf16[1024,128]{1,0:T(8,128)(2,1)} %grad.3) | copy-start | bytes 786436
  25.8 17.3 %copy-start.8 = (bf16[1,128,128]{2,1,0:T(8,128)(2,1)S(1)}, bf16[1,128,128]{2,1,0:T(8,128)(2,1)}, u32[]{:S(2)}) copy-start(bf16[1,128,128]{2,1,0:T(8,128)(2,1)} %param.15) | copy-start | bytes 98308
  25.8 17.3 %copy-start.9 = (f32[1024]{0:T(1024)S(1)}, f32[1024]{0:T(1024)}, u32[]{:S(2)}) copy-start(f32[1024]{0:T(1024)} %param.16) | copy-start | bytes 12292
  25.9 18.5 %collective-permute-start = (f32[32,128,128]{2,1,0:T(8,128)}, f32[32,128,128]{2,1,0:T(8,128)}, u32[]{:S(2)}, u32[]{:S(2)}) collective-permute-start(f32[32,128,128]{2,1,0:T(8,128)} %get-tuple-element.13), channel_id=1, source_target_pairs={{0,4},{4,0},{1,5},{5,1},{2,6},{6,2},{3,7},{7,3},{8,12},{12,8},{9,1... | collective-permute-start | bytes 6291464 | tf_op jit(solution)/shard_map/ppermute | solution.py:232
  31.7 1.4 %copy-start.5 = (f32[32,16,1024]{2,1,0:T(8,128)}, f32[32,16,1024]{2,1,0:T(8,128)S(1)}, u32[]{:S(2)}) copy-start(f32[32,16,1024]{2,1,0:T(8,128)S(1)} %get-tuple-element.14) | copy-start | bytes 6291460
  33.1 11.3 %collective-permute-start.1 = (f32[32,16,1024]{2,1,0:T(8,128)}, f32[32,16,1024]{2,1,0:T(8,128)}, u32[]{:S(2)}, u32[]{:S(2)}) collective-permute-start(f32[32,16,1024]{2,1,0:T(8,128)} %get-tuple-element.15), channel_id=1, source_target_pairs={{0,4},{4,0},{1,5},{5,1},{2,6},{6,2},{3,7},{7,3},{8,12},{12,8},{9,1... | collective-permute-start | bytes 6291464 | tf_op jit(solution)/shard_map/ppermute | solution.py:232
  38.9 4.2 %collective-permute-start.2 = (bf16[32,16,1024]{2,1,0:T(8,128)(2,1)S(1)}, bf16[32,16,1024]{2,1,0:T(8,128)(2,1)S(1)}, u32[]{:S(2)}, u32[]{:S(2)}) collective-permute-start(bf16[32,16,1024]{2,1,0:T(8,128)(2,1)S(1)} %all-to-all-done.slabs.q_own), channel_id=1, source_target_pairs={{0,4},{4,0},{1,5},{5,1},{2,6},{6,2},{3,7},{7,3},{8,12},{12,8},{9,1... | collective-permute-start | bytes 3145736 | tf_op jit(solution)/shard_map/ppermute | solution.py:232
  41.0 3.4 %copy-start.4 = (f32[32,128,128]{2,1,0:T(8,128)S(1)}, f32[32,128,128]{2,1,0:T(8,128)}, u32[]{:S(2)}) copy-start(f32[32,128,128]{2,1,0:T(8,128)} %copy-done.3) | copy-start | bytes 6291460
  43.2 1.2 %copy-start.1 = (bf16[32,16,1024]{2,1,0:T(8,128)(2,1)}, bf16[32,16,1024]{2,1,0:T(8,128)(2,1)S(1)}, u32[]{:S(2)}) copy-start(bf16[32,16,1024]{2,1,0:T(8,128)(2,1)S(1)} %collective-permute-done.2.slabs.q_other) | copy-start | bytes 3145732
  44.0 5.0 %collective-permute-start.3 = (bf16[16,128]{1,0:T(8,128)(2,1)S(1)}, bf16[16,128]{1,0:T(8,128)(2,1)S(1)}, u32[]{:S(2)}, u32[]{:S(2)}) collective-permute-start(bf16[16,128]{1,0:T(8,128)(2,1)S(1)} %get-tuple-element.16), channel_id=1, source_target_pairs={{0,4},{4,0},{1,5},{5,1},{2,6},{6,2},{3,7},{7,3},{8,12},{12,8},{9,1... | collective-permute-start | bytes 12296 | tf_op jit(solution)/shard_map/ppermute | solution.py:232
  44.4 1.6 %copy-start.6 = (f32[32,16,1024]{2,1,0:T(8,128)S(1)}, f32[32,16,1024]{2,1,0:T(8,128)}, u32[]{:S(2)}) copy-start(f32[32,16,1024]{2,1,0:T(8,128)} %copy-done.5) | copy-start | bytes 6291460
  81.3 12.7 %copy-start.2 = (bf16[32,16,1024]{2,1,0:T(8,128)(2,1)S(1)}, bf16[32,16,1024]{2,1,0:T(8,128)(2,1)}, u32[]{:S(2)}) copy-start(bf16[32,16,1024]{2,1,0:T(8,128)(2,1)} %copy-done.1) | copy-start | bytes 3145732
  82.2 12.5 %collective-permute-start.4 = (f32[16,1024]{1,0:T(8,128)S(1)}, f32[16,1024]{1,0:T(8,128)S(1)}, u32[]{:S(2)}, u32[]{:S(2)}) collective-permute-start(f32[16,1024]{1,0:T(8,128)S(1)} %get-tuple-element.18), channel_id=1, source_target_pairs={{0,32},{32,0},{1,33},{33,1},{2,34},{34,2},{3,35},{35,3},{4,36},{36... | collective-permute-start | bytes 196616 | tf_op jit(solution)/shard_map/ppermute | solution.py:232
  82.3 18.1 %all-to-all-start.2 = ((f32[8,40,128]{2,1,0:T(8,128)}), f32[8,40,128]{2,1,0:T(8,128)S(1)}, u32[]{:S(2)}, u32[]{:S(2)}) async-start(f32[8,40,128]{2,1,0:T(8,128)} %get-tuple-element.19), calls=%async_computation.2 | async-start | bytes 327680 | tf_op jit(solution)/shard_map/all_to_all | solution.py:286

commit v3 on v2

--- a/solution.py
+++ b/solution.py
@@ -39,34 +39,50 @@
     quarter = blocks[0].shape[0]
     live = counts[dp] - zl * quarter
     rows = lax.broadcasted_iota(jnp.int32, blocks[0].shape, 0) < live
-    for y in range(4):
-        for src, dst in ((blocks[y], keep), (blocks[4 + y], send)):
-            full = src[...]
-            masked = jnp.where(rows, full, jnp.zeros((), bf16))
-            dst[y] = dot(masked, full, 0, 0)
+    row = lax.broadcasted_iota(jnp.int32, (128, 128), 0)
+    col = lax.broadcasted_iota(jnp.int32, (128, 128), 1)
+    top = lax.broadcasted_iota(jnp.int32, (ROWS_EXTRA, 128), 0) == 0
+
+    def product(ref):
+        full = ref[...]
+        return dot(jnp.where(rows, full, jnp.zeros((), bf16)), full, 0, 0)
+
+    for y in range(2):
+        for at, dst in ((0, keep), (4, send)):
+            first = product(blocks[at + y])
+            second = product(blocks[at + 2 + y])
+            diag = jnp.sum(jnp.where(row == col, second, 0.0), axis=0, keepdims=True)
+            dst[y, 0:ROWS_OUT] = jnp.where(row <= col, first, second).astype(dst.dtype)
+            dst[y, ROWS_OUT:] = jnp.where(top, diag, 0.0).astype(dst.dtype)
 
 
 def cov_out_partial(output_grads, owners, counts, core):
     quarter = output_grads.shape[0]
 
-    def at(y, other):
+    def at(zh, y, other):
         def index(s, owners, counts, core):
             c = 1 - core[0] if other else core[0]
-            return (0, owners[(s * 4 + y) * 2 + c])
+            x, half = s // 2, s % 2
+            return (0, owners[((x * 2 + zh) * 4 + half * 2 + y) * 2 + c])
 
         return pl.BlockSpec((quarter, 128), index)
 
-    out = pl.BlockSpec((4, 128, 128), lambda s, *_: (s, 0, 0))
+    rows = ROWS_OUT + ROWS_EXTRA
+    out = pl.BlockSpec((2, rows, 128), lambda s, *_: (s, 0, 0))
+    order = [(zh, y, other) for other in (False, True) for zh in range(2) for y in range(2)]
     return pl.pallas_call(
         cov_out_kernel,
         grid_spec=pltpu.PrefetchScalarGridSpec(
             num_scalar_prefetch=3,
             grid=(8,),
-            in_specs=[at(y, False) for y in range(4)] + [at(y, True) for y in range(4)],
+            in_specs=[at(*o) for o in order],
             out_specs=[out, out],
         ),
-        out_shape=[jax.ShapeDtypeStruct((32, 128, 128), f32)] * 2,
-        compiler_params=pltpu.CompilerParams(vmem_limit_bytes=VMEM),
+        out_shape=[
+            jax.ShapeDtypeStruct((16, rows, 128), bf16),
+            jax.ShapeDtypeStruct((16, rows, 128), f32),
+        ],
+        compiler_params=pltpu.CompilerParams(vmem_limit_bytes=60 << 20),
         cost_estimate=pl.CostEstimate(
             flops=2 * quarter * 8192 * 128, bytes_accessed=quarter * 8192 * 2 + (4 << 20), transcendentals=0
         ),
@@ -79,14 +95,23 @@
     first = core == 0
     rows = lax.broadcasted_iota(jnp.int32, lhs.shape, 0) < counts[dp]
     masked = jnp.where(rows, lhs[...], jnp.zeros((), bf16))
-    part = dot(masked, rhs[...], 0, 0).reshape(8, 2, 16, 1024)
-    keep[...] = jnp.where(first, part[:, 0], part[:, 1])
-    send[...] = jnp.where(first, part[:, 1], part[:, 0])
+    part = dot(masked, rhs[...], 0, 0)
+    for zh in range(2):
+        for y in range(4):
+            at = (zh * 4 + y) * 32
+            low, high = part[at : at + 16], part[at + 16 : at + 32]
+            for dst, rows in (
+                (keep, jnp.where(first, low, high)),
+                (send, jnp.where(first, high, low).astype(bf16)),
+            ):
+                for c in range(8):
+                    at = c * 32 + zh * 16
+                    dst[y, at : at + 16] = rows[:, c * 128 : c * 128 + 128]
 
 
 def cov_in_partial(activations, counts):
     tok = activations.shape[0]
-    out = pl.BlockSpec((8, 16, 1024), lambda s, *_: (s, 0, 0))
+    out = pl.BlockSpec((4, ROWS_IN, 128), lambda s, *_: (s, 0, 0))
     return pl.pallas_call(
         cov_in_kernel,
         grid_spec=pltpu.PrefetchScalarGridSpec(
@@ -98,7 +123,10 @@
             ],
             out_specs=[out, out],
         ),
-        out_shape=[jax.ShapeDtypeStruct((32, 16, 1024), f32)] * 2,
+        out_shape=[
+            jax.ShapeDtypeStruct((16, ROWS_IN, 128), bf16),
+            jax.ShapeDtypeStruct((16, ROWS_IN, 128), f32),
+        ],
         compiler_params=pltpu.CompilerParams(vmem_limit_bytes=VMEM),
         cost_estimate=pl.CostEstimate(
             flops=2 * tok * 1024 * 1024, bytes_accessed=tok * 4096 + (4 << 20), transcendentals=0
@@ -107,46 +135,26 @@
     )(counts, activations, activations)
 
 
-def pack_kernel(keep_out, recv_out, keep_in, recv_in, msg):
-    row = lax.broadcasted_iota(jnp.int32, (128, 128), 0)
-    col = lax.broadcasted_iota(jnp.int32, (128, 128), 1)
-    for y in range(4):
-        first = keep_out[0, y] + recv_out[0, y]
-        second = keep_out[1, y] + recv_out[1, y]
-        msg[y, ROWS_IN : ROWS_IN + ROWS_OUT] = jnp.where(row <= col, first, second).astype(bf16)
-        diag = jnp.sum(jnp.where(row == col, second, 0.0), axis=0, keepdims=True)
-        top = lax.broadcasted_iota(jnp.int32, (ROWS_EXTRA, 128), 0) == 0
-        msg[y, ROWS_IN + ROWS_OUT :] = jnp.where(top, diag, 0.0).astype(bf16)
-        for zh in range(2):
-            rows = (keep_in[zh, y] + recv_in[zh, y]).astype(bf16)
-            for c in range(8):
-                msg[y, c * 32 + zh * 16 : c * 32 + zh * 16 + 16] = rows[:, c * 128 : c * 128 + 128]
-
-
-def pack(keep_out, recv_out, keep_in, recv_in):
-    outs = pl.BlockSpec((2, 4, 128, 128), lambda x: (x, 0, 0, 0))
-    ins = pl.BlockSpec((2, 4, 16, 1024), lambda x: (x, 0, 0, 0))
-    return pl.pallas_call(
-        pack_kernel,
-        grid=(4,),
-        in_specs=[outs, outs, ins, ins],
-        out_specs=pl.BlockSpec((4, ROWS, 128), lambda x: (x, 0, 0)),
-        out_shape=jax.ShapeDtypeStruct((16, ROWS, 128), bf16),
-        compiler_params=pltpu.CompilerParams(vmem_limit_bytes=VMEM),
-        cost_estimate=pl.CostEstimate(flops=4 << 20, bytes_accessed=10 << 20, transcendentals=0),
-        name="pack",
-    )(
-        keep_out.reshape(8, 4, 128, 128),
-        recv_out.reshape(8, 4, 128, 128),
-        keep_in.reshape(8, 4, 16, 1024),
-        recv_in.reshape(8, 4, 16, 1024),
-    )
+def pack_kernel(keep_in, recv_in, keep_out, recv_out, msg):
+    def step(s, _):
+        msg[s, 0:ROWS_IN] = (keep_in[s] + recv_in[s].astype(f32)).astype(bf16)
+        msg[s, ROWS_IN:] = (keep_out[s] + recv_out[s].astype(f32)).astype(bf16)
+        return 0
+
+    lax.fori_loop(0, 16, step, 0)
+
+
+def slab_rows(core):
+    zh = lax.axis_index("zh")
+    for x in range(4):
+        for y in range(4):
+            for z in (zh, 1 - zh):
+                slab = ((x * 2 + z) * 4 + y) * 2 + core
+                yield pl.ds(pl.multiple_of(slab * 16, 16), 16)
 
 
 def dot_slabs(left, slabs, core):
-    picked = jnp.concatenate(
-        [left[pl.ds(pl.multiple_of((2 * s + core) * 16, 16), 16), :] for s in range(32)], axis=0
-    )
+    picked = jnp.concatenate([left[rows, :] for rows in slab_rows(core)], axis=0)
     return dot(picked, slabs[...].reshape(512, 1024), 0, 0)
 
 
@@ -178,9 +186,15 @@
     core = lax.axis_index("core")
     for src, c in ((q_own, core), (q_other, 1 - core)):
         result = dot(src[...].reshape(512, 1024), back[...], 1, 1)
-        for s in range(32):
-            at = pl.multiple_of((2 * s + c) * 16, 16)
-            precond[pl.ds(at, 16), :] = result[s * 16 : s * 16 + 16]
+        for s, rows in enumerate(slab_rows(c)):
+            precond[rows, :] = result[s * 16 : s * 16 + 16]
+
+
+def clip_kernel(scalars, column, precond, cov_out, update):
+    total = jnp.sum(column[...], axis=0)
+    cov_out[0] = total[0:32] / scalars[0]
+    rate = scalars[1]
+    update[...] = jnp.minimum(1.0, jnp.sqrt(kl_clip / (rate * rate * total[32:33]))) * precond[...]
 
 
 def on_chip(kernel, outs, flops, *args):
@@ -188,7 +202,7 @@
     size = sum(a.size * a.dtype.itemsize for a in args)
     return pl.pallas_call(
         kernel,
-        in_specs=[whole] * len(args),
+        in_specs=[whole if a.ndim > 1 else pl.BlockSpec(memory_space=pltpu.SMEM) for a in args],
         out_specs=[whole] * len(outs),
         out_shape=outs,
         compiler_params=pltpu.CompilerParams(vmem_limit_bytes=VMEM),
@@ -246,15 +260,21 @@
 ):
     token_total = jnp.sum(token_counts).astype(f32)
     shape = jax.ShapeDtypeStruct
-    slabs = jnp.broadcast_to(basis_in, (32,) + basis_in.shape[1:])
-    q_own = lax.all_to_all(slabs, ("x", "zh", "y"), 0, 0, tiled=True)
-
     core = lax.axis_index("core").astype(jnp.int32)[None]
+    mine = basis_in[0]
+    slabs = jnp.concatenate([mine, swap(mine, "zh")], axis=0)
     send_out, keep_out = cov_out_partial(output_grads, owner_blocks, token_counts, core)
+    slabs, send_out, counts = lax.optimization_barrier((slabs, send_out, token_counts))
+    q_own = lax.all_to_all(
+        jnp.broadcast_to(slabs[None], (16,) + slabs.shape), PLANE, 0, 0, tiled=True
+    )
     recv_out = swap(send_out, "core")
-    send_in, keep_in = cov_in_partial(activations, token_counts)
+    send_in, keep_in = cov_in_partial(activations, counts)
     recv_in = swap(send_in, "core")
-    msg = pack(keep_out, recv_out, keep_in, recv_in)
+    q_own, keep_in, recv_out = lax.optimization_barrier((q_own, keep_in, recv_out))
+    (msg,) = on_chip(
+        pack_kernel, [shape((16, ROWS, 128), bf16)], 1 << 20, keep_in, recv_in, keep_out, recv_out
+    )
 
     q_other = swap(q_own, "core")
     (partial,) = on_chip(rotate_kernel, [shape((128, 1024), f32)], 128 << 20, q_own, gradient)
@@ -269,7 +289,8 @@
         values_in[None, :],
         values_out[:, None],
     )
-    parts = jnp.concatenate([parts[1:4], swap(parts, "core")[1:4]], axis=0)
+    other_parts, msg = lax.optimization_barrier((swap(parts, "core"), msg))
+    parts = jnp.concatenate([parts[1:4], other_parts[1:4]], axis=0)
     (precond,) = on_chip(finish_kernel, [shape((1024, 128), f32)], 256 << 20, q_own, q_other, back)
     at = ROWS_IN + ROWS_OUT + 1
     msg = lax.dynamic_update_slice(
@@ -285,12 +306,14 @@
     recv_slab = swap(send_slab, "zh")
     column = lax.all_to_all(column, COLUMN, 0, 0, tiled=True)
     cov_in = ((keep_slab + recv_slab) / token_total)[None]
-    cov_out = (jnp.sum(column[:, :32], axis=0) / token_total)[None]
-    inner = jnp.sum(column[:, 32, 0], axis=0)
-    clip_factor = jnp.minimum(
-        1.0, jnp.sqrt(kl_clip / (learning_rate[0] * learning_rate[0] * inner))
-    )
-    update = clip_factor * precond
+    cov_out, update = on_chip(
+        clip_kernel,
+        [shape((1, 32, 128), f32), shape((1024, 128), f32)],
+        1 << 20,
+        jnp.stack([token_total, learning_rate[0]]),
+        column,
+        precond,
+    )
     return (cov_in, cov_out, update)
 
 

time: 104 us -> 98.5 us (0.947)
  blocking collectives: 32.1 us -> 0 us
  waiting for transfers between devices: 12.7 us -> 34.5 us
  starting transfers between devices: 27.7 us -> 31.9 us
  local copies, waits for them, and re-layouts: 7.42 us -> 9.82 us
  other arithmetic: 3.36 us -> 1.36 us
    all_to_all x1 -> x0, blocking collectives: 32.1 us -> none  [local(): msg = lax.all_to_all(msg, PLANE, 0, 0, tiled=True)]
    all_to_all x1 -> x2, waiting for transfers between devices: 5.86 us -> 27.6 us  [the longest x1 22.4 us: local(): msg = lax.all_to_all(msg, PLANE, 0, 0, tiled=True)]
    ppermute x5 -> x6, starting transfers between devices: 3.38 us -> 18.1 us  [swap(): return lax.ppermute(array, axis, [(0, 1), (1, 0)])]
    all_to_all x1, starting transfers between devices: 9.85 us -> 3.38 us  [local(): column = lax.all_to_all(column, COLUMN, 0, 0, tiled=True)]
    ppermute x5 -> x6, waiting for transfers between devices: 1.82 us -> 6.88 us  [swap(): return lax.ppermute(array, axis, [(0, 1), (1, 0)])]
    all_to_all x1, waiting for transfers between devices: 4.98 us -> 0.01 us  [local(): column = lax.all_to_all(column, COLUMN, 0, 0, tiled=True)]
    all_to_all x1 -> x2, starting transfers between devices: 14.5 us -> 10.5 us  [the longest x1 6.74 us: local(): lax.all_to_all(jnp.broadcast_to(slabs[None], (16,) + slabs.shape), PLANE,...]
    unnamed x28 -> x36, local copies, waits for them, and re-layouts: 5.2 us -> 7.1 us
  transfers between devices with their start and end apart: 7 -> 9, of which waited for: 3 -> 4; matrix products, arithmetic and copies ran while one was open for 1% -> 2% of each run, Pallas kernels for 16% -> 16%
where the time goes in v3:
time: 98.5 us; the launch traced here: 97.5 us
  waiting for transfers between devices  34.5 us (35%)
  starting transfers between devices  31.9 us (32%)
  Pallas kernels  17.8 us (18%)
  local copies, waits for them, and re-layouts  9.82 us (10%)
  between operations  2.13 us (2%)
  other arithmetic  1.36 us (1%)
    all_to_all x1, waiting for transfers between devices, local(): msg = lax.all_to_all(msg, PLANE, 0, 0, tiled=True)  22.4 us
    ppermute x6, starting transfers between devices, swap(): return lax.ppermute(array, axis, [(0, 1), (1, 0)])  18.1 us
    pallas_call x1, Pallas kernels, cov_out_partial(): pl.pallas_call(cov_out_kernel, grid_spec=pltpu.PrefetchScalarGridSpec(num...  8.07 us
    unnamed x36, local copies, waits for them, and re-layouts  7.1 us
    ppermute x6, waiting for transfers between devices, swap(): return lax.ppermute(array, axis, [(0, 1), (1, 0)])  6.88 us
    all_to_all x1, starting transfers between devices, local(): lax.all_to_all(jnp.broadcast_to(slabs[None], (16,) + slabs.shape), PLANE,...  6.74 us
    pallas_call x6, Pallas kernels, on_chip(): pl.pallas_call(kernel, in_specs=[whole if a.ndim > 1 else pl.BlockSpec(me...  5.78 us
    all_to_all x1, waiting for transfers between devices, local(): lax.all_to_all(jnp.broadcast_to(slabs[None], (16,) + slabs.shape), PLANE,...  5.17 us
  transfers between devices with their start and end apart: 9, of which 4 were waited for; matrix products, arithmetic and copies ran while one was open for 2% of the time, Pallas kernels for 16%

profile of v3, /device:TPU:1, one launch (start us, length us, event | category | flops | bytes accessed | tf_op | source)
XLA Modules:
  0.0 97.5 jit_solution(3461347708300260811)
XLA Ops:
  0.6 7.8 %collective-permute-start = (bf16[16,1024]{1,0:T(8,128)(2,1)}, bf16[16,1024]{1,0:T(8,128)(2,1)S(1)}, u32[]{:S(2)}, u32[]{:S(2)}) collective-permute-start(bf16[16,1024]{1,0:T(8,128)(2,1)} %bitcast.10), channel_id=1, source_target_pairs={{0,32},{32,0},{1,33},{33,1},{2,34},{34,2},{3,35},{35,3},{4,36},{36... | collective-permute-start | bytes 98312 | tf_op jit(solution)/shard_map/ppermute | solution.py:246
  8.5 8.1 %cov_out_partial.1 = (bf16[16,144,128]{2,1,0:T(8,128)(2,1)}, f32[16,144,128]{2,1,0:T(8,128)}) custom-call(s32[64]{0:T(128)} %owners.1, s32[64]{0:T(128)} %counts.2, s32[1]{0:T(128)} %bitcast.1.core, bf16[256,8192]{1,0:T(8,128)(2,1)} %refs_7_.1, bf16[256,8192]{1,0:T(8,128)(2,1)} %refs_7_.1, bf16[256,8192]{1,0:T(8,128)(2,1)} %refs_7_.1, ...), custom_call_target="tpu_custom_call" | custom-call | flops 536870912 | bytes 8388608 | tf_op jit(solution)/shard_map/cov_out_partial/pallas_call | solution.py:73
  16.6 1.1 %broadcast_in_dim.25 = bf16[16,32,1024]{2,1,0:T(8,128)(2,1)} broadcast(bf16[32,1024]{1,0:T(8,128)(2,1)S(1)} %pad_maximum_fusion), dimensions={1,2} | broadcast | bytes 1114112 | tf_op jit(solution)/shard_map/broadcast_in_dim | solution.py:269
  17.7 6.7 %all-to-all-start = ((bf16[16,32,1024]{2,1,0:T(8,128)(2,1)}), bf16[16,32,1024]{2,1,0:T(8,128)(2,1)S(1)}, u32[]{:S(2)}, u32[]{:S(2)}) async-start(bf16[16,32,1024]{2,1,0:T(8,128)(2,1)} %broadcast_in_dim.25), calls=%async_computation | async-start | bytes 2097152 | tf_op jit(solution)/shard_map/all_to_all | solution.py:268
  24.5 1.3 %collective-permute-start.1 = (bf16[16,144,128]{2,1,0:T(8,128)(2,1)S(1)}, bf16[16,144,128]{2,1,0:T(8,128)(2,1)S(1)}, u32[]{:S(2)}, u32[]{:S(2)}) collective-permute-start(bf16[16,144,128]{2,1,0:T(8,128)(2,1)S(1)} %copy-done.17), channel_id=1, source_target_pairs={{0,4},{4,0},{1,5},{5,1},{2,6},{6,2},{3,7},{7,3},{8,12},{12,8},{9,1... | collective-permute-start | bytes 1769480 | tf_op jit(solution)/shard_map/ppermute | solution.py:246
  25.8 1.6 %copy-done.13 = bf16[1024,1024]{1,0:T(8,128)(2,1)S(1)} copy-done((bf16[1024,1024]{1,0:T(8,128)(2,1)S(1)}, bf16[1024,1024]{1,0:T(8,128)(2,1)}, u32[]{:S(2)}) %copy-start.13) | copy-done | bytes 2097176
  27.4 4.0 %cov_in_partial.1 = (bf16[16,256,128]{2,1,0:T(8,128)(2,1)S(1)}, f32[16,256,128]{2,1,0:T(8,128)S(1)}) custom-call(s32[64]{0:T(128)S(1)} %copy-done.12, bf16[1024,1024]{1,0:T(8,128)(2,1)S(1)} %copy-done.13, bf16[1024,1024]{1,0:T(8,128)(2,1)S(1)} %copy-done.13), custom_call_target="tpu_custom_call" | custom-call | flops 2147483648 | bytes 8388608 | tf_op jit(solution)/shard_map/cov_in_partial/pallas_call | solution.py:115
  31.4 1.4 %copy-done.2 = f32[16,256,128]{2,1,0:T(8,128)} copy-done((f32[16,256,128]{2,1,0:T(8,128)}, f32[16,256,128]{2,1,0:T(8,128)S(1)}, u32[]{:S(2)}) %copy-start.2) | copy-done | bytes 2097176
  32.7 1.0 %copy-done.14 = bf16[16,256,128]{2,1,0:T(8,128)(2,1)} copy-done((bf16[16,256,128]{2,1,0:T(8,128)(2,1)}, bf16[16,256,128]{2,1,0:T(8,128)(2,1)S(1)}, u32[]{:S(2)}) %copy-start.14) | copy-done | bytes 1048600
  33.8 0.8 copy-done.6
  34.6 5.2 %all-to-all-done.slabs.q_own = bf16[16,32,1024]{2,1,0:T(8,128)(2,1)S(1)} async-done(((bf16[16,32,1024]{2,1,0:T(8,128)(2,1)}), bf16[16,32,1024]{2,1,0:T(8,128)(2,1)S(1)}, u32[]{:S(2)}, u32[]{:S(2)}) %all-to-all-start) | async-done | bytes 1048608 | tf_op jit(solution)/shard_map/all_to_all | solution.py:268
  39.7 3.2 %collective-permute-start.2 = (bf16[16,32,1024]{2,1,0:T(8,128)(2,1)S(1)}, bf16[16,32,1024]{2,1,0:T(8,128)(2,1)S(1)}, u32[]{:S(2)}, u32[]{:S(2)}) collective-permute-start(bf16[16,32,1024]{2,1,0:T(8,128)(2,1)S(1)} %all-to-all-done.slabs.q_own), channel_id=1, source_target_pairs={{0,4},{4,0},{1,5},{5,1},{2,6},{6,2},{3,7},{7,3},{8,12},{12,8},{9,1... | collective-permute-start | bytes 3145736 | tf_op jit(solution)/shard_map/ppermute | solution.py:246
  43.5 3.3 %collective-permute-done.2.slabs.q_other = bf16[16,32,1024]{2,1,0:T(8,128)(2,1)S(1)} collective-permute-done((bf16[16,32,1024]{2,1,0:T(8,128)(2,1)S(1)}, bf16[16,32,1024]{2,1,0:T(8,128)(2,1)S(1)}, u32[]{:S(2)}, u32[]{:S(2)}) %collective-permute-start.2) | collective-permute-done | bytes 1048608 | tf_op jit(solution)/shard_map/ppermute | solution.py:246
  48.0 1.1 %copy-done.7 = bf16[16,144,128]{2,1,0:T(8,128)(2,1)S(1)} copy-done((bf16[16,144,128]{2,1,0:T(8,128)(2,1)S(1)}, bf16[16,144,128]{2,1,0:T(8,128)(2,1)}, u32[]{:S(2)}) %copy-start.7) | copy-done | bytes 589848
  49.1 1.6 %pack.1 = bf16[16,400,128]{2,1,0:T(8,128)(2,1)} custom-call(f32[16,256,128]{2,1,0:T(8,128)S(1)} %copy-done.3, bf16[16,256,128]{2,1,0:T(8,128)(2,1)S(1)} %collective-permute-done.4.recv_in, f32[16,144,128]{2,1,0:T(8,128)S(1)} %copy-done.4, bf16[16,144,128]{2,1,0:T(8,128)(2,1)S(1)} %copy-done.7), custom_call_target="tpu_custom_call" | custom-call | flops 1048576 | bytes 4915200 | tf_op jit(solution)/shard_map/pack/pallas_call | solution.py:203
  50.7 1.4 %dynamic_update_slice.3 = bf16[16,400,128]{2,1,0:T(8,128)(2,1)} dynamic-update-slice(bf16[16,400,128]{2,1,0:T(8,128)(2,1)} %pack.1, bf16[16,6,128]{2,1,0:T(8,128)(2,1)S(1)} %broadcast_in_dim.28, s32[]{:T(128)} %constant.8.clone.1, s32[]{:T(128)} %constant.9.clone.1, s32[]{:T(128)} %constant.8.clone.1) | dynamic-update-slice | bytes 49156 | tf_op jit(solution)/shard_map/dynamic_update_slice | solution.py:296
  52.1 3.7 %all-to-all-start.1 = ((bf16[16,400,128]{2,1,0:T(8,128)(2,1)}), bf16[16,400,128]{2,1,0:T(8,128)(2,1)S(1)}, u32[]{:S(2)}, u32[]{:S(2)}) async-start(bf16[16,400,128]{2,1,0:T(8,128)(2,1)} %dynamic_update_slice.3), calls=%async_computation.1 | async-start | bytes 3276800 | tf_op jit(solution)/shard_map/all_to_all | solution.py:299
  57.8 22.4 %all-to-all-done.1.msg = bf16[16,400,128]{2,1,0:T(8,128)(2,1)S(1)} async-done(((bf16[16,400,128]{2,1,0:T(8,128)(2,1)}), bf16[16,400,128]{2,1,0:T(8,128)(2,1)S(1)}, u32[]{:S(2)}, u32[]{:S(2)}) %all-to-all-start.1) | async-done | bytes 1638432 | tf_op jit(solution)/shard_map/all_to_all | solution.py:299
  80.2 1.0 unpack.1
  81.2 3.4 %all-to-all-start.2 = ((f32[8,40,128]{2,1,0:T(8,128)}), f32[8,40,128]{2,1,0:T(8,128)S(1)}, u32[]{:S(2)}, u32[]{:S(2)}) async-start(f32[8,40,128]{2,1,0:T(8,128)} %get-tuple-element.37), calls=%async_computation.2 | async-start | bytes 327680 | tf_op jit(solution)/shard_map/all_to_all | solution.py:307
  84.6 5.3 %collective-permute-start.5 = (f32[16,1024]{1,0:T(8,128)S(1)}, f32[16,1024]{1,0:T(8,128)S(1)}, u32[]{:S(2)}, u32[]{:S(2)}) collective-permute-start(f32[16,1024]{1,0:T(8,128)S(1)} %get-tuple-element.36), channel_id=1, source_target_pairs={{0,32},{32,0},{1,33},{33,1},{2,34},{34,2},{3,35},{35,3},{4,36},{36... | collective-permute-start | bytes 196616 | tf_op jit(solution)/shard_map/ppermute | solution.py:246
  89.9 1.2 %copy-done.1 = bf16[16,32,1024]{2,1,0:T(8,128)(2,1)S(1)} copy-done((bf16[16,32,1024]{2,1,0:T(8,128)(2,1)S(1)}, bf16[16,32,1024]{2,1,0:T(8,128)(2,1)}, u32[]{:S(2)}) %copy-start.1) | copy-done | bytes 1048600
  91.9 3.6 %collective-permute-done.5 = f32[16,1024]{1,0:T(8,128)S(1)} collective-permute-done((f32[16,1024]{1,0:T(8,128)S(1)}, f32[16,1024]{1,0:T(8,128)S(1)}, u32[]{:S(2)}, u32[]{:S(2)}) %collective-permute-start.5) | collective-permute-done | bytes 65568 | tf_op jit(solution)/shard_map/ppermute | solution.py:246
  96.1 1.4 %clip.1 = (f32[1,32,128]{2,1,0:T(8,128)}, f32[1024,128]{1,0:T(8,128)}) custom-call(f32[2]{0:T(128)S(1)} %pad_maximum_fusion.2.scalars, f32[8,40,128]{2,1,0:T(8,128)S(1)} %all-to-all-done.2.column, f32[1024,128]{1,0:T(8,128)S(1)} %finish.1.precond), custom_call_target="tpu_custom_call" | custom-call | flops 1048576 | bytes 688136 | tf_op jit(solution)/shard_map/clip/pallas_call | solution.py:203
  (49 shorter events, 3.9 us)
Async XLA Ops:
  0.6 15.9 %collective-permute-start = (bf16[16,1024]{1,0:T(8,128)(2,1)}, bf16[16,1024]{1,0:T(8,128)(2,1)S(1)}, u32[]{:S(2)}, u32[]{:S(2)}) collective-permute-start(bf16[16,1024]{1,0:T(8,128)(2,1)} %bitcast.10), channel_id=1, source_target_pairs={{0,32},{32,0},{1,33},{33,1},{2,34},{34,2},{3,35},{35,3},{4,36},{36... | collective-permute-start | bytes 98312 | tf_op jit(solution)/shard_map/ppermute | solution.py:246
  8.5 8.1 %copy-start.15 = (bf16[1,16,1024]{2,1,0:T(8,128)(2,1)S(1)}, bf16[1,16,1024]{2,1,0:T(8,128)(2,1)}, u32[]{:S(2)}) copy-start(bf16[1,16,1024]{2,1,0:T(8,128)(2,1)} %param.14) | copy-start | bytes 98308
  16.6 7.9 %copy-start.17 = (bf16[16,144,128]{2,1,0:T(8,128)(2,1)S(1)}, bf16[16,144,128]{2,1,0:T(8,128)(2,1)}, u32[]{:S(2)}) copy-start(bf16[16,144,128]{2,1,0:T(8,128)(2,1)} %get-tuple-element.26) | copy-start | bytes 1769476
  16.6 9.2 %copy-start.12 = (s32[64]{0:T(128)S(1)}, s32[64]{0:T(128)}, u32[]{:S(2)}) copy-start(s32[64]{0:T(128)} %counts.2) | copy-start | bytes 772
  17.7 22.0 %all-to-all-start = ((bf16[16,32,1024]{2,1,0:T(8,128)(2,1)}), bf16[16,32,1024]{2,1,0:T(8,128)(2,1)S(1)}, u32[]{:S(2)}, u32[]{:S(2)}) async-start(bf16[16,32,1024]{2,1,0:T(8,128)(2,1)} %broadcast_in_dim.25), calls=%async_computation | async-start | bytes 2097152 | tf_op jit(solution)/shard_map/all_to_all | solution.py:268
  24.5 18.6 %copy-start.5 = (bf16[1024,128]{1,0:T(8,128)(2,1)S(1)}, bf16[1024,128]{1,0:T(8,128)(2,1)}, u32[]{:S(2)}) copy-start(bf16[1024,128]{1,0:T(8,128)(2,1)} %grad.3) | copy-start | bytes 786436
  24.5 9.3 %collective-permute-start.1 = (bf16[16,144,128]{2,1,0:T(8,128)(2,1)S(1)}, bf16[16,144,128]{2,1,0:T(8,128)(2,1)S(1)}, u32[]{:S(2)}, u32[]{:S(2)}) collective-permute-start(bf16[16,144,128]{2,1,0:T(8,128)(2,1)S(1)} %copy-done.17), channel_id=1, source_target_pairs={{0,4},{4,0},{1,5},{5,1},{2,6},{6,2},{3,7},{7,3},{8,12},{12,8},{9,1... | collective-permute-start | bytes 1769480 | tf_op jit(solution)/shard_map/ppermute | solution.py:246
  25.8 1.6 %copy-start.13 = (bf16[1024,1024]{1,0:T(8,128)(2,1)S(1)}, bf16[1024,1024]{1,0:T(8,128)(2,1)}, u32[]{:S(2)}) copy-start(bf16[1024,1024]{1,0:T(8,128)(2,1)} %rhs.1) | copy-start | bytes 6291460
  27.4 15.6 %copy-start.16 = (f32[128]{0:T(128)S(1)}, f32[128]{0:T(128)}, u32[]{:S(2)}) copy-start(f32[128]{0:T(128)} %param.17) | copy-start | bytes 1540
  31.4 1.4 %copy-start.2 = (f32[16,256,128]{2,1,0:T(8,128)}, f32[16,256,128]{2,1,0:T(8,128)S(1)}, u32[]{:S(2)}) copy-start(f32[16,256,128]{2,1,0:T(8,128)S(1)} %get-tuple-element.29.keep_in) | copy-start | bytes 6291460
  33.8 13.0 %copy-start.10 = (bf16[1,128,128]{2,1,0:T(8,128)(2,1)S(1)}, bf16[1,128,128]{2,1,0:T(8,128)(2,1)}, u32[]{:S(2)}) copy-start(bf16[1,128,128]{2,1,0:T(8,128)(2,1)} %param.15) | copy-start | bytes 98308
  33.8 13.0 %copy-start.11 = (f32[1024]{0:T(1024)S(1)}, f32[1024]{0:T(1024)}, u32[]{:S(2)}) copy-start(f32[1024]{0:T(1024)} %param.16) | copy-start | bytes 12292
  39.7 7.0 %collective-permute-start.2 = (bf16[16,32,1024]{2,1,0:T(8,128)(2,1)S(1)}, bf16[16,32,1024]{2,1,0:T(8,128)(2,1)S(1)}, u32[]{:S(2)}, u32[]{:S(2)}) collective-permute-start(bf16[16,32,1024]{2,1,0:T(8,128)(2,1)S(1)} %all-to-all-done.slabs.q_own), channel_id=1, source_target_pairs={{0,4},{4,0},{1,5},{5,1},{2,6},{6,2},{3,7},{7,3},{8,12},{12,8},{9,1... | collective-permute-start | bytes 3145736 | tf_op jit(solution)/shard_map/ppermute | solution.py:246
  43.0 5.0 %collective-permute-start.4 = (bf16[16,256,128]{2,1,0:T(8,128)(2,1)}, bf16[16,256,128]{2,1,0:T(8,128)(2,1)S(1)}, u32[]{:S(2)}, u32[]{:S(2)}) collective-permute-start(bf16[16,256,128]{2,1,0:T(8,128)(2,1)} %copy-done.14), channel_id=1, source_target_pairs={{0,4},{4,0},{1,5},{5,1},{2,6},{6,2},{3,7},{7,3},{8,12},{12,8},{9,1... | collective-permute-start | bytes 3145736 | tf_op jit(solution)/shard_map/ppermute | solution.py:246
  43.1 4.9 %copy-start.3 = (f32[16,256,128]{2,1,0:T(8,128)S(1)}, f32[16,256,128]{2,1,0:T(8,128)}, u32[]{:S(2)}) copy-start(f32[16,256,128]{2,1,0:T(8,128)} %copy-done.2) | copy-start | bytes 6291460
  43.1 4.9 %copy-start.4 = (f32[16,144,128]{2,1,0:T(8,128)S(1)}, f32[16,144,128]{2,1,0:T(8,128)}, u32[]{:S(2)}) copy-start(f32[16,144,128]{2,1,0:T(8,128)} %get-tuple-element.31.keep_out) | copy-start | bytes 3538948
  46.7 3.9 %copy-start = (bf16[16,32,1024]{2,1,0:T(8,128)(2,1)}, bf16[16,32,1024]{2,1,0:T(8,128)(2,1)S(1)}, u32[]{:S(2)}) copy-start(bf16[16,32,1024]{2,1,0:T(8,128)(2,1)S(1)} %collective-permute-done.2.slabs.q_other) | copy-start | bytes 3145732
  47.5 3.1 %copy-start.8 = (bf16[128,1024]{1,0:T(8,128)(2,1)}, bf16[128,1024]{1,0:T(8,128)(2,1)S(1)}, u32[]{:S(2)}) copy-start(bf16[128,1024]{1,0:T(8,128)(2,1)S(1)} %get-tuple-element.38.back) | copy-start | bytes 786436
  47.5 3.1 %collective-permute-start.3 = (bf16[16,128]{1,0:T(8,128)(2,1)S(1)}, bf16[16,128]{1,0:T(8,128)(2,1)S(1)}, u32[]{:S(2)}, u32[]{:S(2)}) collective-permute-start(bf16[16,128]{1,0:T(8,128)(2,1)S(1)} %get-tuple-element.28), channel_id=1, source_target_pairs={{0,4},{4,0},{1,5},{5,1},{2,6},{6,2},{3,7},{7,3},{8,12},{12,8},{9,1... | collective-permute-start | bytes 12296 | tf_op jit(solution)/shard_map/ppermute | solution.py:246
  52.1 28.1 %all-to-all-start.1 = ((bf16[16,400,128]{2,1,0:T(8,128)(2,1)}), bf16[16,400,128]{2,1,0:T(8,128)(2,1)S(1)}, u32[]{:S(2)}, u32[]{:S(2)}) async-start(bf16[16,400,128]{2,1,0:T(8,128)(2,1)} %dynamic_update_slice.3), calls=%async_computation.1 | async-start | bytes 3276800 | tf_op jit(solution)/shard_map/all_to_all | solution.py:299
  55.8 34.1 %copy-start.9 = (bf16[128,1024]{1,0:T(8,128)(2,1)S(1)}, bf16[128,1024]{1,0:T(8,128)(2,1)}, u32[]{:S(2)}) copy-start(bf16[128,1024]{1,0:T(8,128)(2,1)} %copy-done.8) | copy-start | bytes 786436
  81.2 15.0 %all-to-all-start.2 = ((f32[8,40,128]{2,1,0:T(8,128)}), f32[8,40,128]{2,1,0:T(8,128)S(1)}, u32[]{:S(2)}, u32[]{:S(2)}) async-start(f32[8,40,128]{2,1,0:T(8,128)} %get-tuple-element.37), calls=%async_computation.2 | async-start | bytes 327680 | tf_op jit(solution)/shard_map/all_to_all | solution.py:307
  84.6 10.9 %collective-permute-start.5 = (f32[16,1024]{1,0:T(8,128)S(1)}, f32[16,1024]{1,0:T(8,128)S(1)}, u32[]{:S(2)}, u32[]{:S(2)}) collective-permute-start(f32[16,1024]{1,0:T(8,128)S(1)} %get-tuple-element.36), channel_id=1, source_target_pairs={{0,32},{32,0},{1,33},{33,1},{2,34},{34,2},{3,35},{35,3},{4,36},{36... | collective-permute-start | bytes 196616 | tf_op jit(solution)/shard_map/ppermute | solution.py:246
  89.9 1.2 %copy-start.1 = (bf16[16,32,1024]{2,1,0:T(8,128)(2,1)S(1)}, bf16[16,32,1024]{2,1,0:T(8,128)(2,1)}, u32[]{:S(2)}) copy-start(bf16[16,32,1024]{2,1,0:T(8,128)(2,1)} %copy-done) | copy-start | bytes 3145732
  (3 other events, 2.9 us)

commit v4 on v3

--- a/solution.py
+++ b/solution.py
@@ -20,7 +20,6 @@
 ROWS_IN = 256
 ROWS_OUT = 128
 ROWS_EXTRA = 16
-ROWS = ROWS_IN + ROWS_OUT + ROWS_EXTRA
 
 
 def dot(a, b, ca, cb):
@@ -43,14 +42,12 @@
     col = lax.broadcasted_iota(jnp.int32, (128, 128), 1)
     top = lax.broadcasted_iota(jnp.int32, (ROWS_EXTRA, 128), 0) == 0
 
-    def product(ref):
-        full = ref[...]
-        return dot(jnp.where(rows, full, jnp.zeros((), bf16)), full, 0, 0)
-
+    rows = jnp.concatenate([rows, rows], axis=1)
     for y in range(2):
         for at, dst in ((0, keep), (4, send)):
-            first = product(blocks[at + y])
-            second = product(blocks[at + 2 + y])
+            full = jnp.concatenate([blocks[at + y][...], blocks[at + 2 + y][...]], axis=1)
+            both = dot(jnp.where(rows, full, jnp.zeros((), bf16)), full, 0, 0)
+            first, second = both[:128, :128], both[128:, 128:]
             diag = jnp.sum(jnp.where(row == col, second, 0.0), axis=0, keepdims=True)
             dst[y, 0:ROWS_OUT] = jnp.where(row <= col, first, second).astype(dst.dtype)
             dst[y, ROWS_OUT:] = jnp.where(top, diag, 0.0).astype(dst.dtype)
@@ -82,7 +79,7 @@
             jax.ShapeDtypeStruct((16, rows, 128), bf16),
             jax.ShapeDtypeStruct((16, rows, 128), f32),
         ],
-        compiler_params=pltpu.CompilerParams(vmem_limit_bytes=60 << 20),
+        compiler_params=pltpu.CompilerParams(vmem_limit_bytes=VMEM),
         cost_estimate=pl.CostEstimate(
             flops=2 * quarter * 8192 * 128, bytes_accessed=quarter * 8192 * 2 + (4 << 20), transcendentals=0
         ),
@@ -135,10 +132,29 @@
     )(counts, activations, activations)
 
 
-def pack_kernel(keep_in, recv_in, keep_out, recv_out, msg):
+def pack_in_kernel(keep, recv, msg):
     def step(s, _):
-        msg[s, 0:ROWS_IN] = (keep_in[s] + recv_in[s].astype(f32)).astype(bf16)
-        msg[s, ROWS_IN:] = (keep_out[s] + recv_out[s].astype(f32)).astype(bf16)
+        msg[s] = (keep[s] + recv[s].astype(f32)).astype(bf16)
+        return 0
+
+    lax.fori_loop(0, 16, step, 0)
+
+
+def pack_out_kernel(keep, recv, inner, other_inner, msg):
+    total = inner[0:1] + other_inner[0:1]
+    high = total.astype(bf16).astype(f32)
+    rest = total - high
+    middle = rest.astype(bf16).astype(f32)
+    low = rest - middle
+    row = lax.broadcasted_iota(jnp.int32, (ROWS_EXTRA, 128), 0)
+    parts = jnp.where(
+        row == 1, high, jnp.where(row == 2, middle, jnp.where(row == 3, low, 0.0))
+    )
+
+    def step(s, _):
+        both = keep[s] + recv[s].astype(f32)
+        msg[s, 0:ROWS_OUT] = both[0:ROWS_OUT].astype(bf16)
+        msg[s, ROWS_OUT:] = (both[ROWS_OUT:] + parts).astype(bf16)
         return 0
 
     lax.fori_loop(0, 16, step, 0)
@@ -162,7 +178,7 @@
     rotated[...] = dot_slabs(grad, slabs, lax.axis_index("core"))
 
 
-def scale_kernel(slabs, grad, partial, q_out, values_in, values_out, back, parts):
+def scale_kernel(slabs, grad, partial, q_out, values_in, values_out, back, inner_out):
     total = partial[...] + dot_slabs(grad, slabs, 1 - lax.axis_index("core"))
     q = q_out[...]
     spectral = dot(q, total.astype(bf16), 0, 0)
@@ -172,14 +188,7 @@
     inner = jnp.sum(
         jnp.sum(back_rot.astype(f32) * total, axis=0, keepdims=True), axis=1, keepdims=True
     )
-    high = inner.astype(bf16).astype(f32)
-    rest = inner - high
-    middle = rest.astype(bf16).astype(f32)
-    low = rest - middle
-    row = lax.broadcasted_iota(jnp.int32, (16, 128), 0)
-    parts[...] = jnp.where(
-        row == 1, high, jnp.where(row == 2, middle, jnp.where(row == 3, low, 0.0))
-    ).astype(bf16)
+    inner_out[...] = jnp.broadcast_to(inner, (8, 128))
 
 
 def finish_kernel(q_own, q_other, back, precond):
@@ -211,30 +220,31 @@
     )(*args)
 
 
-def unpack_kernel(msg, column, keep_in, send_in):
+def total(msg, at, rows):
+    out = msg[0, at : at + rows].astype(f32)
+    for s in range(1, 16):
+        out = out + msg[s, at : at + rows].astype(f32)
+    return out
+
+
+def unpack_in_kernel(msg, keep, send):
     first = lax.axis_index("zh") == 0
-
-    def total(at, rows):
-        out = msg[0, at : at + rows].astype(f32)
-        for s in range(1, 16):
-            out = out + msg[s, at : at + rows].astype(f32)
-        return out
-
     for c in range(8):
-        pair = total(c * 32, 32)
-        lo, hi = pair[:16], pair[16:]
-        keep_in[:, c * 128 : c * 128 + 128] = jnp.where(first, lo, hi)
-        send_in[:, c * 128 : c * 128 + 128] = jnp.where(first, hi, lo)
-    folded = total(ROWS_IN, ROWS_OUT)
-    extra = total(ROWS_IN + ROWS_OUT, ROWS_EXTRA)
+        pair = total(msg, c * 32, 32)
+        low, high = pair[:16], pair[16:]
+        keep[:, c * 128 : c * 128 + 128] = jnp.where(first, low, high)
+        send[:, c * 128 : c * 128 + 128] = jnp.where(first, high, low)
+
+
+def unpack_out_kernel(msg, column):
+    folded = total(msg, 0, ROWS_OUT)
+    extra = total(msg, ROWS_OUT, ROWS_EXTRA)
     turned = folded.T
     row = lax.broadcasted_iota(jnp.int32, (128, 128), 0)
     col = lax.broadcasted_iota(jnp.int32, (128, 128), 1)
     one = jnp.where(row <= col, folded, turned)
     two = jnp.where(row > col, folded, jnp.where(row == col, extra[0:1], turned))
-    row = lax.broadcasted_iota(jnp.int32, extra.shape, 0)
-    inner = jnp.sum(jnp.where((row >= 1) & (row < 7), extra, 0.0), axis=0, keepdims=True)
-    inner = jnp.broadcast_to(inner, (8, 128))
+    inner = jnp.broadcast_to(extra[1:2] + extra[2:3] + extra[3:4], (8, 128))
     for z in range(4):
         column[z, 0:32] = one[z * 32 : z * 32 + 32]
         column[4 + z, 0:32] = two[z * 32 : z * 32 + 32]
@@ -263,25 +273,23 @@
     core = lax.axis_index("core").astype(jnp.int32)[None]
     mine = basis_in[0]
     slabs = jnp.concatenate([mine, swap(mine, "zh")], axis=0)
-    send_out, keep_out = cov_out_partial(output_grads, owner_blocks, token_counts, core)
-    slabs, send_out, counts = lax.optimization_barrier((slabs, send_out, token_counts))
+    send_in, keep_in = cov_in_partial(activations, token_counts)
+    slabs, send_in, counts = lax.optimization_barrier((slabs, send_in, token_counts))
+    recv_in = swap(send_in, "core")
     q_own = lax.all_to_all(
         jnp.broadcast_to(slabs[None], (16,) + slabs.shape), PLANE, 0, 0, tiled=True
     )
+    send_out, keep_out = cov_out_partial(output_grads, owner_blocks, counts, core)
     recv_out = swap(send_out, "core")
-    send_in, keep_in = cov_in_partial(activations, counts)
-    recv_in = swap(send_in, "core")
-    q_own, keep_in, recv_out = lax.optimization_barrier((q_own, keep_in, recv_out))
-    (msg,) = on_chip(
-        pack_kernel, [shape((16, ROWS, 128), bf16)], 1 << 20, keep_in, recv_in, keep_out, recv_out
-    )
-
+    (msg_in,) = on_chip(pack_in_kernel, [shape((16, ROWS_IN, 128), bf16)], 1024, keep_in, recv_in)
+    q_own, msg_in, keep_out = lax.optimization_barrier((q_own, msg_in, keep_out))
+    got_in = lax.all_to_all(msg_in, PLANE, 0, 0, tiled=True)
     q_other = swap(q_own, "core")
-    (partial,) = on_chip(rotate_kernel, [shape((128, 1024), f32)], 128 << 20, q_own, gradient)
-    back, parts = on_chip(
+    (partial,) = on_chip(rotate_kernel, [shape((128, 1024), f32)], 1024, q_own, gradient)
+    back, inner = on_chip(
         scale_kernel,
-        [shape((128, 1024), bf16), shape((16, 128), bf16)],
-        256 << 20,
+        [shape((128, 1024), bf16), shape((8, 128), f32)],
+        1024,
         q_other,
         gradient,
         partial,
@@ -289,22 +297,23 @@
         values_in[None, :],
         values_out[:, None],
     )
-    other_parts, msg = lax.optimization_barrier((swap(parts, "core"), msg))
-    parts = jnp.concatenate([parts[1:4], other_parts[1:4]], axis=0)
-    (precond,) = on_chip(finish_kernel, [shape((1024, 128), f32)], 256 << 20, q_own, q_other, back)
-    at = ROWS_IN + ROWS_OUT + 1
-    msg = lax.dynamic_update_slice(
-        msg, jnp.broadcast_to(parts[None], (16, 6, 128)), (0, at, 0)
-    )
-    msg = lax.all_to_all(msg, PLANE, 0, 0, tiled=True)
-    column, keep_slab, send_slab = on_chip(
-        unpack_kernel,
-        [shape((8, 40, 128), f32), shape((16, 1024), f32), shape((16, 1024), f32)],
-        2 << 20,
-        msg,
-    )
+    (msg_out,) = on_chip(
+        pack_out_kernel,
+        [shape((16, ROWS_OUT + ROWS_EXTRA, 128), bf16)],
+        1024,
+        keep_out,
+        recv_out,
+        inner,
+        swap(inner, "core"),
+    )
+    got_in, msg_out = lax.optimization_barrier((got_in, msg_out))
+    got_out = lax.all_to_all(msg_out, PLANE, 0, 0, tiled=True)
+    keep_slab, send_slab = on_chip(unpack_in_kernel, [shape((16, 1024), f32)] * 2, 1024, got_in)
     recv_slab = swap(send_slab, "zh")
+    (column,) = on_chip(unpack_out_kernel, [shape((8, 40, 128), f32)], 1024, got_out)
+    column, recv_slab = lax.optimization_barrier((column, recv_slab))
     column = lax.all_to_all(column, COLUMN, 0, 0, tiled=True)
+    (precond,) = on_chip(finish_kernel, [shape((1024, 128), f32)], 1024, q_own, q_other, back)
     cov_in = ((keep_slab + recv_slab) / token_total)[None]
     cov_out, update = on_chip(
         clip_kernel,

time: 98.5 us -> 97.1 us (0.986)
  starting transfers between devices: 31.9 us -> 29.4 us
    ppermute x6, starting transfers between devices: 18.1 us -> 11.3 us  [swap(): return lax.ppermute(array, axis, [(0, 1), (1, 0)])]
    all_to_all x1, waiting for transfers between devices: 0.01 us -> 6.76 us  [local(): column = lax.all_to_all(column, COLUMN, 0, 0, tiled=True)]
    ppermute x6, waiting for transfers between devices: 6.88 us -> 0.83 us  [swap(): return lax.ppermute(array, axis, [(0, 1), (1, 0)])]
    all_to_all x1 -> x2, starting transfers between devices: 3.71 us -> 7.91 us  [the longest x1 4.25 us: local(): got_out = lax.all_to_all(msg_out, PLANE, 0, 0, tiled=True)]
    pallas_call x1, Pallas kernels: 8.07 us -> 5.73 us  [cov_out_partial(): pl.pallas_call(cov_out_kernel, grid_spec=pltpu.PrefetchScalarGridSpec(num...]
    unnamed x36, local copies, waits for them, and re-layouts: 7.1 us -> 9.23 us
    pallas_call x6 -> x8, Pallas kernels: 5.78 us -> 7.77 us  [on_chip(): pl.pallas_call(kernel, in_specs=[whole if a.ndim > 1 else pl.BlockSpec(me...]
    dynamic_update_slice x1 -> x0, local copies, waits for them, and re-layouts: 1.45 us -> none  [local(): lax.dynamic_update_slice(msg, jnp.broadcast_to(parts[None], (16, 6, 128))...]
  transfers between devices with their start and end apart: 9 -> 10, of which waited for: 4 -> 5; matrix products, arithmetic and copies ran while one was open for 2% -> 3% of each run, Pallas kernels for 16% -> 17%
where the time goes in v4:
time: 97.1 us; the launch traced here: 96.1 us
  waiting for transfers between devices  34.6 us (36%)
  starting transfers between devices  29.4 us (30%)
  Pallas kernels  18.2 us (19%)
  local copies, waits for them, and re-layouts  10.5 us (11%)
  between operations  2.13 us (2%)
  other arithmetic  1.36 us (1%)
    all_to_all x1, waiting for transfers between devices, local(): got_in = lax.all_to_all(msg_in, PLANE, 0, 0, tiled=True)  12.3 us
    ppermute x6, starting transfers between devices, swap(): return lax.ppermute(array, axis, [(0, 1), (1, 0)])  11.3 us
    unnamed x36, local copies, waits for them, and re-layouts  9.23 us
    all_to_all x1, waiting for transfers between devices, local(): got_out = lax.all_to_all(msg_out, PLANE, 0, 0, tiled=True)  8.76 us
    pallas_call x8, Pallas kernels, on_chip(): pl.pallas_call(kernel, in_specs=[whole if a.ndim > 1 else pl.BlockSpec(me...  7.77 us
    all_to_all x1, waiting for transfers between devices, local(): column = lax.all_to_all(column, COLUMN, 0, 0, tiled=True)  6.76 us
    all_to_all x1, starting transfers between devices, local(): lax.all_to_all(jnp.broadcast_to(slabs[None], (16,) + slabs.shape), PLANE,...  6.74 us
    all_to_all x1, waiting for transfers between devices, local(): lax.all_to_all(jnp.broadcast_to(slabs[None], (16,) + slabs.shape), PLANE,...  5.88 us
  transfers between devices with their start and end apart: 10, of which 5 were waited for; matrix products, arithmetic and copies ran while one was open for 3% of the time, Pallas kernels for 17%

profile of v4, /device:TPU:1, one launch (start us, length us, event | category | flops | bytes accessed | tf_op | source)
XLA Modules:
  0.0 96.1 jit_solution(7416308298784951482)
XLA Ops:
  0.6 7.8 %collective-permute-start = (bf16[16,1024]{1,0:T(8,128)(2,1)}, bf16[16,1024]{1,0:T(8,128)(2,1)S(1)}, u32[]{:S(2)}, u32[]{:S(2)}) collective-permute-start(bf16[16,1024]{1,0:T(8,128)(2,1)} %bitcast.10), channel_id=1, source_target_pairs={{0,32},{32,0},{1,33},{33,1},{2,34},{34,2},{3,35},{35,3},{4,36},{36... | collective-permute-start | bytes 98312 | tf_op jit(solution)/shard_map/ppermute | solution.py:256
  9.1 1.6 %copy-done.14 = bf16[1024,1024]{1,0:T(8,128)(2,1)S(1)} copy-done((bf16[1024,1024]{1,0:T(8,128)(2,1)S(1)}, bf16[1024,1024]{1,0:T(8,128)(2,1)}, u32[]{:S(2)}) %copy-start.14) | copy-done | bytes 2097176
  10.7 4.7 %cov_in_partial.1 = (bf16[16,256,128]{2,1,0:T(8,128)(2,1)}, f32[16,256,128]{2,1,0:T(8,128)S(1)}) custom-call(s32[64]{0:T(128)S(1)} %copy-done.12, bf16[1024,1024]{1,0:T(8,128)(2,1)S(1)} %copy-done.14, bf16[1024,1024]{1,0:T(8,128)(2,1)S(1)} %copy-done.14), custom_call_target="tpu_custom_call" | custom-call | flops 2147483648 | bytes 8388608 | tf_op jit(solution)/shard_map/cov_in_partial/pallas_call | solution.py:112
  15.4 1.3 %copy-done.2 = f32[16,256,128]{2,1,0:T(8,128)} copy-done((f32[16,256,128]{2,1,0:T(8,128)}, f32[16,256,128]{2,1,0:T(8,128)S(1)}, u32[]{:S(2)}) %copy-start.2) | copy-done | bytes 2097176
  16.8 1.1 %collective-permute-start.1 = (bf16[16,256,128]{2,1,0:T(8,128)(2,1)}, bf16[16,256,128]{2,1,0:T(8,128)(2,1)S(1)}, u32[]{:S(2)}, u32[]{:S(2)}) collective-permute-start(bf16[16,256,128]{2,1,0:T(8,128)(2,1)} %get-tuple-element.26), channel_id=1, source_target_pairs={{0,4},{4,0},{1,5},{5,1},{2,6},{6,2},{3,7},{7,3},{8,12},{12,8},{9,1... | collective-permute-start | bytes 3145736 | tf_op jit(solution)/shard_map/ppermute | solution.py:256
  17.8 1.1 %broadcast_in_dim.18 = bf16[16,32,1024]{2,1,0:T(8,128)(2,1)} broadcast(bf16[32,1024]{1,0:T(8,128)(2,1)S(1)} %pad_maximum_fusion), dimensions={1,2} | broadcast | bytes 1114112 | tf_op jit(solution)/shard_map/broadcast_in_dim | solution.py:280
  18.9 6.7 %all-to-all-start = ((bf16[16,32,1024]{2,1,0:T(8,128)(2,1)}), bf16[16,32,1024]{2,1,0:T(8,128)(2,1)S(1)}, u32[]{:S(2)}, u32[]{:S(2)}) async-start(bf16[16,32,1024]{2,1,0:T(8,128)(2,1)} %broadcast_in_dim.18), calls=%async_computation | async-start | bytes 2097152 | tf_op jit(solution)/shard_map/all_to_all | solution.py:279
  25.7 2.2 %copy-done = bf16[256,8192]{1,0:T(8,128)(2,1)S(1)} copy-done((bf16[256,8192]{1,0:T(8,128)(2,1)S(1)}, bf16[256,8192]{1,0:T(8,128)(2,1)}, u32[]{:S(2)}) %copy-start) | copy-done | bytes 4194328
  27.9 5.7 %cov_out_partial.1 = (bf16[16,144,128]{2,1,0:T(8,128)(2,1)S(1)}, f32[16,144,128]{2,1,0:T(8,128)S(1)}) custom-call(s32[64]{0:T(128)S(1)} %copy-done.11, s32[64]{0:T(128)S(1)} %copy-done.13, s32[1]{0:T(128)} %bitcast.1.core, bf16[256,8192]{1,0:T(8,128)(2,1)S(1)} %copy-done, bf16[256,8192]{1,0:T(8,128)(2,1)S(1)} %copy-done, bf16[256,8192]{1,0:T(8,128)(2,1)S(1)} %copy-done, ...), custom_call_target="tpu_custom_call" | custom-call | flops 536870912 | bytes 8388608 | tf_op jit(solution)/shard_map/cov_out_partial/pallas_call | solution.py:70
  33.7 1.0 %copy-done.4 = f32[16,144,128]{2,1,0:T(8,128)} copy-done((f32[16,144,128]{2,1,0:T(8,128)}, f32[16,144,128]{2,1,0:T(8,128)S(1)}, u32[]{:S(2)}) %copy-start.4) | copy-done | bytes 1179672
  34.7 0.8 copy-done.15
  35.5 1.2 %pack_in.1 = bf16[16,256,128]{2,1,0:T(8,128)(2,1)} custom-call(f32[16,256,128]{2,1,0:T(8,128)S(1)} %copy-done.3, bf16[16,256,128]{2,1,0:T(8,128)(2,1)S(1)} %collective-permute-done.1.recv), custom_call_target="tpu_custom_call" | custom-call | flops 1024 | bytes 3145728 | tf_op jit(solution)/shard_map/pack_in/pallas_call | solution.py:212
  36.8 5.9 %all-to-all-done.slabs.q_own = bf16[16,32,1024]{2,1,0:T(8,128)(2,1)S(1)} async-done(((bf16[16,32,1024]{2,1,0:T(8,128)(2,1)}), bf16[16,32,1024]{2,1,0:T(8,128)(2,1)S(1)}, u32[]{:S(2)}, u32[]{:S(2)}) %all-to-all-start) | async-done | bytes 1048608 | tf_op jit(solution)/shard_map/all_to_all | solution.py:279
  42.7 1.8 %collective-permute-start.3 = (bf16[16,32,1024]{2,1,0:T(8,128)(2,1)S(1)}, bf16[16,32,1024]{2,1,0:T(8,128)(2,1)S(1)}, u32[]{:S(2)}, u32[]{:S(2)}) collective-permute-start(bf16[16,32,1024]{2,1,0:T(8,128)(2,1)S(1)} %all-to-all-done.slabs.q_own), channel_id=1, source_target_pairs={{0,4},{4,0},{1,5},{5,1},{2,6},{6,2},{3,7},{7,3},{8,12},{12,8},{9,1... | collective-permute-start | bytes 3145736 | tf_op jit(solution)/shard_map/ppermute | solution.py:256
  44.5 3.7 %all-to-all-start.1 = ((bf16[16,256,128]{2,1,0:T(8,128)(2,1)}), bf16[16,256,128]{2,1,0:T(8,128)(2,1)S(1)}, u32[]{:S(2)}, u32[]{:S(2)}) async-start(bf16[16,256,128]{2,1,0:T(8,128)(2,1)} %pack_in.1), calls=%async_computation.1 | async-start | bytes 2097152 | tf_op jit(solution)/shard_map/all_to_all | solution.py:286
  51.6 1.3 %pack_out.1 = bf16[16,144,128]{2,1,0:T(8,128)(2,1)S(1)} custom-call(f32[16,144,128]{2,1,0:T(8,128)S(1)} %copy-done.5, bf16[16,144,128]{2,1,0:T(8,128)(2,1)} %collective-permute-done.2.recv, f32[8,128]{1,0:T(8,128)S(1)} %get-tuple-element.33.inner, f32[8,128]{1,0:T(8,128)S(1)} %collective-permute-done.4.other_inner), custom_call_target="tpu_custom_call" | custom-call | flops 1024 | bytes 1777664 | tf_op jit(solution)/shard_map/pack_out/pallas_call | solution.py:212
  52.8 0.8 copy-done.1
  53.7 12.3 %all-to-all-done.1.msg = bf16[16,256,128]{2,1,0:T(8,128)(2,1)S(1)} async-done(((bf16[16,256,128]{2,1,0:T(8,128)(2,1)}), bf16[16,256,128]{2,1,0:T(8,128)(2,1)S(1)}, u32[]{:S(2)}, u32[]{:S(2)}) %all-to-all-start.1) | async-done | bytes 1048608 | tf_op jit(solution)/shard_map/all_to_all | solution.py:286
  66.0 4.3 %all-to-all-start.2 = ((bf16[16,144,128]{2,1,0:T(8,128)(2,1)}), bf16[16,144,128]{2,1,0:T(8,128)(2,1)}, u32[]{:S(2)}, u32[]{:S(2)}) async-start(bf16[16,144,128]{2,1,0:T(8,128)(2,1)} %copy-done.1), calls=%async_computation.2 | async-start | bytes 1179648 | tf_op jit(solution)/shard_map/all_to_all | solution.py:310
  72.4 8.8 %all-to-all-done.2.msg = bf16[16,144,128]{2,1,0:T(8,128)(2,1)} async-done(((bf16[16,144,128]{2,1,0:T(8,128)(2,1)}), bf16[16,144,128]{2,1,0:T(8,128)(2,1)}, u32[]{:S(2)}, u32[]{:S(2)}) %all-to-all-start.2) | async-done | bytes 589856 | tf_op jit(solution)/shard_map/all_to_all | solution.py:310
  81.2 1.9 %unpack_out.1 = f32[8,40,128]{2,1,0:T(8,128)} custom-call(bf16[16,144,128]{2,1,0:T(8,128)(2,1)} %all-to-all-done.2.msg), custom_call_target="tpu_custom_call" | custom-call | flops 1024 | bytes 589824 | tf_op jit(solution)/shard_map/unpack_out/pallas_call | solution.py:212
  83.1 3.4 %all-to-all-start.3 = ((f32[8,40,128]{2,1,0:T(8,128)}), f32[8,40,128]{2,1,0:T(8,128)S(1)}, u32[]{:S(2)}, u32[]{:S(2)}) async-start(f32[8,40,128]{2,1,0:T(8,128)} %unpack_out.1), calls=%async_computation.3 | async-start | bytes 327680 | tf_op jit(solution)/shard_map/all_to_all | solution.py:315
  87.9 6.8 %all-to-all-done.3.column = f32[8,40,128]{2,1,0:T(8,128)S(1)} async-done(((f32[8,40,128]{2,1,0:T(8,128)}), f32[8,40,128]{2,1,0:T(8,128)S(1)}, u32[]{:S(2)}, u32[]{:S(2)}) %all-to-all-start.3) | async-done | bytes 163872 | tf_op jit(solution)/shard_map/all_to_all | solution.py:315
  94.7 1.4 %clip.1 = (f32[1,32,128]{2,1,0:T(8,128)}, f32[1024,128]{1,0:T(8,128)}) custom-call(f32[2]{0:T(128)S(1)} %pad_maximum_fusion.1.scalars, f32[8,40,128]{2,1,0:T(8,128)S(1)} %all-to-all-done.3.column, f32[1024,128]{1,0:T(8,128)S(1)} %finish.1.precond), custom_call_target="tpu_custom_call" | custom-call | flops 1048576 | bytes 688136 | tf_op jit(solution)/shard_map/clip/pallas_call | solution.py:212
  (48 shorter events, 6.4 us)
Async XLA Ops:
  0.6 16.1 %collective-permute-start = (bf16[16,1024]{1,0:T(8,128)(2,1)}, bf16[16,1024]{1,0:T(8,128)(2,1)S(1)}, u32[]{:S(2)}, u32[]{:S(2)}) collective-permute-start(bf16[16,1024]{1,0:T(8,128)(2,1)} %bitcast.10), channel_id=1, source_target_pairs={{0,32},{32,0},{1,33},{33,1},{2,34},{34,2},{3,35},{35,3},{4,36},{36... | collective-permute-start | bytes 98312 | tf_op jit(solution)/shard_map/ppermute | solution.py:256
  9.1 1.6 %copy-start.14 = (bf16[1024,1024]{1,0:T(8,128)(2,1)S(1)}, bf16[1024,1024]{1,0:T(8,128)(2,1)}, u32[]{:S(2)}) copy-start(bf16[1024,1024]{1,0:T(8,128)(2,1)} %rhs.1) | copy-start | bytes 6291460
  10.7 6.0 %copy-start.16 = (bf16[1,16,1024]{2,1,0:T(8,128)(2,1)S(1)}, bf16[1,16,1024]{2,1,0:T(8,128)(2,1)}, u32[]{:S(2)}) copy-start(bf16[1,16,1024]{2,1,0:T(8,128)(2,1)} %param.14) | copy-start | bytes 98308
  15.4 1.4 %copy-start.2 = (f32[16,256,128]{2,1,0:T(8,128)}, f32[16,256,128]{2,1,0:T(8,128)S(1)}, u32[]{:S(2)}) copy-start(f32[16,256,128]{2,1,0:T(8,128)S(1)} %get-tuple-element.25.keep) | copy-start | bytes 6291460
  16.7 9.0 %copy-start.11 = (s32[64]{0:T(128)S(1)}, s32[64]{0:T(128)}, u32[]{:S(2)}) copy-start(s32[64]{0:T(128)} %owners.1) | copy-start | bytes 772
  16.7 9.0 %copy-start.13 = (s32[64]{0:T(128)S(1)}, s32[64]{0:T(128)}, u32[]{:S(2)}) copy-start(s32[64]{0:T(128)} %counts.2) | copy-start | bytes 772
  16.8 18.8 %collective-permute-start.1 = (bf16[16,256,128]{2,1,0:T(8,128)(2,1)}, bf16[16,256,128]{2,1,0:T(8,128)(2,1)S(1)}, u32[]{:S(2)}, u32[]{:S(2)}) collective-permute-start(bf16[16,256,128]{2,1,0:T(8,128)(2,1)} %get-tuple-element.26), channel_id=1, source_target_pairs={{0,4},{4,0},{1,5},{5,1},{2,6},{6,2},{3,7},{7,3},{8,12},{12,8},{9,1... | collective-permute-start | bytes 3145736 | tf_op jit(solution)/shard_map/ppermute | solution.py:256
  18.9 23.7 %all-to-all-start = ((bf16[16,32,1024]{2,1,0:T(8,128)(2,1)}), bf16[16,32,1024]{2,1,0:T(8,128)(2,1)S(1)}, u32[]{:S(2)}, u32[]{:S(2)}) async-start(bf16[16,32,1024]{2,1,0:T(8,128)(2,1)} %broadcast_in_dim.18), calls=%async_computation | async-start | bytes 2097152 | tf_op jit(solution)/shard_map/all_to_all | solution.py:279
  25.7 2.2 %copy-start = (bf16[256,8192]{1,0:T(8,128)(2,1)S(1)}, bf16[256,8192]{1,0:T(8,128)(2,1)}, u32[]{:S(2)}) copy-start(bf16[256,8192]{1,0:T(8,128)(2,1)} %refs_7_.1) | copy-start | bytes 12582916
  27.9 7.6 %copy-start.3 = (f32[16,256,128]{2,1,0:T(8,128)S(1)}, f32[16,256,128]{2,1,0:T(8,128)}, u32[]{:S(2)}) copy-start(f32[16,256,128]{2,1,0:T(8,128)} %copy-done.2) | copy-start | bytes 6291460
  33.7 1.1 %copy-start.4 = (f32[16,144,128]{2,1,0:T(8,128)}, f32[16,144,128]{2,1,0:T(8,128)S(1)}, u32[]{:S(2)}) copy-start(f32[16,144,128]{2,1,0:T(8,128)S(1)} %get-tuple-element.30.keep) | copy-start | bytes 3538948
  36.8 11.4 %copy-start.17 = (f32[128]{0:T(128)S(1)}, f32[128]{0:T(128)}, u32[]{:S(2)}) copy-start(f32[128]{0:T(128)} %param.17) | copy-start | bytes 1540
  36.8 11.6 %copy-start.6 = (bf16[1024,128]{1,0:T(8,128)(2,1)S(1)}, bf16[1024,128]{1,0:T(8,128)(2,1)}, u32[]{:S(2)}) copy-start(bf16[1024,128]{1,0:T(8,128)(2,1)} %grad.3) | copy-start | bytes 786436
  36.8 11.9 %copy-start.9 = (bf16[1,128,128]{2,1,0:T(8,128)(2,1)S(1)}, bf16[1,128,128]{2,1,0:T(8,128)(2,1)}, u32[]{:S(2)}) copy-start(bf16[1,128,128]{2,1,0:T(8,128)(2,1)} %param.15) | copy-start | bytes 98308
  36.8 11.9 %copy-start.10 = (f32[1024]{0:T(1024)S(1)}, f32[1024]{0:T(1024)}, u32[]{:S(2)}) copy-start(f32[1024]{0:T(1024)} %param.16) | copy-start | bytes 12292
  42.7 6.0 %collective-permute-start.3 = (bf16[16,32,1024]{2,1,0:T(8,128)(2,1)S(1)}, bf16[16,32,1024]{2,1,0:T(8,128)(2,1)S(1)}, u32[]{:S(2)}, u32[]{:S(2)}) collective-permute-start(bf16[16,32,1024]{2,1,0:T(8,128)(2,1)S(1)} %all-to-all-done.slabs.q_own), channel_id=1, source_target_pairs={{0,4},{4,0},{1,5},{5,1},{2,6},{6,2},{3,7},{7,3},{8,12},{12,8},{9,1... | collective-permute-start | bytes 3145736 | tf_op jit(solution)/shard_map/ppermute | solution.py:256
  44.5 21.5 %all-to-all-start.1 = ((bf16[16,256,128]{2,1,0:T(8,128)(2,1)}), bf16[16,256,128]{2,1,0:T(8,128)(2,1)S(1)}, u32[]{:S(2)}, u32[]{:S(2)}) async-start(bf16[16,256,128]{2,1,0:T(8,128)(2,1)} %pack_in.1), calls=%async_computation.1 | async-start | bytes 2097152 | tf_op jit(solution)/shard_map/all_to_all | solution.py:286
  48.1 2.6 %collective-permute-start.2 = (bf16[16,144,128]{2,1,0:T(8,128)(2,1)}, bf16[16,144,128]{2,1,0:T(8,128)(2,1)}, u32[]{:S(2)}, u32[]{:S(2)}) collective-permute-start(bf16[16,144,128]{2,1,0:T(8,128)(2,1)} %copy-done.15), channel_id=1, source_target_pairs={{0,4},{4,0},{1,5},{5,1},{2,6},{6,2},{3,7},{7,3},{8,12},{12,8},{9,1... | collective-permute-start | bytes 1769480 | tf_op jit(solution)/shard_map/ppermute | solution.py:256
  48.3 3.2 %copy-start.5 = (f32[16,144,128]{2,1,0:T(8,128)S(1)}, f32[16,144,128]{2,1,0:T(8,128)}, u32[]{:S(2)}) copy-start(f32[16,144,128]{2,1,0:T(8,128)} %copy-done.4) | copy-start | bytes 3538948
  50.2 1.3 %collective-permute-start.4 = (f32[8,128]{1,0:T(8,128)S(1)}, f32[8,128]{1,0:T(8,128)S(1)}, u32[]{:S(2)}, u32[]{:S(2)}) collective-permute-start(f32[8,128]{1,0:T(8,128)S(1)} %get-tuple-element.33.inner), channel_id=1, source_target_pairs={{0,4},{4,0},{1,5},{5,1},{2,6},{6,2},{3,7},{7,3},{8,12},{12,8},{9,1... | collective-permute-start | bytes 12296 | tf_op jit(solution)/shard_map/ppermute | solution.py:256
  53.7 32.9 %copy-start.8 = (bf16[128,1024]{1,0:T(8,128)(2,1)S(1)}, bf16[128,1024]{1,0:T(8,128)(2,1)}, u32[]{:S(2)}) copy-start(bf16[128,1024]{1,0:T(8,128)(2,1)} %copy-done.7) | copy-start | bytes 786436
  66.0 15.2 %all-to-all-start.2 = ((bf16[16,144,128]{2,1,0:T(8,128)(2,1)}), bf16[16,144,128]{2,1,0:T(8,128)(2,1)}, u32[]{:S(2)}, u32[]{:S(2)}) async-start(bf16[16,144,128]{2,1,0:T(8,128)(2,1)} %copy-done.1), calls=%async_computation.2 | async-start | bytes 1179648 | tf_op jit(solution)/shard_map/all_to_all | solution.py:310
  70.4 12.7 %collective-permute-start.5 = (f32[16,1024]{1,0:T(8,128)S(1)}, f32[16,1024]{1,0:T(8,128)S(1)}, u32[]{:S(2)}, u32[]{:S(2)}) collective-permute-start(f32[16,1024]{1,0:T(8,128)S(1)} %get-tuple-element.37), channel_id=1, source_target_pairs={{0,32},{32,0},{1,33},{33,1},{2,34},{34,2},{3,35},{35,3},{4,36},{36... | collective-permute-start | bytes 196616 | tf_op jit(solution)/shard_map/ppermute | solution.py:256
  83.1 11.6 %all-to-all-start.3 = ((f32[8,40,128]{2,1,0:T(8,128)}), f32[8,40,128]{2,1,0:T(8,128)S(1)}, u32[]{:S(2)}, u32[]{:S(2)}) async-start(f32[8,40,128]{2,1,0:T(8,128)} %unpack_out.1), calls=%async_computation.3 | async-start | bytes 327680 | tf_op jit(solution)/shard_map/all_to_all | solution.py:315
  (4 other events, 3.0 us)

commit v5 on v4

--- a/solution.py
+++ b/solution.py
@@ -20,6 +20,7 @@
 ROWS_IN = 256
 ROWS_OUT = 128
 ROWS_EXTRA = 16
+ROWS = ROWS_IN + ROWS_OUT + ROWS_EXTRA
 
 
 def dot(a, b, ca, cb):
@@ -132,40 +133,21 @@
     )(counts, activations, activations)
 
 
-def pack_in_kernel(keep, recv, msg):
+def pack_kernel(keep_in, recv_in, keep_out, recv_out, msg):
     def step(s, _):
-        msg[s] = (keep[s] + recv[s].astype(f32)).astype(bf16)
+        msg[s, 0:ROWS_IN] = (keep_in[s] + recv_in[s].astype(f32)).astype(bf16)
+        msg[s, ROWS_IN:] = (keep_out[s] + recv_out[s].astype(f32)).astype(bf16)
         return 0
 
     lax.fori_loop(0, 16, step, 0)
 
 
-def pack_out_kernel(keep, recv, inner, other_inner, msg):
-    total = inner[0:1] + other_inner[0:1]
-    high = total.astype(bf16).astype(f32)
-    rest = total - high
-    middle = rest.astype(bf16).astype(f32)
-    low = rest - middle
-    row = lax.broadcasted_iota(jnp.int32, (ROWS_EXTRA, 128), 0)
-    parts = jnp.where(
-        row == 1, high, jnp.where(row == 2, middle, jnp.where(row == 3, low, 0.0))
-    )
-
-    def step(s, _):
-        both = keep[s] + recv[s].astype(f32)
-        msg[s, 0:ROWS_OUT] = both[0:ROWS_OUT].astype(bf16)
-        msg[s, ROWS_OUT:] = (both[ROWS_OUT:] + parts).astype(bf16)
-        return 0
-
-    lax.fori_loop(0, 16, step, 0)
-
-
 def slab_rows(core):
-    zh = lax.axis_index("zh")
-    for x in range(4):
-        for y in range(4):
+    x, zh = lax.axis_index("x"), lax.axis_index("zh")
+    for y in range(4):
+        for step in range(4):
             for z in (zh, 1 - zh):
-                slab = ((x * 2 + z) * 4 + y) * 2 + core
+                slab = ((lax.rem(x + 4 - step, 4) * 2 + z) * 4 + y) * 2 + core
                 yield pl.ds(pl.multiple_of(slab * 16, 16), 16)
 
 
@@ -227,29 +209,30 @@
     return out
 
 
-def unpack_in_kernel(msg, keep, send):
+def unpack_kernel(msg, keep, send, column):
     first = lax.axis_index("zh") == 0
     for c in range(8):
         pair = total(msg, c * 32, 32)
         low, high = pair[:16], pair[16:]
         keep[:, c * 128 : c * 128 + 128] = jnp.where(first, low, high)
         send[:, c * 128 : c * 128 + 128] = jnp.where(first, high, low)
-
-
-def unpack_out_kernel(msg, column):
-    folded = total(msg, 0, ROWS_OUT)
-    extra = total(msg, ROWS_OUT, ROWS_EXTRA)
+    folded = total(msg, ROWS_IN, ROWS_OUT)
+    diag = total(msg, ROWS_IN + ROWS_OUT, ROWS_EXTRA)[0:1]
     turned = folded.T
     row = lax.broadcasted_iota(jnp.int32, (128, 128), 0)
     col = lax.broadcasted_iota(jnp.int32, (128, 128), 1)
     one = jnp.where(row <= col, folded, turned)
-    two = jnp.where(row > col, folded, jnp.where(row == col, extra[0:1], turned))
-    inner = jnp.broadcast_to(extra[1:2] + extra[2:3] + extra[3:4], (8, 128))
+    two = jnp.where(row > col, folded, jnp.where(row == col, diag, turned))
     for z in range(4):
-        column[z, 0:32] = one[z * 32 : z * 32 + 32]
-        column[4 + z, 0:32] = two[z * 32 : z * 32 + 32]
-        column[z, 32:40] = inner
-        column[4 + z, 32:40] = inner
+        column[z] = one[z * 32 : z * 32 + 32]
+        column[4 + z] = two[z * 32 : z * 32 + 32]
+
+
+def join_kernel(column, inner, joined):
+    total = jnp.sum(inner[...], axis=0)
+    for z in range(8):
+        joined[z, 0:32] = column[z]
+        joined[z, 32:40] = total
 
 
 def swap(array, axis):
@@ -275,15 +258,20 @@
     slabs = jnp.concatenate([mine, swap(mine, "zh")], axis=0)
     send_in, keep_in = cov_in_partial(activations, token_counts)
     slabs, send_in, counts = lax.optimization_barrier((slabs, send_in, token_counts))
+    slabs = [slabs] + [
+        lax.ppermute(slabs, "x", [(j, (j + step) % 4) for j in range(4)]) for step in (1, 2, 3)
+    ]
     recv_in = swap(send_in, "core")
-    q_own = lax.all_to_all(
-        jnp.broadcast_to(slabs[None], (16,) + slabs.shape), PLANE, 0, 0, tiled=True
-    )
     send_out, keep_out = cov_out_partial(output_grads, owner_blocks, counts, core)
+    slabs, send_out, recv_in = lax.optimization_barrier(
+        (jnp.concatenate(slabs, axis=0), send_out, recv_in)
+    )
+    q_own = lax.all_gather(slabs, "y", axis=0, tiled=False)
     recv_out = swap(send_out, "core")
-    (msg_in,) = on_chip(pack_in_kernel, [shape((16, ROWS_IN, 128), bf16)], 1024, keep_in, recv_in)
-    q_own, msg_in, keep_out = lax.optimization_barrier((q_own, msg_in, keep_out))
-    got_in = lax.all_to_all(msg_in, PLANE, 0, 0, tiled=True)
+    (msg,) = on_chip(
+        pack_kernel, [shape((16, ROWS, 128), bf16)], 1024, keep_in, recv_in, keep_out, recv_out
+    )
+    msg = lax.all_to_all(msg, PLANE, 0, 0, tiled=True)
     q_other = swap(q_own, "core")
     (partial,) = on_chip(rotate_kernel, [shape((128, 1024), f32)], 1024, q_own, gradient)
     back, inner = on_chip(
@@ -297,20 +285,18 @@
         values_in[None, :],
         values_out[:, None],
     )
-    (msg_out,) = on_chip(
-        pack_out_kernel,
-        [shape((16, ROWS_OUT + ROWS_EXTRA, 128), bf16)],
+    msg, inner = lax.optimization_barrier((msg, inner))
+    inner = lax.all_to_all(
+        jnp.broadcast_to(inner[None], (32, 8, 128)), ("x", "y", "core"), 0, 0, tiled=True
+    )
+    keep_slab, send_slab, column = on_chip(
+        unpack_kernel,
+        [shape((16, 1024), f32), shape((16, 1024), f32), shape((8, 32, 128), f32)],
         1024,
-        keep_out,
-        recv_out,
-        inner,
-        swap(inner, "core"),
-    )
-    got_in, msg_out = lax.optimization_barrier((got_in, msg_out))
-    got_out = lax.all_to_all(msg_out, PLANE, 0, 0, tiled=True)
-    keep_slab, send_slab = on_chip(unpack_in_kernel, [shape((16, 1024), f32)] * 2, 1024, got_in)
+        msg,
+    )
     recv_slab = swap(send_slab, "zh")
-    (column,) = on_chip(unpack_out_kernel, [shape((8, 40, 128), f32)], 1024, got_out)
+    (column,) = on_chip(join_kernel, [shape((8, 40, 128), f32)], 1024, column, inner)
     column, recv_slab = lax.optimization_barrier((column, recv_slab))
     column = lax.all_to_all(column, COLUMN, 0, 0, tiled=True)
     (precond,) = on_chip(finish_kernel, [shape((1024, 128), f32)], 1024, q_own, q_other, back)

time: 97.1 us -> 123 us (1.27)
  between operations: 2.13 us -> 15.4 us
  starting transfers between devices: 29.4 us -> 37.8 us
  waiting for transfers between devices: 34.6 us -> 37.3 us
    all_gather x0 -> x1, waiting for transfers between devices: none -> 27.8 us  [local(): q_own = lax.all_gather(slabs, 'y', axis=0, tiled=False)]
    all_to_all x3 -> x2, waiting for transfers between devices: 27 us -> 1.38 us  [the longest x1 1.38 us: local(): lax.all_to_all(jnp.broadcast_to(inner[None], (32, 8, 128)), ('x', 'y', 'c...]
    ppermute x0 -> x3, starting transfers between devices: none -> 3.63 us  [local(): lax.ppermute(slabs, 'x', [(j, (j + step) % 4) for j in range(4)])]
    ppermute x6 -> x5, starting transfers between devices: 11.3 us -> 14.6 us  [swap(): return lax.ppermute(array, axis, [(0, 1), (1, 0)])]
    all_to_all x1, starting transfers between devices: 3.38 us -> 6.15 us  [local(): column = lax.all_to_all(column, COLUMN, 0, 0, tiled=True)]
    ppermute x6 -> x5, waiting for transfers between devices: 0.83 us -> 2.64 us  [swap(): return lax.ppermute(array, axis, [(0, 1), (1, 0)])]
    all_to_all x1, waiting for transfers between devices: 6.76 us -> 5.39 us  [local(): column = lax.all_to_all(column, COLUMN, 0, 0, tiled=True)]
    all_to_all x3 -> x2, starting transfers between devices: 14.7 us -> 13.4 us  [the longest x1 7.12 us: local(): lax.all_to_all(jnp.broadcast_to(inner[None], (32, 8, 128)), ('x', 'y', 'c...]
  transfers between devices with their start and end apart: 10 -> 12, of which waited for: 5 -> 5; matrix products, arithmetic and copies ran while one was open for 3% -> 2% of each run, Pallas kernels for 17% -> 13%
where the time goes in v5:
time: 123 us; the launch traced here: 121 us
  starting transfers between devices  37.8 us (31%)
  waiting for transfers between devices  37.3 us (30%)
  Pallas kernels  17.5 us (14%)
  between operations  15.4 us (13%)
  local copies, waits for them, and re-layouts  10.7 us (9%)
  other arithmetic  2.08 us (2%)
    all_gather x1, waiting for transfers between devices, local(): q_own = lax.all_gather(slabs, 'y', axis=0, tiled=False)  27.8 us
    ppermute x5, starting transfers between devices, swap(): return lax.ppermute(array, axis, [(0, 1), (1, 0)])  14.6 us
    unnamed x32, local copies, waits for them, and re-layouts  9.93 us
    all_to_all x1, starting transfers between devices, local(): lax.all_to_all(jnp.broadcast_to(inner[None], (32, 8, 128)), ('x', 'y', 'c...  7.12 us
    pallas_call x7, Pallas kernels, on_chip(): pl.pallas_call(kernel, in_specs=[whole if a.ndim > 1 else pl.BlockSpec(me...  7.03 us
    all_to_all x1, starting transfers between devices, local(): msg = lax.all_to_all(msg, PLANE, 0, 0, tiled=True)  6.23 us
    all_to_all x1, starting transfers between devices, local(): column = lax.all_to_all(column, COLUMN, 0, 0, tiled=True)  6.15 us
    pallas_call x1, Pallas kernels, cov_out_partial(): pl.pallas_call(cov_out_kernel, grid_spec=pltpu.PrefetchScalarGridSpec(num...  5.73 us
  transfers between devices with their start and end apart: 12, of which 5 were waited for; matrix products, arithmetic and copies ran while one was open for 2% of the time, Pallas kernels for 13%

profile of v5, /device:TPU:1, one launch (start us, length us, event | category | flops | bytes accessed | tf_op | source)
XLA Modules:
  0.0 120.8 jit_solution(5432537060958959870)
XLA Ops:
  7.2 7.8 %collective-permute-start = (bf16[16,1024]{1,0:T(8,128)(2,1)}, bf16[16,1024]{1,0:T(8,128)(2,1)S(1)}, u32[]{:S(2)}, u32[]{:S(2)}) collective-permute-start(bf16[16,1024]{1,0:T(8,128)(2,1)} %bitcast.14), channel_id=1, source_target_pairs={{0,32},{32,0},{1,33},{33,1},{2,34},{34,2},{3,35},{35,3},{4,36},{36... | collective-permute-start | bytes 98312 | tf_op jit(solution)/shard_map/ppermute | solution.py:239
  15.7 1.6 %copy-done.12 = bf16[1024,1024]{1,0:T(8,128)(2,1)S(1)} copy-done((bf16[1024,1024]{1,0:T(8,128)(2,1)S(1)}, bf16[1024,1024]{1,0:T(8,128)(2,1)}, u32[]{:S(2)}) %copy-start.12) | copy-done | bytes 2097176
  17.3 4.7 %cov_in_partial.1 = (bf16[16,256,128]{2,1,0:T(8,128)(2,1)}, f32[16,256,128]{2,1,0:T(8,128)S(1)}) custom-call(s32[64]{0:T(128)S(1)} %copy-done.10, bf16[1024,1024]{1,0:T(8,128)(2,1)S(1)} %copy-done.12, bf16[1024,1024]{1,0:T(8,128)(2,1)S(1)} %copy-done.12), custom_call_target="tpu_custom_call" | custom-call | flops 2147483648 | bytes 8388608 | tf_op jit(solution)/shard_map/cov_in_partial/pallas_call | solution.py:113
  22.0 1.0 collective-permute-start.4
  23.0 2.5 %collective-permute-start.3 = (bf16[32,1024]{1,0:T(8,128)(2,1)S(1)}, bf16[32,1024]{1,0:T(8,128)(2,1)S(1)}, u32[]{:S(2)}, u32[]{:S(2)}) collective-permute-start(bf16[32,1024]{1,0:T(8,128)(2,1)S(1)} %pad_maximum_fusion.1), channel_id=1, source_target_pairs={{0,192},{64,0},{128,64},{192,128},{1,193},{65,1},{129,65},{193,129... | collective-permute-start | bytes 196616 | tf_op jit(solution)/shard_map/ppermute | solution.py:262
  26.7 2.2 %copy-done = bf16[256,8192]{1,0:T(8,128)(2,1)S(1)} copy-done((bf16[256,8192]{1,0:T(8,128)(2,1)S(1)}, bf16[256,8192]{1,0:T(8,128)(2,1)}, u32[]{:S(2)}) %copy-start) | copy-done | bytes 4194328
  28.9 5.7 %cov_out_partial.1 = (bf16[16,144,128]{2,1,0:T(8,128)(2,1)S(1)}, f32[16,144,128]{2,1,0:T(8,128)S(1)}) custom-call(s32[64]{0:T(128)S(1)} %copy-done.9, s32[64]{0:T(128)S(1)} %copy-done.11, s32[1]{0:T(128)} %bitcast.1.core, bf16[256,8192]{1,0:T(8,128)(2,1)S(1)} %copy-done, bf16[256,8192]{1,0:T(8,128)(2,1)S(1)} %copy-done, bf16[256,8192]{1,0:T(8,128)(2,1)S(1)} %copy-done, ...), custom_call_target="tpu_custom_call" | custom-call | flops 536870912 | bytes 8388608 | tf_op jit(solution)/shard_map/cov_out_partial/pallas_call | solution.py:71
  34.6 0.8 copy-done.13
  36.2 1.0 collective-permute-start.5
  37.2 1.8 %collective-permute-done.5.recv_out = bf16[16,144,128]{2,1,0:T(8,128)(2,1)S(1)} collective-permute-done((bf16[16,144,128]{2,1,0:T(8,128)(2,1)}, bf16[16,144,128]{2,1,0:T(8,128)(2,1)S(1)}, u32[]{:S(2)}, u32[]{:S(2)}) %collective-permute-start.5) | collective-permute-done | bytes 589856 | tf_op jit(solution)/shard_map/ppermute | solution.py:239
  39.0 2.8 %pack.1 = bf16[16,400,128]{2,1,0:T(8,128)(2,1)} custom-call(f32[16,256,128]{2,1,0:T(8,128)S(1)} %get-tuple-element.24.keep_in, bf16[16,256,128]{2,1,0:T(8,128)(2,1)} %collective-permute-done.4.recv_in, f32[16,144,128]{2,1,0:T(8,128)S(1)} %get-tuple-element.31.keep_out, bf16[16,144,128]{2,1,0:T(8,128)(2,1)S(1)} %collective-permute-done.5.recv_out), custom_call_target="tpu_custom_call" | custom-call | flops 1024 | bytes 4915200 | tf_op jit(solution)/shard_map/pack/pallas_call | solution.py:194
  41.8 6.2 %all-to-all-start = ((bf16[16,400,128]{2,1,0:T(8,128)(2,1)}), bf16[16,400,128]{2,1,0:T(8,128)(2,1)S(1)}, u32[]{:S(2)}, u32[]{:S(2)}) async-start(bf16[16,400,128]{2,1,0:T(8,128)(2,1)} %pack.1), calls=%async_computation | async-start | bytes 3276800 | tf_op jit(solution)/shard_map/all_to_all | solution.py:274
  48.1 27.8 %all-gather.3.cloned.1.call-done = bf16[512,1024]{1,0:T(8,128)(2,1)} async-done(((bf16[128,1024]{1,0:T(8,128)(2,1)}), bf16[512,1024]{1,0:T(8,128)(2,1)}) %all-gather.3.cloned.1.call-update) | async-done | bytes 1048592 | tf_op jit(solution)/shard_map/all_gather | solution.py:269
  76.7 1.2 %copy-done.1 = bf16[512,1024]{1,0:T(8,128)(2,1)S(1)} copy-done((bf16[512,1024]{1,0:T(8,128)(2,1)S(1)}, bf16[512,1024]{1,0:T(8,128)(2,1)}, u32[]{:S(2)}) %copy-start.1) | copy-done | bytes 1048600
  79.1 1.0 copy-done.3
  80.1 1.2 %copy-done.4 = bf16[4,128,1024]{2,1,0:T(8,128)(2,1)S(1)} copy-done((bf16[4,128,1024]{2,1,0:T(8,128)(2,1)S(1)}, bf16[4,128,1024]{2,1,0:T(8,128)(2,1)}, u32[]{:S(2)}) %copy-start.4) | copy-done | bytes 1048600
  81.3 0.8 scale.1
  82.8 7.1 %all-to-all-start.1 = ((f32[32,8,128]{2,1,0:T(8,128)}), f32[32,8,128]{2,1,0:T(8,128)S(1)}, u32[]{:S(2)}, u32[]{:S(2)}) async-start(f32[32,8,128]{2,1,0:T(8,128)} %broadcast_in_dim.21), calls=%async_computation.1 | async-start | bytes 262144 | tf_op jit(solution)/shard_map/all_to_all | solution.py:289
  90.2 4.1 %collective-permute-start.7 = (f32[16,1024]{1,0:T(8,128)S(1)}, f32[16,1024]{1,0:T(8,128)S(1)}, u32[]{:S(2)}, u32[]{:S(2)}) collective-permute-start(f32[16,1024]{1,0:T(8,128)S(1)} %get-tuple-element.39), channel_id=1, source_target_pairs={{0,32},{32,0},{1,33},{33,1},{2,34},{34,2},{3,35},{35,3},{4,36},{36... | collective-permute-start | bytes 196616 | tf_op jit(solution)/shard_map/ppermute | solution.py:239
  96.2 1.4 %all-to-all-done.1.inner = f32[32,8,128]{2,1,0:T(8,128)S(1)} async-done(((f32[32,8,128]{2,1,0:T(8,128)}), f32[32,8,128]{2,1,0:T(8,128)S(1)}, u32[]{:S(2)}, u32[]{:S(2)}) %all-to-all-start.1) | async-done | bytes 131104 | tf_op jit(solution)/shard_map/all_to_all | solution.py:289
  98.3 6.1 %all-to-all-start.2 = ((f32[8,40,128]{2,1,0:T(8,128)}), f32[8,40,128]{2,1,0:T(8,128)S(1)}, u32[]{:S(2)}, u32[]{:S(2)}) async-start(f32[8,40,128]{2,1,0:T(8,128)} %join.1), calls=%async_computation.2 | async-start | bytes 327680 | tf_op jit(solution)/shard_map/all_to_all | solution.py:301
  104.5 1.2 %copy-done.5 = bf16[4,128,1024]{2,1,0:T(8,128)(2,1)S(1)} copy-done((bf16[4,128,1024]{2,1,0:T(8,128)(2,1)S(1)}, bf16[4,128,1024]{2,1,0:T(8,128)(2,1)}, u32[]{:S(2)}) %copy-start.5) | copy-done | bytes 1048600
  107.1 5.4 %all-to-all-done.2.column = f32[8,40,128]{2,1,0:T(8,128)S(1)} async-done(((f32[8,40,128]{2,1,0:T(8,128)}), f32[8,40,128]{2,1,0:T(8,128)S(1)}, u32[]{:S(2)}, u32[]{:S(2)}) %all-to-all-start.2) | async-done | bytes 163872 | tf_op jit(solution)/shard_map/all_to_all | solution.py:301
  112.5 1.4 %clip.1 = (f32[1,32,128]{2,1,0:T(8,128)}, f32[1024,128]{1,0:T(8,128)}) custom-call(f32[2]{0:T(128)S(1)} %pad_maximum_fusion.2.scalars, f32[8,40,128]{2,1,0:T(8,128)S(1)} %all-to-all-done.2.column, f32[1024,128]{1,0:T(8,128)S(1)} %finish.1.precond), custom_call_target="tpu_custom_call" | custom-call | flops 1048576 | bytes 688136 | tf_op jit(solution)/shard_map/clip/pallas_call | solution.py:194
  (49 shorter events, 8.3 us)
Async XLA Ops:
  7.2 68.8 %all-gather.3.cloned.1.call-start = ((), (), s32[]{:S(2)}) async-start(), calls=%async_computation.3 | async-start | bytes 1310720 | tf_op jit(solution)/shard_map/all_gather | solution.py:269
  7.2 19.5 %copy-start.9 = (s32[64]{0:T(128)S(1)}, s32[64]{0:T(128)}, u32[]{:S(2)}) copy-start(s32[64]{0:T(128)} %owners.1) | copy-start | bytes 772
  7.2 14.8 %collective-permute-start = (bf16[16,1024]{1,0:T(8,128)(2,1)}, bf16[16,1024]{1,0:T(8,128)(2,1)S(1)}, u32[]{:S(2)}, u32[]{:S(2)}) collective-permute-start(bf16[16,1024]{1,0:T(8,128)(2,1)} %bitcast.14), channel_id=1, source_target_pairs={{0,32},{32,0},{1,33},{33,1},{2,34},{34,2},{3,35},{35,3},{4,36},{36... | collective-permute-start | bytes 98312 | tf_op jit(solution)/shard_map/ppermute | solution.py:239
  15.7 1.6 %copy-start.12 = (bf16[1024,1024]{1,0:T(8,128)(2,1)S(1)}, bf16[1024,1024]{1,0:T(8,128)(2,1)}, u32[]{:S(2)}) copy-start(bf16[1024,1024]{1,0:T(8,128)(2,1)} %rhs.1) | copy-start | bytes 6291460
  17.3 4.7 %copy-start.14 = (bf16[1,16,1024]{2,1,0:T(8,128)(2,1)S(1)}, bf16[1,16,1024]{2,1,0:T(8,128)(2,1)}, u32[]{:S(2)}) copy-start(bf16[1,16,1024]{2,1,0:T(8,128)(2,1)} %param.14) | copy-start | bytes 98308
  17.3 9.4 %copy-start.11 = (s32[64]{0:T(128)S(1)}, s32[64]{0:T(128)}, u32[]{:S(2)}) copy-start(s32[64]{0:T(128)} %counts.2) | copy-start | bytes 772
  22.0 14.2 %collective-permute-start.4 = (bf16[16,256,128]{2,1,0:T(8,128)(2,1)}, bf16[16,256,128]{2,1,0:T(8,128)(2,1)}, u32[]{:S(2)}, u32[]{:S(2)}) collective-permute-start(bf16[16,256,128]{2,1,0:T(8,128)(2,1)} %get-tuple-element.29), channel_id=1, source_target_pairs={{0,4},{4,0},{1,5},{5,1},{2,6},{6,2},{3,7},{7,3},{8,12},{12,8},{9,1... | collective-permute-start | bytes 3145736 | tf_op jit(solution)/shard_map/ppermute | solution.py:239
  23.0 12.4 %collective-permute-start.3 = (bf16[32,1024]{1,0:T(8,128)(2,1)S(1)}, bf16[32,1024]{1,0:T(8,128)(2,1)S(1)}, u32[]{:S(2)}, u32[]{:S(2)}) collective-permute-start(bf16[32,1024]{1,0:T(8,128)(2,1)S(1)} %pad_maximum_fusion.1), channel_id=1, source_target_pairs={{0,192},{64,0},{128,64},{192,128},{1,193},{65,1},{129,65},{193,129... | collective-permute-start | bytes 196616 | tf_op jit(solution)/shard_map/ppermute | solution.py:262
  25.5 9.9 %collective-permute-start.2 = (bf16[32,1024]{1,0:T(8,128)(2,1)S(1)}, bf16[32,1024]{1,0:T(8,128)(2,1)S(1)}, u32[]{:S(2)}, u32[]{:S(2)}) collective-permute-start(bf16[32,1024]{1,0:T(8,128)(2,1)S(1)} %pad_maximum_fusion.1), channel_id=1, source_target_pairs={{0,128},{64,192},{128,0},{192,64},{1,129},{65,193},{129,1},{193,65... | collective-permute-start | bytes 196616 | tf_op jit(solution)/shard_map/ppermute | solution.py:262
  26.1 9.4 %collective-permute-start.1 = (bf16[32,1024]{1,0:T(8,128)(2,1)S(1)}, bf16[32,1024]{1,0:T(8,128)(2,1)S(1)}, u32[]{:S(2)}, u32[]{:S(2)}) collective-permute-start(bf16[32,1024]{1,0:T(8,128)(2,1)S(1)} %pad_maximum_fusion.1), channel_id=1, source_target_pairs={{0,64},{64,128},{128,192},{192,0},{1,65},{65,129},{129,193},{193,1... | collective-permute-start | bytes 196616 | tf_op jit(solution)/shard_map/ppermute | solution.py:262
  26.7 2.2 %copy-start = (bf16[256,8192]{1,0:T(8,128)(2,1)S(1)}, bf16[256,8192]{1,0:T(8,128)(2,1)}, u32[]{:S(2)}) copy-start(bf16[256,8192]{1,0:T(8,128)(2,1)} %refs_7_.1) | copy-start | bytes 12582916
  36.2 2.8 %collective-permute-start.5 = (bf16[16,144,128]{2,1,0:T(8,128)(2,1)}, bf16[16,144,128]{2,1,0:T(8,128)(2,1)S(1)}, u32[]{:S(2)}, u32[]{:S(2)}) collective-permute-start(bf16[16,144,128]{2,1,0:T(8,128)(2,1)} %copy-done.13), channel_id=1, source_target_pairs={{0,4},{4,0},{1,5},{5,1},{2,6},{6,2},{3,7},{7,3},{8,12},{12,8},{9,1... | collective-permute-start | bytes 1769480 | tf_op jit(solution)/shard_map/ppermute | solution.py:239
  41.8 34.8 %copy-start.15 = (f32[128]{0:T(128)S(1)}, f32[128]{0:T(128)}, u32[]{:S(2)}) copy-start(f32[128]{0:T(128)} %param.17) | copy-start | bytes 1540
  41.8 34.9 %copy-start.6 = (bf16[1024,128]{1,0:T(8,128)(2,1)S(1)}, bf16[1024,128]{1,0:T(8,128)(2,1)}, u32[]{:S(2)}) copy-start(bf16[1024,128]{1,0:T(8,128)(2,1)} %grad.3) | copy-start | bytes 786436
  41.8 38.3 %copy-start.7 = (bf16[1,128,128]{2,1,0:T(8,128)(2,1)S(1)}, bf16[1,128,128]{2,1,0:T(8,128)(2,1)}, u32[]{:S(2)}) copy-start(bf16[1,128,128]{2,1,0:T(8,128)(2,1)} %param.15) | copy-start | bytes 98308
  41.8 38.3 %copy-start.8 = (f32[1024]{0:T(1024)S(1)}, f32[1024]{0:T(1024)}, u32[]{:S(2)}) copy-start(f32[1024]{0:T(1024)} %param.16) | copy-start | bytes 12292
  41.8 40.3 %all-to-all-start = ((bf16[16,400,128]{2,1,0:T(8,128)(2,1)}), bf16[16,400,128]{2,1,0:T(8,128)(2,1)S(1)}, u32[]{:S(2)}, u32[]{:S(2)}) async-start(bf16[16,400,128]{2,1,0:T(8,128)(2,1)} %pack.1), calls=%async_computation | async-start | bytes 3276800 | tf_op jit(solution)/shard_map/all_to_all | solution.py:274
  75.9 3.2 %collective-permute-start.6 = (bf16[4,128,1024]{2,1,0:T(8,128)(2,1)}, bf16[4,128,1024]{2,1,0:T(8,128)(2,1)S(1)}, u32[]{:S(2)}, u32[]{:S(2)}) collective-permute-start(bf16[4,128,1024]{2,1,0:T(8,128)(2,1)} %bitcast.9), channel_id=1, source_target_pairs={{0,4},{4,0},{1,5},{5,1},{2,6},{6,2},{3,7},{7,3},{8,12},{12,8},{9,1... | collective-permute-start | bytes 3145736 | tf_op jit(solution)/shard_map/ppermute | solution.py:239
  76.7 1.2 %copy-start.1 = (bf16[512,1024]{1,0:T(8,128)(2,1)S(1)}, bf16[512,1024]{1,0:T(8,128)(2,1)}, u32[]{:S(2)}) copy-start(bf16[512,1024]{1,0:T(8,128)(2,1)} %all-gather.3.cloned.1.call-done) | copy-start | bytes 3145732
  80.1 1.2 %copy-start.4 = (bf16[4,128,1024]{2,1,0:T(8,128)(2,1)S(1)}, bf16[4,128,1024]{2,1,0:T(8,128)(2,1)}, u32[]{:S(2)}) copy-start(bf16[4,128,1024]{2,1,0:T(8,128)(2,1)} %copy-done.3) | copy-start | bytes 3145732
  81.3 23.2 %copy-start.2 = (bf16[512,1024]{1,0:T(8,128)(2,1)S(1)}, bf16[512,1024]{1,0:T(8,128)(2,1)}, u32[]{:S(2)}) copy-start(bf16[512,1024]{1,0:T(8,128)(2,1)} %all-gather.3.cloned.1.call-done) | copy-start | bytes 3145732
  82.8 14.8 %all-to-all-start.1 = ((f32[32,8,128]{2,1,0:T(8,128)}), f32[32,8,128]{2,1,0:T(8,128)S(1)}, u32[]{:S(2)}, u32[]{:S(2)}) async-start(f32[32,8,128]{2,1,0:T(8,128)} %broadcast_in_dim.21), calls=%async_computation.1 | async-start | bytes 262144 | tf_op jit(solution)/shard_map/all_to_all | solution.py:289
  90.2 8.1 %collective-permute-start.7 = (f32[16,1024]{1,0:T(8,128)S(1)}, f32[16,1024]{1,0:T(8,128)S(1)}, u32[]{:S(2)}, u32[]{:S(2)}) collective-permute-start(f32[16,1024]{1,0:T(8,128)S(1)} %get-tuple-element.39), channel_id=1, source_target_pairs={{0,32},{32,0},{1,33},{33,1},{2,34},{34,2},{3,35},{35,3},{4,36},{36... | collective-permute-start | bytes 196616 | tf_op jit(solution)/shard_map/ppermute | solution.py:239
  98.3 14.2 %all-to-all-start.2 = ((f32[8,40,128]{2,1,0:T(8,128)}), f32[8,40,128]{2,1,0:T(8,128)S(1)}, u32[]{:S(2)}, u32[]{:S(2)}) async-start(f32[8,40,128]{2,1,0:T(8,128)} %join.1), calls=%async_computation.2 | async-start | bytes 327680 | tf_op jit(solution)/shard_map/all_to_all | solution.py:301
  (4 other events, 3.7 us)
Sparse Core Ops, SparseCore 0:
  36.3 39.5 all-gather.2

commit v6 on v4

--- a/solution.py
+++ b/solution.py
@@ -17,7 +17,6 @@
 COLUMN = ("zh", "zl")
 VMEM = 20 << 20
 
-ROWS_IN = 256
 ROWS_OUT = 128
 ROWS_EXTRA = 16
 
@@ -87,57 +86,49 @@
     )(owners, counts, core, *([output_grads] * 8))
 
 
-def cov_in_kernel(counts, lhs, rhs, send, keep):
+def cov_in_kernel(counts, tokens, send, keep):
     dp, core, _ = counted()
     first = core == 0
-    rows = lax.broadcasted_iota(jnp.int32, lhs.shape, 0) < counts[dp]
-    masked = jnp.where(rows, lhs[...], jnp.zeros((), bf16))
-    part = dot(masked, rhs[...], 0, 0)
+    start = pl.multiple_of(pl.program_id(0) * 256, 256)
+    some = tokens[:, pl.ds(start, 256)]
+    live = lax.broadcasted_iota(jnp.int32, some.shape, 0) < counts[dp]
+    part = dot(jnp.where(live, some, jnp.zeros((), bf16)), tokens[...], 0, 0)
     for zh in range(2):
         for y in range(4):
             at = (zh * 4 + y) * 32
             low, high = part[at : at + 16], part[at + 16 : at + 32]
-            for dst, rows in (
-                (keep, jnp.where(first, low, high)),
-                (send, jnp.where(first, high, low).astype(bf16)),
-            ):
-                for c in range(8):
-                    at = c * 32 + zh * 16
-                    dst[y, at : at + 16] = rows[:, c * 128 : c * 128 + 128]
+            keep[y, zh * 16 : zh * 16 + 16] = jnp.where(first, low, high)
+            send[y, zh * 16 : zh * 16 + 16] = jnp.where(first, high, low).astype(bf16)
 
 
 def cov_in_partial(activations, counts):
     tok = activations.shape[0]
-    out = pl.BlockSpec((4, ROWS_IN, 128), lambda s, *_: (s, 0, 0))
+    out = pl.BlockSpec((4, 32, 1024), lambda s, *_: (s, 0, 0))
     return pl.pallas_call(
         cov_in_kernel,
         grid_spec=pltpu.PrefetchScalarGridSpec(
             num_scalar_prefetch=1,
             grid=(4,),
-            in_specs=[
-                pl.BlockSpec((tok, 256), lambda s, *_: (0, s)),
-                pl.BlockSpec((tok, 1024), lambda s, *_: (0, 0)),
-            ],
+            in_specs=[pl.BlockSpec((tok, 1024), lambda s, *_: (0, 0))],
             out_specs=[out, out],
         ),
         out_shape=[
-            jax.ShapeDtypeStruct((16, ROWS_IN, 128), bf16),
-            jax.ShapeDtypeStruct((16, ROWS_IN, 128), f32),
+            jax.ShapeDtypeStruct((16, 32, 1024), bf16),
+            jax.ShapeDtypeStruct((16, 32, 1024), f32),
         ],
-        compiler_params=pltpu.CompilerParams(vmem_limit_bytes=VMEM),
+        compiler_params=pltpu.CompilerParams(vmem_limit_bytes=60 << 20),
         cost_estimate=pl.CostEstimate(
             flops=2 * tok * 1024 * 1024, bytes_accessed=tok * 4096 + (4 << 20), transcendentals=0
         ),
         name="cov_in_partial",
-    )(counts, activations, activations)
-
-
-def pack_in_kernel(keep, recv, msg):
-    def step(s, _):
-        msg[s] = (keep[s] + recv[s].astype(f32)).astype(bf16)
-        return 0
-
-    lax.fori_loop(0, 16, step, 0)
+    )(counts, activations)
+
+
+def pack_in_kernel(mine, pair, keep, recv, msg):
+    for s in range(msg.shape[0]):
+        msg[s, 0:16] = mine[...]
+        msg[s, 16:32] = pair[...]
+        msg[s, 32:64] = (keep[s] + recv[s].astype(f32)).astype(bf16)
 
 
 def pack_out_kernel(keep, recv, inner, other_inner, msg):
@@ -150,14 +141,28 @@
     parts = jnp.where(
         row == 1, high, jnp.where(row == 2, middle, jnp.where(row == 3, low, 0.0))
     )
-
-    def step(s, _):
+    for s in range(msg.shape[0]):
         both = keep[s] + recv[s].astype(f32)
         msg[s, 0:ROWS_OUT] = both[0:ROWS_OUT].astype(bf16)
         msg[s, ROWS_OUT:] = (both[ROWS_OUT:] + parts).astype(bf16)
-        return 0
-
-    lax.fori_loop(0, 16, step, 0)
+
+
+def streamed(kernel, steps, out, *args):
+    def spec(a):
+        if a.shape[0] == 16 and a.ndim == 3:
+            return pl.BlockSpec((16 // steps,) + a.shape[1:], lambda s: (s, 0, 0))
+        return pl.BlockSpec(a.shape, lambda s: (0,) * a.ndim)
+
+    return pl.pallas_call(
+        kernel,
+        grid=(steps,),
+        in_specs=[spec(a) for a in args],
+        out_specs=spec(out),
+        out_shape=out,
+        compiler_params=pltpu.CompilerParams(vmem_limit_bytes=52 << 20),
+        cost_estimate=pl.CostEstimate(flops=1024, bytes_accessed=1024, transcendentals=0),
+        name=kernel.__name__[:-7],
+    )(*args)
 
 
 def slab_rows(core):
@@ -229,11 +234,10 @@
 
 def unpack_in_kernel(msg, keep, send):
     first = lax.axis_index("zh") == 0
-    for c in range(8):
-        pair = total(msg, c * 32, 32)
-        low, high = pair[:16], pair[16:]
-        keep[:, c * 128 : c * 128 + 128] = jnp.where(first, low, high)
-        send[:, c * 128 : c * 128 + 128] = jnp.where(first, high, low)
+    pair = total(msg, 32, 32)
+    low, high = pair[:16], pair[16:]
+    keep[...] = jnp.where(first, low, high)
+    send[...] = jnp.where(first, high, low)
 
 
 def unpack_out_kernel(msg, column):
@@ -272,18 +276,19 @@
     shape = jax.ShapeDtypeStruct
     core = lax.axis_index("core").astype(jnp.int32)[None]
     mine = basis_in[0]
-    slabs = jnp.concatenate([mine, swap(mine, "zh")], axis=0)
+    pair = swap(mine, "zh")
     send_in, keep_in = cov_in_partial(activations, token_counts)
-    slabs, send_in, counts = lax.optimization_barrier((slabs, send_in, token_counts))
+    pair, send_in = lax.optimization_barrier((pair, send_in))
     recv_in = swap(send_in, "core")
-    q_own = lax.all_to_all(
-        jnp.broadcast_to(slabs[None], (16,) + slabs.shape), PLANE, 0, 0, tiled=True
-    )
+    msg_in = streamed(
+        pack_in_kernel, 4, shape((16, 64, 1024), bf16), mine, pair, keep_in, recv_in
+    )
+    msg_in, counts = lax.optimization_barrier((msg_in, token_counts))
+    got_in = lax.all_to_all(msg_in, PLANE, 0, 0, tiled=True)
     send_out, keep_out = cov_out_partial(output_grads, owner_blocks, counts, core)
     recv_out = swap(send_out, "core")
-    (msg_in,) = on_chip(pack_in_kernel, [shape((16, ROWS_IN, 128), bf16)], 1024, keep_in, recv_in)
-    q_own, msg_in, keep_out = lax.optimization_barrier((q_own, msg_in, keep_out))
-    got_in = lax.all_to_all(msg_in, PLANE, 0, 0, tiled=True)
+    got_in, keep_out, recv_out = lax.optimization_barrier((got_in, keep_out, recv_out))
+    q_own = got_in[:, :32]
     q_other = swap(q_own, "core")
     (partial,) = on_chip(rotate_kernel, [shape((128, 1024), f32)], 1024, q_own, gradient)
     back, inner = on_chip(
@@ -297,14 +302,16 @@
         values_in[None, :],
         values_out[:, None],
     )
-    (msg_out,) = on_chip(
+    (precond,) = on_chip(finish_kernel, [shape((1024, 128), f32)], 1024, q_own, q_other, back)
+    other_inner, precond = lax.optimization_barrier((swap(inner, "core"), precond))
+    msg_out = streamed(
         pack_out_kernel,
-        [shape((16, ROWS_OUT + ROWS_EXTRA, 128), bf16)],
-        1024,
+        2,
+        shape((16, ROWS_OUT + ROWS_EXTRA, 128), bf16),
         keep_out,
         recv_out,
         inner,
-        swap(inner, "core"),
+        other_inner,
     )
     got_in, msg_out = lax.optimization_barrier((got_in, msg_out))
     got_out = lax.all_to_all(msg_out, PLANE, 0, 0, tiled=True)
@@ -313,7 +320,6 @@
     (column,) = on_chip(unpack_out_kernel, [shape((8, 40, 128), f32)], 1024, got_out)
     column, recv_slab = lax.optimization_barrier((column, recv_slab))
     column = lax.all_to_all(column, COLUMN, 0, 0, tiled=True)
-    (precond,) = on_chip(finish_kernel, [shape((1024, 128), f32)], 1024, q_own, q_other, back)
     cov_in = ((keep_slab + recv_slab) / token_total)[None]
     cov_out, update = on_chip(
         clip_kernel,

time: 97.1 us -> 101 us (1.040)
  Pallas kernels: 18.2 us -> 24.8 us
  local copies, waits for them, and re-layouts: 10.5 us -> 5.03 us
  waiting for transfers between devices: 34.6 us -> 37.9 us
  starting transfers between devices: 29.4 us -> 28 us
    all_to_all x1 -> x0, starting transfers between devices: 6.74 us -> none  [local(): lax.all_to_all(jnp.broadcast_to(slabs[None], (16,) + slabs.shape), PLANE,...]
    pallas_call x0 -> x2, Pallas kernels: none -> 5.91 us  [streamed(): pl.pallas_call(kernel, grid=(steps,), in_specs=[spec(a) for a in args], o...]
    all_to_all x1 -> x0, waiting for transfers between devices: 5.88 us -> none  [local(): lax.all_to_all(jnp.broadcast_to(slabs[None], (16,) + slabs.shape), PLANE,...]
    ppermute x6, waiting for transfers between devices: 0.83 us -> 6.08 us  [swap(): return lax.ppermute(array, axis, [(0, 1), (1, 0)])]
    all_to_all x1, waiting for transfers between devices: 12.3 us -> 17 us  [local(): got_in = lax.all_to_all(msg_in, PLANE, 0, 0, tiled=True)]
    unnamed x36 -> x26, local copies, waits for them, and re-layouts: 9.23 us -> 4.83 us
    all_to_all x1, starting transfers between devices: 3.65 us -> 6.89 us  [local(): got_in = lax.all_to_all(msg_in, PLANE, 0, 0, tiled=True)]
    ppermute x6, starting transfers between devices: 11.3 us -> 14 us  [swap(): return lax.ppermute(array, axis, [(0, 1), (1, 0)])]
  transfers between devices with their start and end apart: 10 -> 9, of which waited for: 5 -> 6; matrix products, arithmetic and copies ran while one was open for 3% -> 1% of each run, Pallas kernels for 17% -> 16%
where the time goes in v6:
time: 101 us; the launch traced here: 99.1 us
  waiting for transfers between devices  37.9 us (38%)
  starting transfers between devices  28 us (28%)
  Pallas kernels  24.8 us (25%)
  local copies, waits for them, and re-layouts  5.03 us (5%)
  between operations  2.07 us (2%)
  other arithmetic  1.35 us (1%)
    all_to_all x1, waiting for transfers between devices, local(): got_in = lax.all_to_all(msg_in, PLANE, 0, 0, tiled=True)  17 us
    ppermute x6, starting transfers between devices, swap(): return lax.ppermute(array, axis, [(0, 1), (1, 0)])  14 us
    all_to_all x1, waiting for transfers between devices, local(): column = lax.all_to_all(column, COLUMN, 0, 0, tiled=True)  7.57 us
    all_to_all x1, waiting for transfers between devices, local(): got_out = lax.all_to_all(msg_out, PLANE, 0, 0, tiled=True)  7.19 us
    all_to_all x1, starting transfers between devices, local(): got_in = lax.all_to_all(msg_in, PLANE, 0, 0, tiled=True)  6.89 us
    pallas_call x6, Pallas kernels, on_chip(): pl.pallas_call(kernel, in_specs=[whole if a.ndim > 1 else pl.BlockSpec(me...  6.72 us
    pallas_call x1, Pallas kernels, cov_in_partial(): pl.pallas_call(cov_in_kernel, grid_spec=pltpu.PrefetchScalarGridSpec(num_...  6.41 us
    ppermute x6, waiting for transfers between devices, swap(): return lax.ppermute(array, axis, [(0, 1), (1, 0)])  6.08 us
  transfers between devices with their start and end apart: 9, of which 6 were waited for; matrix products, arithmetic and copies ran while one was open for 1% of the time, Pallas kernels for 16%

profile of v6, /device:TPU:1, one launch (start us, length us, event | category | flops | bytes accessed | tf_op | source)
XLA Modules:
  0.0 99.1 jit_solution(17096565725012328858)
XLA Ops:
  0.6 7.8 %collective-permute-start = (bf16[16,1024]{1,0:T(8,128)(2,1)}, bf16[16,1024]{1,0:T(8,128)(2,1)S(1)}, u32[]{:S(2)}, u32[]{:S(2)}) collective-permute-start(bf16[16,1024]{1,0:T(8,128)(2,1)} %bitcast.9), channel_id=1, source_target_pairs={{0,32},{32,0},{1,33},{33,1},{2,34},{34,2},{3,35},{35,3},{4,36},{36... | collective-permute-start | bytes 98312 | tf_op jit(solution)/shard_map/ppermute | solution.py:260
  8.5 6.4 %cov_in_partial.1 = (bf16[16,32,1024]{2,1,0:T(8,128)(2,1)}, f32[16,32,1024]{2,1,0:T(8,128)}) custom-call(s32[64]{0:T(128)} %counts.2, bf16[1024,1024]{1,0:T(8,128)(2,1)} %tokens.1), custom_call_target="tpu_custom_call" | custom-call | flops 2147483648 | bytes 8388608 | tf_op jit(solution)/shard_map/cov_in_partial/pallas_call | solution.py:107
  14.9 1.0 collective-permute-start.1
  15.8 2.5 %collective-permute-done.1.recv = bf16[16,32,1024]{2,1,0:T(8,128)(2,1)S(1)} collective-permute-done((bf16[16,32,1024]{2,1,0:T(8,128)(2,1)}, bf16[16,32,1024]{2,1,0:T(8,128)(2,1)S(1)}, u32[]{:S(2)}, u32[]{:S(2)}) %collective-permute-start.1) | collective-permute-done | bytes 1048608 | tf_op jit(solution)/shard_map/ppermute | solution.py:260
  18.3 3.9 %pack_in.1 = bf16[16,64,1024]{2,1,0:T(8,128)(2,1)} custom-call(bf16[16,1024]{1,0:T(8,128)(2,1)S(1)} %bitcast.10, bf16[16,1024]{1,0:T(8,128)(2,1)S(1)} %collective-permute-done.pair, f32[16,32,1024]{2,1,0:T(8,128)} %get-tuple-element.28.keep, bf16[16,32,1024]{2,1,0:T(8,128)(2,1)S(1)} %collective-permute-done.1.recv), custom_call_target="tpu_custom_call" | custom-call | flops 1024 | bytes 1024 | tf_op jit(solution)/shard_map/pack_in/pallas_call | solution.py:156
  22.2 6.9 %all-to-all-start = ((bf16[16,64,1024]{2,1,0:T(8,128)(2,1)}), bf16[16,64,1024]{2,1,0:T(8,128)(2,1)S(1)}, u32[]{:S(2)}, u32[]{:S(2)}) async-start(bf16[16,64,1024]{2,1,0:T(8,128)(2,1)} %pack_in.1), calls=%async_computation | async-start | bytes 4194304 | tf_op jit(solution)/shard_map/all_to_all | solution.py:287
  29.1 2.2 %copy-done = bf16[256,8192]{1,0:T(8,128)(2,1)S(1)} copy-done((bf16[256,8192]{1,0:T(8,128)(2,1)S(1)}, bf16[256,8192]{1,0:T(8,128)(2,1)}, u32[]{:S(2)}) %copy-start) | copy-done | bytes 4194328
  31.3 5.7 %cov_out_partial.1 = (bf16[16,144,128]{2,1,0:T(8,128)(2,1)S(1)}, f32[16,144,128]{2,1,0:T(8,128)S(1)}) custom-call(s32[64]{0:T(128)S(1)} %copy-done.10, s32[64]{0:T(128)S(1)} %copy-done.11, s32[1]{0:T(128)} %bitcast.1.core, bf16[256,8192]{1,0:T(8,128)(2,1)S(1)} %copy-done, bf16[256,8192]{1,0:T(8,128)(2,1)S(1)} %copy-done, bf16[256,8192]{1,0:T(8,128)(2,1)S(1)} %copy-done, ...), custom_call_target="tpu_custom_call" | custom-call | flops 536870912 | bytes 8388608 | tf_op jit(solution)/shard_map/cov_out_partial/pallas_call | solution.py:69
  37.1 1.0 %copy-done.3 = f32[16,144,128]{2,1,0:T(8,128)} copy-done((f32[16,144,128]{2,1,0:T(8,128)}, f32[16,144,128]{2,1,0:T(8,128)S(1)}, u32[]{:S(2)}) %copy-start.3) | copy-done | bytes 1179672
  38.8 1.6 %collective-permute-done.2.recv = bf16[16,144,128]{2,1,0:T(8,128)(2,1)S(1)} collective-permute-done((bf16[16,144,128]{2,1,0:T(8,128)(2,1)S(1)}, bf16[16,144,128]{2,1,0:T(8,128)(2,1)S(1)}, u32[]{:S(2)}, u32[]{:S(2)}) %collective-permute-start.2) | collective-permute-done | bytes 589856 | tf_op jit(solution)/shard_map/ppermute | solution.py:260
  40.5 0.8 copy-done.5
  41.3 17.0 %all-to-all-done.msg = bf16[16,64,1024]{2,1,0:T(8,128)(2,1)S(1)} async-done(((bf16[16,64,1024]{2,1,0:T(8,128)(2,1)}), bf16[16,64,1024]{2,1,0:T(8,128)(2,1)S(1)}, u32[]{:S(2)}, u32[]{:S(2)}) %all-to-all-start) | async-done | bytes 2097184 | tf_op jit(solution)/shard_map/all_to_all | solution.py:287
  58.4 2.7 %collective-permute-start.3 = (bf16[16,32,1024]{2,1,0:T(8,128)(2,1)S(1)}, bf16[16,32,1024]{2,1,0:T(8,128)(2,1)}, u32[]{:S(2)}, u32[]{:S(2)}) collective-permute-start(bf16[16,32,1024]{2,1,0:T(8,128)(2,1)S(1)} %slice.3.slabs.q_own), channel_id=1, source_target_pairs={{0,4},{4,0},{1,5},{5,1},{2,6},{6,2},{3,7},{7,3},{8,12},{12,8},{9,1... | collective-permute-start | bytes 3145736 | tf_op jit(solution)/shard_map/ppermute | solution.py:260
  61.6 1.9 %collective-permute-done.3.slabs.q_other = bf16[16,32,1024]{2,1,0:T(8,128)(2,1)} collective-permute-done((bf16[16,32,1024]{2,1,0:T(8,128)(2,1)S(1)}, bf16[16,32,1024]{2,1,0:T(8,128)(2,1)}, u32[]{:S(2)}, u32[]{:S(2)}) %collective-permute-start.3) | collective-permute-done | bytes 1048608 | tf_op jit(solution)/shard_map/ppermute | solution.py:260
  63.5 2.1 %scale.1 = (bf16[128,1024]{1,0:T(8,128)(2,1)S(1)}, f32[8,128]{1,0:T(8,128)S(1)}) custom-call(bf16[16,32,1024]{2,1,0:T(8,128)(2,1)} %collective-permute-done.3.slabs.q_other, bf16[1024,128]{1,0:T(8,128)(2,1)S(1)} %copy-done.4, f32[128,1024]{1,0:T(8,128)S(1)} %rotate.1.partial, bf16[128,128]{1,0:T(8,128)(2,1)S(1)} %bitcast.8, f32[1,1024]{1,0:T(1,128)S(1)} %bitcast.11, ...), custom_call_target="tpu_custom_call" | custom-call | flops 1024 | bytes 1872384 | tf_op jit(solution)/shard_map/scale/pallas_call | solution.py:217
  66.0 1.9 %finish.1.precond = f32[1024,128]{1,0:T(8,128)S(1)} custom-call(bf16[16,32,1024]{2,1,0:T(8,128)(2,1)S(1)} %slice.3.slabs.q_own, bf16[16,32,1024]{2,1,0:T(8,128)(2,1)} %collective-permute-done.3.slabs.q_other, bf16[128,1024]{1,0:T(8,128)(2,1)S(1)} %get-tuple-element.38.back), custom_call_target="tpu_custom_call" | custom-call | flops 1024 | bytes 2359296 | tf_op jit(solution)/shard_map/finish/pallas_call | solution.py:217
  68.7 2.0 %pack_out.1 = bf16[16,144,128]{2,1,0:T(8,128)(2,1)} custom-call(f32[16,144,128]{2,1,0:T(8,128)} %copy-done.3, bf16[16,144,128]{2,1,0:T(8,128)(2,1)S(1)} %copy-done.6, f32[8,128]{1,0:T(8,128)S(1)} %get-tuple-element.37.inner, f32[8,128]{1,0:T(8,128)S(1)} %collective-permute-done.4.other_inner), custom_call_target="tpu_custom_call" | custom-call | flops 1024 | bytes 1024 | tf_op jit(solution)/shard_map/pack_out/pallas_call | solution.py:156
  70.8 3.7 %all-to-all-start.1 = ((bf16[16,144,128]{2,1,0:T(8,128)(2,1)}), bf16[16,144,128]{2,1,0:T(8,128)(2,1)S(1)}, u32[]{:S(2)}, u32[]{:S(2)}) async-start(bf16[16,144,128]{2,1,0:T(8,128)(2,1)} %pack_out.1), calls=%async_computation.1 | async-start | bytes 1179648 | tf_op jit(solution)/shard_map/all_to_all | solution.py:317
  74.7 1.4 %collective-permute-start.5 = (f32[16,1024]{1,0:T(8,128)S(1)}, f32[16,1024]{1,0:T(8,128)S(1)}, u32[]{:S(2)}, u32[]{:S(2)}) collective-permute-start(f32[16,1024]{1,0:T(8,128)S(1)} %get-tuple-element.43), channel_id=1, source_target_pairs={{0,32},{32,0},{1,33},{33,1},{2,34},{34,2},{3,35},{35,3},{4,36},{36... | collective-permute-start | bytes 196616 | tf_op jit(solution)/shard_map/ppermute | solution.py:260
  78.0 7.2 %all-to-all-done.1.msg = bf16[16,144,128]{2,1,0:T(8,128)(2,1)S(1)} async-done(((bf16[16,144,128]{2,1,0:T(8,128)(2,1)}), bf16[16,144,128]{2,1,0:T(8,128)(2,1)S(1)}, u32[]{:S(2)}, u32[]{:S(2)}) %all-to-all-start.1) | async-done | bytes 589856 | tf_op jit(solution)/shard_map/all_to_all | solution.py:317
  85.2 0.8 unpack_out.1
  86.0 3.4 %all-to-all-start.2 = ((f32[8,40,128]{2,1,0:T(8,128)}), f32[8,40,128]{2,1,0:T(8,128)S(1)}, u32[]{:S(2)}, u32[]{:S(2)}) async-start(f32[8,40,128]{2,1,0:T(8,128)} %unpack_out.1), calls=%async_computation.2 | async-start | bytes 327680 | tf_op jit(solution)/shard_map/all_to_all | solution.py:322
  90.1 7.6 %all-to-all-done.2.column = f32[8,40,128]{2,1,0:T(8,128)S(1)} async-done(((f32[8,40,128]{2,1,0:T(8,128)}), f32[8,40,128]{2,1,0:T(8,128)S(1)}, u32[]{:S(2)}, u32[]{:S(2)}) %all-to-all-start.2) | async-done | bytes 163872 | tf_op jit(solution)/shard_map/all_to_all | solution.py:322
  97.7 1.4 %clip.1 = (f32[1,32,128]{2,1,0:T(8,128)}, f32[1024,128]{1,0:T(8,128)}) custom-call(f32[2]{0:T(128)S(1)} %pad_maximum_fusion.scalars, f32[8,40,128]{2,1,0:T(8,128)S(1)} %all-to-all-done.2.column, f32[1024,128]{1,0:T(8,128)S(1)} %copy-done.2), custom_call_target="tpu_custom_call" | custom-call | flops 1048576 | bytes 688136 | tf_op jit(solution)/shard_map/clip/pallas_call | solution.py:217
  (35 shorter events, 4.0 us)
Async XLA Ops:
  0.6 17.7 %copy-start.8 = (bf16[1,16,1024]{2,1,0:T(8,128)(2,1)S(1)}, bf16[1,16,1024]{2,1,0:T(8,128)(2,1)}, u32[]{:S(2)}) copy-start(bf16[1,16,1024]{2,1,0:T(8,128)(2,1)} %param.14) | copy-start | bytes 98308
  0.6 14.2 %collective-permute-start = (bf16[16,1024]{1,0:T(8,128)(2,1)}, bf16[16,1024]{1,0:T(8,128)(2,1)S(1)}, u32[]{:S(2)}, u32[]{:S(2)}) collective-permute-start(bf16[16,1024]{1,0:T(8,128)(2,1)} %bitcast.9), channel_id=1, source_target_pairs={{0,32},{32,0},{1,33},{33,1},{2,34},{34,2},{3,35},{35,3},{4,36},{36... | collective-permute-start | bytes 98312 | tf_op jit(solution)/shard_map/ppermute | solution.py:260
  14.9 3.5 %collective-permute-start.1 = (bf16[16,32,1024]{2,1,0:T(8,128)(2,1)}, bf16[16,32,1024]{2,1,0:T(8,128)(2,1)S(1)}, u32[]{:S(2)}, u32[]{:S(2)}) collective-permute-start(bf16[16,32,1024]{2,1,0:T(8,128)(2,1)} %get-tuple-element.29), channel_id=1, source_target_pairs={{0,4},{4,0},{1,5},{5,1},{2,6},{6,2},{3,7},{7,3},{8,12},{12,8},{9,1... | collective-permute-start | bytes 3145736 | tf_op jit(solution)/shard_map/ppermute | solution.py:260
  22.2 6.9 %copy-start.10 = (s32[64]{0:T(128)S(1)}, s32[64]{0:T(128)}, u32[]{:S(2)}) copy-start(s32[64]{0:T(128)} %owners.1) | copy-start | bytes 772
  22.2 6.9 %copy-start.11 = (s32[64]{0:T(128)S(1)}, s32[64]{0:T(128)}, u32[]{:S(2)}) copy-start(s32[64]{0:T(128)} %counts.2) | copy-start | bytes 772
  22.2 36.1 %all-to-all-start = ((bf16[16,64,1024]{2,1,0:T(8,128)(2,1)}), bf16[16,64,1024]{2,1,0:T(8,128)(2,1)S(1)}, u32[]{:S(2)}, u32[]{:S(2)}) async-start(bf16[16,64,1024]{2,1,0:T(8,128)(2,1)} %pack_in.1), calls=%async_computation | async-start | bytes 4194304 | tf_op jit(solution)/shard_map/all_to_all | solution.py:287
  29.1 2.2 %copy-start = (bf16[256,8192]{1,0:T(8,128)(2,1)S(1)}, bf16[256,8192]{1,0:T(8,128)(2,1)}, u32[]{:S(2)}) copy-start(bf16[256,8192]{1,0:T(8,128)(2,1)} %refs_7_.1) | copy-start | bytes 12582916
  37.1 1.0 %copy-start.3 = (f32[16,144,128]{2,1,0:T(8,128)}, f32[16,144,128]{2,1,0:T(8,128)S(1)}, u32[]{:S(2)}) copy-start(f32[16,144,128]{2,1,0:T(8,128)S(1)} %get-tuple-element.35.keep) | copy-start | bytes 3538948
  38.1 23.0 %copy-start.12 = (f32[128]{0:T(128)S(1)}, f32[128]{0:T(128)}, u32[]{:S(2)}) copy-start(f32[128]{0:T(128)} %param.17) | copy-start | bytes 1540
  38.1 23.1 %copy-start.4 = (bf16[1024,128]{1,0:T(8,128)(2,1)S(1)}, bf16[1024,128]{1,0:T(8,128)(2,1)}, u32[]{:S(2)}) copy-start(bf16[1024,128]{1,0:T(8,128)(2,1)} %grad.3) | copy-start | bytes 786436
  38.1 25.4 %copy-start.7 = (bf16[1,128,128]{2,1,0:T(8,128)(2,1)S(1)}, bf16[1,128,128]{2,1,0:T(8,128)(2,1)}, u32[]{:S(2)}) copy-start(bf16[1,128,128]{2,1,0:T(8,128)(2,1)} %param.15) | copy-start | bytes 98308
  38.1 25.4 %copy-start.9 = (f32[1024]{0:T(1024)S(1)}, f32[1024]{0:T(1024)}, u32[]{:S(2)}) copy-start(f32[1024]{0:T(1024)} %param.16) | copy-start | bytes 12292
  38.1 2.4 %collective-permute-start.2 = (bf16[16,144,128]{2,1,0:T(8,128)(2,1)S(1)}, bf16[16,144,128]{2,1,0:T(8,128)(2,1)S(1)}, u32[]{:S(2)}, u32[]{:S(2)}) collective-permute-start(bf16[16,144,128]{2,1,0:T(8,128)(2,1)S(1)} %get-tuple-element.33), channel_id=1, source_target_pairs={{0,4},{4,0},{1,5},{5,1},{2,6},{6,2},{3,7},{7,3},{8,12},{12,8},{9,1... | collective-permute-start | bytes 1769480 | tf_op jit(solution)/shard_map/ppermute | solution.py:260
  40.5 0.8 copy-start.5
  58.4 5.1 %collective-permute-start.3 = (bf16[16,32,1024]{2,1,0:T(8,128)(2,1)S(1)}, bf16[16,32,1024]{2,1,0:T(8,128)(2,1)}, u32[]{:S(2)}, u32[]{:S(2)}) collective-permute-start(bf16[16,32,1024]{2,1,0:T(8,128)(2,1)S(1)} %slice.3.slabs.q_own), channel_id=1, source_target_pairs={{0,4},{4,0},{1,5},{5,1},{2,6},{6,2},{3,7},{7,3},{8,12},{12,8},{9,1... | collective-permute-start | bytes 3145736 | tf_op jit(solution)/shard_map/ppermute | solution.py:260
  63.5 5.2 %copy-start.6 = (bf16[16,144,128]{2,1,0:T(8,128)(2,1)S(1)}, bf16[16,144,128]{2,1,0:T(8,128)(2,1)}, u32[]{:S(2)}) copy-start(bf16[16,144,128]{2,1,0:T(8,128)(2,1)} %copy-done.5) | copy-start | bytes 1769476
  65.6 3.1 %collective-permute-start.4 = (f32[8,128]{1,0:T(8,128)S(1)}, f32[8,128]{1,0:T(8,128)S(1)}, u32[]{:S(2)}, u32[]{:S(2)}) collective-permute-start(f32[8,128]{1,0:T(8,128)S(1)} %get-tuple-element.37.inner), channel_id=1, source_target_pairs={{0,4},{4,0},{1,5},{5,1},{2,6},{6,2},{3,7},{7,3},{8,12},{12,8},{9,1... | collective-permute-start | bytes 12296 | tf_op jit(solution)/shard_map/ppermute | solution.py:260
  67.9 0.8 copy-start.1
  70.8 26.9 %copy-start.2 = (f32[1024,128]{1,0:T(8,128)S(1)}, f32[1024,128]{1,0:T(8,128)}, u32[]{:S(2)}) copy-start(f32[1024,128]{1,0:T(8,128)} %copy-done.1) | copy-start | bytes 1572868
  70.8 14.4 %all-to-all-start.1 = ((bf16[16,144,128]{2,1,0:T(8,128)(2,1)}), bf16[16,144,128]{2,1,0:T(8,128)(2,1)S(1)}, u32[]{:S(2)}, u32[]{:S(2)}) async-start(bf16[16,144,128]{2,1,0:T(8,128)(2,1)} %pack_out.1), calls=%async_computation.1 | async-start | bytes 1179648 | tf_op jit(solution)/shard_map/all_to_all | solution.py:317
  74.7 11.4 %collective-permute-start.5 = (f32[16,1024]{1,0:T(8,128)S(1)}, f32[16,1024]{1,0:T(8,128)S(1)}, u32[]{:S(2)}, u32[]{:S(2)}) collective-permute-start(f32[16,1024]{1,0:T(8,128)S(1)} %get-tuple-element.43), channel_id=1, source_target_pairs={{0,32},{32,0},{1,33},{33,1},{2,34},{34,2},{3,35},{35,3},{4,36},{36... | collective-permute-start | bytes 196616 | tf_op jit(solution)/shard_map/ppermute | solution.py:260
  86.0 11.7 %all-to-all-start.2 = ((f32[8,40,128]{2,1,0:T(8,128)}), f32[8,40,128]{2,1,0:T(8,128)S(1)}, u32[]{:S(2)}, u32[]{:S(2)}) async-start(f32[8,40,128]{2,1,0:T(8,128)} %unpack_out.1), calls=%async_computation.2 | async-start | bytes 327680 | tf_op jit(solution)/shard_map/all_to_all | solution.py:322

commit v7 on v4

--- a/solution.py
+++ b/solution.py
@@ -17,7 +17,6 @@
 COLUMN = ("zh", "zl")
 VMEM = 20 << 20
 
-ROWS_IN = 256
 ROWS_OUT = 128
 ROWS_EXTRA = 16
 
@@ -32,104 +31,47 @@
     return dp, core, lax.axis_index("zl")
 
 
-def cov_out_kernel(owners, counts, core, *refs):
-    blocks, (send, keep) = refs[:8], refs[8:]
-    dp, _, zl = counted()
-    quarter = blocks[0].shape[0]
+def cov_out_kernel(owners, counts, tokens, send, keep):
+    dp, core, zl = counted()
+    quarter = tokens.shape[0]
     live = counts[dp] - zl * quarter
-    rows = lax.broadcasted_iota(jnp.int32, blocks[0].shape, 0) < live
+    live = lax.broadcasted_iota(jnp.int32, (quarter, 256), 0) < live
     row = lax.broadcasted_iota(jnp.int32, (128, 128), 0)
     col = lax.broadcasted_iota(jnp.int32, (128, 128), 1)
     top = lax.broadcasted_iota(jnp.int32, (ROWS_EXTRA, 128), 0) == 0
 
-    rows = jnp.concatenate([rows, rows], axis=1)
-    for y in range(2):
-        for at, dst in ((0, keep), (4, send)):
-            full = jnp.concatenate([blocks[at + y][...], blocks[at + 2 + y][...]], axis=1)
-            both = dot(jnp.where(rows, full, jnp.zeros((), bf16)), full, 0, 0)
+    def block(x, zh, y, c):
+        at = owners[((x * 2 + zh) * 4 + y) * 2 + c]
+        return tokens[:, pl.ds(pl.multiple_of(at * 128, 128), 128)]
+
+    def step(s, _):
+        x, y = s // 4, s % 4
+        for c, dst in ((core, keep), (1 - core, send)):
+            full = jnp.concatenate([block(x, 0, y, c), block(x, 1, y, c)], axis=1)
+            both = dot(jnp.where(live, full, jnp.zeros((), bf16)), full, 0, 0)
             first, second = both[:128, :128], both[128:, 128:]
             diag = jnp.sum(jnp.where(row == col, second, 0.0), axis=0, keepdims=True)
-            dst[y, 0:ROWS_OUT] = jnp.where(row <= col, first, second).astype(dst.dtype)
-            dst[y, ROWS_OUT:] = jnp.where(top, diag, 0.0).astype(dst.dtype)
-
-
-def cov_out_partial(output_grads, owners, counts, core):
-    quarter = output_grads.shape[0]
-
-    def at(zh, y, other):
-        def index(s, owners, counts, core):
-            c = 1 - core[0] if other else core[0]
-            x, half = s // 2, s % 2
-            return (0, owners[((x * 2 + zh) * 4 + half * 2 + y) * 2 + c])
-
-        return pl.BlockSpec((quarter, 128), index)
-
-    rows = ROWS_OUT + ROWS_EXTRA
-    out = pl.BlockSpec((2, rows, 128), lambda s, *_: (s, 0, 0))
-    order = [(zh, y, other) for other in (False, True) for zh in range(2) for y in range(2)]
-    return pl.pallas_call(
-        cov_out_kernel,
-        grid_spec=pltpu.PrefetchScalarGridSpec(
-            num_scalar_prefetch=3,
-            grid=(8,),
-            in_specs=[at(*o) for o in order],
-            out_specs=[out, out],
-        ),
-        out_shape=[
-            jax.ShapeDtypeStruct((16, rows, 128), bf16),
-            jax.ShapeDtypeStruct((16, rows, 128), f32),
-        ],
-        compiler_params=pltpu.CompilerParams(vmem_limit_bytes=VMEM),
-        cost_estimate=pl.CostEstimate(
-            flops=2 * quarter * 8192 * 128, bytes_accessed=quarter * 8192 * 2 + (4 << 20), transcendentals=0
-        ),
-        name="cov_out_partial",
-    )(owners, counts, core, *([output_grads] * 8))
-
-
-def cov_in_kernel(counts, lhs, rhs, send, keep):
+            dst[s, 0:ROWS_OUT] = jnp.where(row <= col, first, second).astype(dst.dtype)
+            dst[s, ROWS_OUT:] = jnp.where(top, diag, 0.0).astype(dst.dtype)
+        return 0
+
+    lax.fori_loop(0, 16, step, 0, unroll=2)
+
+
+def cov_in_kernel(counts, tokens, send, keep):
     dp, core, _ = counted()
     first = core == 0
-    rows = lax.broadcasted_iota(jnp.int32, lhs.shape, 0) < counts[dp]
-    masked = jnp.where(rows, lhs[...], jnp.zeros((), bf16))
-    part = dot(masked, rhs[...], 0, 0)
-    for zh in range(2):
-        for y in range(4):
-            at = (zh * 4 + y) * 32
-            low, high = part[at : at + 16], part[at + 16 : at + 32]
-            for dst, rows in (
-                (keep, jnp.where(first, low, high)),
-                (send, jnp.where(first, high, low).astype(bf16)),
-            ):
-                for c in range(8):
-                    at = c * 32 + zh * 16
-                    dst[y, at : at + 16] = rows[:, c * 128 : c * 128 + 128]
-
-
-def cov_in_partial(activations, counts):
-    tok = activations.shape[0]
-    out = pl.BlockSpec((4, ROWS_IN, 128), lambda s, *_: (s, 0, 0))
-    return pl.pallas_call(
-        cov_in_kernel,
-        grid_spec=pltpu.PrefetchScalarGridSpec(
-            num_scalar_prefetch=1,
-            grid=(4,),
-            in_specs=[
-                pl.BlockSpec((tok, 256), lambda s, *_: (0, s)),
-                pl.BlockSpec((tok, 1024), lambda s, *_: (0, 0)),
-            ],
-            out_specs=[out, out],
-        ),
-        out_shape=[
-            jax.ShapeDtypeStruct((16, ROWS_IN, 128), bf16),
-            jax.ShapeDtypeStruct((16, ROWS_IN, 128), f32),
-        ],
-        compiler_params=pltpu.CompilerParams(vmem_limit_bytes=VMEM),
-        cost_estimate=pl.CostEstimate(
-            flops=2 * tok * 1024 * 1024, bytes_accessed=tok * 4096 + (4 << 20), transcendentals=0
-        ),
-        name="cov_in_partial",
-    )(counts, activations, activations)
+    live = lax.broadcasted_iota(jnp.int32, (tokens.shape[0], 256), 0) < counts[dp]
+    for x in range(4):
+        some = jnp.where(live, tokens[:, x * 256 : x * 256 + 256], jnp.zeros((), bf16))
+        part = dot(some, tokens[...], 0, 0)
+        for zh in range(2):
+            for y in range(4):
+                at = (zh * 4 + y) * 32
+                low, high = part[at : at + 16], part[at + 16 : at + 32]
+                to = slice(zh * 16, zh * 16 + 16)
+                keep[x * 4 + y, to] = jnp.where(first, low, high)
+                send[x * 4 + y, to] = jnp.where(first, high, low).astype(bf16)
 
 
 def pack_in_kernel(keep, recv, msg):
@@ -229,11 +171,10 @@
 
 def unpack_in_kernel(msg, keep, send):
     first = lax.axis_index("zh") == 0
-    for c in range(8):
-        pair = total(msg, c * 32, 32)
-        low, high = pair[:16], pair[16:]
-        keep[:, c * 128 : c * 128 + 128] = jnp.where(first, low, high)
-        send[:, c * 128 : c * 128 + 128] = jnp.where(first, high, low)
+    pair = total(msg, 0, 32)
+    low, high = pair[:16], pair[16:]
+    keep[...] = jnp.where(first, low, high)
+    send[...] = jnp.where(first, high, low)
 
 
 def unpack_out_kernel(msg, column):
@@ -270,18 +211,28 @@
 ):
     token_total = jnp.sum(token_counts).astype(f32)
     shape = jax.ShapeDtypeStruct
-    core = lax.axis_index("core").astype(jnp.int32)[None]
     mine = basis_in[0]
     slabs = jnp.concatenate([mine, swap(mine, "zh")], axis=0)
-    send_in, keep_in = cov_in_partial(activations, token_counts)
+    rows = (16, 32, 1024)
+    send_in, keep_in = on_chip(
+        cov_in_kernel, [shape(rows, bf16), shape(rows, f32)], 2 << 30, token_counts, activations
+    )
     slabs, send_in, counts = lax.optimization_barrier((slabs, send_in, token_counts))
     recv_in = swap(send_in, "core")
     q_own = lax.all_to_all(
         jnp.broadcast_to(slabs[None], (16,) + slabs.shape), PLANE, 0, 0, tiled=True
     )
-    send_out, keep_out = cov_out_partial(output_grads, owner_blocks, counts, core)
+    folded = (16, ROWS_OUT + ROWS_EXTRA, 128)
+    send_out, keep_out = on_chip(
+        cov_out_kernel,
+        [shape(folded, bf16), shape(folded, f32)],
+        1 << 30,
+        owner_blocks,
+        counts,
+        output_grads,
+    )
     recv_out = swap(send_out, "core")
-    (msg_in,) = on_chip(pack_in_kernel, [shape((16, ROWS_IN, 128), bf16)], 1024, keep_in, recv_in)
+    (msg_in,) = on_chip(pack_in_kernel, [shape(rows, bf16)], 1024, keep_in, recv_in)
     q_own, msg_in, keep_out = lax.optimization_barrier((q_own, msg_in, keep_out))
     got_in = lax.all_to_all(msg_in, PLANE, 0, 0, tiled=True)
     q_other = swap(q_own, "core")
@@ -297,14 +248,16 @@
         values_in[None, :],
         values_out[:, None],
     )
+    (precond,) = on_chip(finish_kernel, [shape((1024, 128), f32)], 1024, q_own, q_other, back)
+    other_inner, precond = lax.optimization_barrier((swap(inner, "core"), precond))
     (msg_out,) = on_chip(
         pack_out_kernel,
-        [shape((16, ROWS_OUT + ROWS_EXTRA, 128), bf16)],
+        [shape(folded, bf16)],
         1024,
         keep_out,
         recv_out,
         inner,
-        swap(inner, "core"),
+        other_inner,
     )
     got_in, msg_out = lax.optimization_barrier((got_in, msg_out))
     got_out = lax.all_to_all(msg_out, PLANE, 0, 0, tiled=True)
@@ -313,7 +266,6 @@
     (column,) = on_chip(unpack_out_kernel, [shape((8, 40, 128), f32)], 1024, got_out)
     column, recv_slab = lax.optimization_barrier((column, recv_slab))
     column = lax.all_to_all(column, COLUMN, 0, 0, tiled=True)
-    (precond,) = on_chip(finish_kernel, [shape((1024, 128), f32)], 1024, q_own, q_other, back)
     cov_in = ((keep_slab + recv_slab) / token_total)[None]
     cov_out, update = on_chip(
         clip_kernel,

time: 97.1 us -> 93.3 us (0.961)
  local copies, waits for them, and re-layouts: 10.5 us -> 8.33 us
  Pallas kernels: 18.2 us -> 16.3 us
    pallas_call x2 -> x0, Pallas kernels: 10.4 us -> none  [the longest x1 5.73 us: cov_out_partial(): pl.pallas_call(cov_out_kernel, grid_spec=pltpu.PrefetchScalarGridSpec(num...]
    pallas_call x8 -> x10, Pallas kernels: 7.77 us -> 16.3 us  [on_chip(): pl.pallas_call(kernel, in_specs=[whole if a.ndim > 1 else pl.BlockSpec(me...]
    unnamed x36 -> x30, local copies, waits for them, and re-layouts: 9.23 us -> 7.09 us
    all_to_all x1, waiting for transfers between devices: 8.76 us -> 7.23 us  [local(): got_out = lax.all_to_all(msg_out, PLANE, 0, 0, tiled=True)]
    ppermute x6, starting transfers between devices: 11.3 us -> 12.8 us  [swap(): return lax.ppermute(array, axis, [(0, 1), (1, 0)])]
  transfers between devices with their start and end apart: 10 -> 10, of which waited for: 5 -> 4; matrix products, arithmetic and copies ran while one was open for 3% -> 3% of each run, Pallas kernels for 17% -> 16%
where the time goes in v7:
time: 93.3 us; the launch traced here: 92.2 us
  waiting for transfers between devices  33.9 us (36%)
  starting transfers between devices  30.2 us (32%)
  Pallas kernels  16.3 us (17%)
  local copies, waits for them, and re-layouts  8.33 us (9%)
  between operations  2.11 us (2%)
  other arithmetic  1.36 us (1%)
    pallas_call x10, Pallas kernels, on_chip(): pl.pallas_call(kernel, in_specs=[whole if a.ndim > 1 else pl.BlockSpec(me...  16.3 us
    ppermute x6, starting transfers between devices, swap(): return lax.ppermute(array, axis, [(0, 1), (1, 0)])  12.8 us
    all_to_all x1, waiting for transfers between devices, local(): got_in = lax.all_to_all(msg_in, PLANE, 0, 0, tiled=True)  12.3 us
    all_to_all x1, waiting for transfers between devices, local(): column = lax.all_to_all(column, COLUMN, 0, 0, tiled=True)  7.49 us
    all_to_all x1, waiting for transfers between devices, local(): got_out = lax.all_to_all(msg_out, PLANE, 0, 0, tiled=True)  7.23 us
    unnamed x30, local copies, waits for them, and re-layouts  7.09 us
    all_to_all x1, waiting for transfers between devices, local(): lax.all_to_all(jnp.broadcast_to(slabs[None], (16,) + slabs.shape), PLANE,...  6.84 us
    all_to_all x1, starting transfers between devices, local(): lax.all_to_all(jnp.broadcast_to(slabs[None], (16,) + slabs.shape), PLANE,...  6.75 us
  transfers between devices with their start and end apart: 10, of which 4 were waited for; matrix products, arithmetic and copies ran while one was open for 3% of the time, Pallas kernels for 16%

profile of v7, /device:TPU:1, one launch (start us, length us, event | category | flops | bytes accessed | tf_op | source)
XLA Modules:
  0.0 92.2 jit_solution(18370351019663663233)
XLA Ops:
  0.6 7.8 %collective-permute-start = (bf16[16,1024]{1,0:T(8,128)(2,1)}, bf16[16,1024]{1,0:T(8,128)(2,1)S(1)}, u32[]{:S(2)}, u32[]{:S(2)}) collective-permute-start(bf16[16,1024]{1,0:T(8,128)(2,1)} %bitcast.9), channel_id=1, source_target_pairs={{0,32},{32,0},{1,33},{33,1},{2,34},{34,2},{3,35},{35,3},{4,36},{36... | collective-permute-start | bytes 98312 | tf_op jit(solution)/shard_map/ppermute | solution.py:197
  9.1 1.6 %copy-done.11 = bf16[1024,1024]{1,0:T(8,128)(2,1)S(1)} copy-done((bf16[1024,1024]{1,0:T(8,128)(2,1)S(1)}, bf16[1024,1024]{1,0:T(8,128)(2,1)}, u32[]{:S(2)}) %copy-start.11) | copy-done | bytes 2097176
  10.7 4.0 %cov_in.1 = (bf16[16,32,1024]{2,1,0:T(8,128)(2,1)}, f32[16,32,1024]{2,1,0:T(8,128)S(1)}) custom-call(s32[64]{0:T(128)S(1)} %copy-done.9, bf16[1024,1024]{1,0:T(8,128)(2,1)S(1)} %copy-done.11), custom_call_target="tpu_custom_call" | custom-call | flops 2147483648 | bytes 2097408 | tf_op jit(solution)/shard_map/cov_in/pallas_call | solution.py:154
  14.7 1.0 %collective-permute-start.1 = (bf16[16,32,1024]{2,1,0:T(8,128)(2,1)}, bf16[16,32,1024]{2,1,0:T(8,128)(2,1)}, u32[]{:S(2)}, u32[]{:S(2)}) collective-permute-start(bf16[16,32,1024]{2,1,0:T(8,128)(2,1)} %get-tuple-element.28), channel_id=1, source_target_pairs={{0,4},{4,0},{1,5},{5,1},{2,6},{6,2},{3,7},{7,3},{8,12},{12,8},{9,1... | collective-permute-start | bytes 3145736 | tf_op jit(solution)/shard_map/ppermute | solution.py:197
  15.8 1.1 %broadcast_in_dim.15 = bf16[16,32,1024]{2,1,0:T(8,128)(2,1)} broadcast(bf16[32,1024]{1,0:T(8,128)(2,1)S(1)} %pad_maximum_fusion), dimensions={1,2} | broadcast | bytes 1114112 | tf_op jit(solution)/shard_map/broadcast_in_dim | solution.py:223
  16.9 6.8 %all-to-all-start = ((bf16[16,32,1024]{2,1,0:T(8,128)(2,1)}), bf16[16,32,1024]{2,1,0:T(8,128)(2,1)S(1)}, u32[]{:S(2)}, u32[]{:S(2)}) async-start(bf16[16,32,1024]{2,1,0:T(8,128)(2,1)} %broadcast_in_dim.15), calls=%async_computation | async-start | bytes 2097152 | tf_op jit(solution)/shard_map/all_to_all | solution.py:222
  23.7 2.2 %copy-done = bf16[256,8192]{1,0:T(8,128)(2,1)S(1)} copy-done((bf16[256,8192]{1,0:T(8,128)(2,1)S(1)}, bf16[256,8192]{1,0:T(8,128)(2,1)}, u32[]{:S(2)}) %copy-start) | copy-done | bytes 4194328
  25.9 3.6 %cov_out.1 = (bf16[16,144,128]{2,1,0:T(8,128)(2,1)S(1)}, f32[16,144,128]{2,1,0:T(8,128)S(1)}) custom-call(s32[64]{0:T(128)S(1)} %copy-done.8, s32[64]{0:T(128)S(1)} %copy-done.10, bf16[256,8192]{1,0:T(8,128)(2,1)S(1)} %copy-done), custom_call_target="tpu_custom_call" | custom-call | flops 1073741824 | bytes 4194816 | tf_op jit(solution)/shard_map/cov_out/pallas_call | solution.py:154
  29.5 1.0 %copy-done.3 = f32[16,144,128]{2,1,0:T(8,128)} copy-done((f32[16,144,128]{2,1,0:T(8,128)}, f32[16,144,128]{2,1,0:T(8,128)S(1)}, u32[]{:S(2)}) %copy-start.3) | copy-done | bytes 1179672
  30.5 0.8 copy-done.12
  31.3 2.4 %pack_in.1 = bf16[16,32,1024]{2,1,0:T(8,128)(2,1)} custom-call(f32[16,32,1024]{2,1,0:T(8,128)S(1)} %get-tuple-element.27.keep, bf16[16,32,1024]{2,1,0:T(8,128)(2,1)} %collective-permute-done.1.recv), custom_call_target="tpu_custom_call" | custom-call | flops 1024 | bytes 3145728 | tf_op jit(solution)/shard_map/pack_in/pallas_call | solution.py:154
  33.8 6.8 %all-to-all-done.slabs.q_own = bf16[16,32,1024]{2,1,0:T(8,128)(2,1)S(1)} async-done(((bf16[16,32,1024]{2,1,0:T(8,128)(2,1)}), bf16[16,32,1024]{2,1,0:T(8,128)(2,1)S(1)}, u32[]{:S(2)}, u32[]{:S(2)}) %all-to-all-start) | async-done | bytes 1048608 | tf_op jit(solution)/shard_map/all_to_all | solution.py:222
  40.6 1.8 %collective-permute-start.3 = (bf16[16,32,1024]{2,1,0:T(8,128)(2,1)S(1)}, bf16[16,32,1024]{2,1,0:T(8,128)(2,1)S(1)}, u32[]{:S(2)}, u32[]{:S(2)}) collective-permute-start(bf16[16,32,1024]{2,1,0:T(8,128)(2,1)S(1)} %all-to-all-done.slabs.q_own), channel_id=1, source_target_pairs={{0,4},{4,0},{1,5},{5,1},{2,6},{6,2},{3,7},{7,3},{8,12},{12,8},{9,1... | collective-permute-start | bytes 3145736 | tf_op jit(solution)/shard_map/ppermute | solution.py:197
  42.4 3.7 %all-to-all-start.1 = ((bf16[16,32,1024]{2,1,0:T(8,128)(2,1)}), bf16[16,32,1024]{2,1,0:T(8,128)(2,1)S(1)}, u32[]{:S(2)}, u32[]{:S(2)}) async-start(bf16[16,32,1024]{2,1,0:T(8,128)(2,1)} %pack_in.1), calls=%async_computation.1 | async-start | bytes 2097152 | tf_op jit(solution)/shard_map/all_to_all | solution.py:237
  46.7 0.8 scale.1
  49.5 2.1 %pack_out.1 = bf16[16,144,128]{2,1,0:T(8,128)(2,1)} custom-call(f32[16,144,128]{2,1,0:T(8,128)S(1)} %copy-done.4, bf16[16,144,128]{2,1,0:T(8,128)(2,1)} %collective-permute-done.2.recv, f32[8,128]{1,0:T(8,128)S(1)} %get-tuple-element.35.inner, f32[8,128]{1,0:T(8,128)S(1)} %collective-permute-done.4.other_inner), custom_call_target="tpu_custom_call" | custom-call | flops 1024 | bytes 1777664 | tf_op jit(solution)/shard_map/pack_out/pallas_call | solution.py:154
  51.6 12.3 %all-to-all-done.1.msg = bf16[16,32,1024]{2,1,0:T(8,128)(2,1)S(1)} async-done(((bf16[16,32,1024]{2,1,0:T(8,128)(2,1)}), bf16[16,32,1024]{2,1,0:T(8,128)(2,1)S(1)}, u32[]{:S(2)}, u32[]{:S(2)}) %all-to-all-start.1) | async-done | bytes 1048608 | tf_op jit(solution)/shard_map/all_to_all | solution.py:237
  63.9 3.6 %all-to-all-start.2 = ((bf16[16,144,128]{2,1,0:T(8,128)(2,1)}), bf16[16,144,128]{2,1,0:T(8,128)(2,1)S(1)}, u32[]{:S(2)}, u32[]{:S(2)}) async-start(bf16[16,144,128]{2,1,0:T(8,128)(2,1)} %pack_out.1), calls=%async_computation.2 | async-start | bytes 1179648 | tf_op jit(solution)/shard_map/all_to_all | solution.py:263
  67.7 1.6 %collective-permute-start.5 = (f32[16,1024]{1,0:T(8,128)S(1)}, f32[16,1024]{1,0:T(8,128)S(1)}, u32[]{:S(2)}, u32[]{:S(2)}) collective-permute-start(f32[16,1024]{1,0:T(8,128)S(1)} %get-tuple-element.41), channel_id=1, source_target_pairs={{0,32},{32,0},{1,33},{33,1},{2,34},{34,2},{3,35},{35,3},{4,36},{36... | collective-permute-start | bytes 196616 | tf_op jit(solution)/shard_map/ppermute | solution.py:197
  71.2 7.2 %all-to-all-done.2.msg = bf16[16,144,128]{2,1,0:T(8,128)(2,1)S(1)} async-done(((bf16[16,144,128]{2,1,0:T(8,128)(2,1)}), bf16[16,144,128]{2,1,0:T(8,128)(2,1)S(1)}, u32[]{:S(2)}, u32[]{:S(2)}) %all-to-all-start.2) | async-done | bytes 589856 | tf_op jit(solution)/shard_map/all_to_all | solution.py:263
  78.4 0.8 unpack_out.1
  79.2 3.4 %all-to-all-start.3 = ((f32[8,40,128]{2,1,0:T(8,128)}), f32[8,40,128]{2,1,0:T(8,128)S(1)}, u32[]{:S(2)}, u32[]{:S(2)}) async-start(f32[8,40,128]{2,1,0:T(8,128)} %unpack_out.1), calls=%async_computation.3 | async-start | bytes 327680 | tf_op jit(solution)/shard_map/all_to_all | solution.py:268
  83.3 7.5 %all-to-all-done.3.column = f32[8,40,128]{2,1,0:T(8,128)S(1)} async-done(((f32[8,40,128]{2,1,0:T(8,128)}), f32[8,40,128]{2,1,0:T(8,128)S(1)}, u32[]{:S(2)}, u32[]{:S(2)}) %all-to-all-start.3) | async-done | bytes 163872 | tf_op jit(solution)/shard_map/all_to_all | solution.py:268
  90.8 1.4 %clip.1 = (f32[1,32,128]{2,1,0:T(8,128)}, f32[1024,128]{1,0:T(8,128)}) custom-call(f32[2]{0:T(128)S(1)} %pad_maximum_fusion.1.scalars, f32[8,40,128]{2,1,0:T(8,128)S(1)} %all-to-all-done.3.column, f32[1024,128]{1,0:T(8,128)S(1)} %copy-done.2), custom_call_target="tpu_custom_call" | custom-call | flops 1048576 | bytes 688136 | tf_op jit(solution)/shard_map/clip/pallas_call | solution.py:154
  (42 shorter events, 4.8 us)
Async XLA Ops:
  0.6 14.1 %collective-permute-start = (bf16[16,1024]{1,0:T(8,128)(2,1)}, bf16[16,1024]{1,0:T(8,128)(2,1)S(1)}, u32[]{:S(2)}, u32[]{:S(2)}) collective-permute-start(bf16[16,1024]{1,0:T(8,128)(2,1)} %bitcast.9), channel_id=1, source_target_pairs={{0,32},{32,0},{1,33},{33,1},{2,34},{34,2},{3,35},{35,3},{4,36},{36... | collective-permute-start | bytes 98312 | tf_op jit(solution)/shard_map/ppermute | solution.py:197
  9.1 1.6 %copy-start.11 = (bf16[1024,1024]{1,0:T(8,128)(2,1)S(1)}, bf16[1024,1024]{1,0:T(8,128)(2,1)}, u32[]{:S(2)}) copy-start(bf16[1024,1024]{1,0:T(8,128)(2,1)} %tokens.2) | copy-start | bytes 6291460
  10.7 4.0 %copy-start.13 = (bf16[1,16,1024]{2,1,0:T(8,128)(2,1)S(1)}, bf16[1,16,1024]{2,1,0:T(8,128)(2,1)}, u32[]{:S(2)}) copy-start(bf16[1,16,1024]{2,1,0:T(8,128)(2,1)} %param.14) | copy-start | bytes 98308
  14.7 9.0 %copy-start.8 = (s32[64]{0:T(128)S(1)}, s32[64]{0:T(128)}, u32[]{:S(2)}) copy-start(s32[64]{0:T(128)} %owners.1) | copy-start | bytes 772
  14.7 9.0 %copy-start.10 = (s32[64]{0:T(128)S(1)}, s32[64]{0:T(128)}, u32[]{:S(2)}) copy-start(s32[64]{0:T(128)} %counts.2) | copy-start | bytes 772
  14.7 16.6 %collective-permute-start.1 = (bf16[16,32,1024]{2,1,0:T(8,128)(2,1)}, bf16[16,32,1024]{2,1,0:T(8,128)(2,1)}, u32[]{:S(2)}, u32[]{:S(2)}) collective-permute-start(bf16[16,32,1024]{2,1,0:T(8,128)(2,1)} %get-tuple-element.28), channel_id=1, source_target_pairs={{0,4},{4,0},{1,5},{5,1},{2,6},{6,2},{3,7},{7,3},{8,12},{12,8},{9,1... | collective-permute-start | bytes 3145736 | tf_op jit(solution)/shard_map/ppermute | solution.py:197
  16.9 23.7 %all-to-all-start = ((bf16[16,32,1024]{2,1,0:T(8,128)(2,1)}), bf16[16,32,1024]{2,1,0:T(8,128)(2,1)S(1)}, u32[]{:S(2)}, u32[]{:S(2)}) async-start(bf16[16,32,1024]{2,1,0:T(8,128)(2,1)} %broadcast_in_dim.15), calls=%async_computation | async-start | bytes 2097152 | tf_op jit(solution)/shard_map/all_to_all | solution.py:222
  23.7 2.2 %copy-start = (bf16[256,8192]{1,0:T(8,128)(2,1)S(1)}, bf16[256,8192]{1,0:T(8,128)(2,1)}, u32[]{:S(2)}) copy-start(bf16[256,8192]{1,0:T(8,128)(2,1)} %tokens.3) | copy-start | bytes 12582916
  29.5 1.0 %copy-start.3 = (f32[16,144,128]{2,1,0:T(8,128)}, f32[16,144,128]{2,1,0:T(8,128)S(1)}, u32[]{:S(2)}) copy-start(f32[16,144,128]{2,1,0:T(8,128)S(1)} %get-tuple-element.32.keep) | copy-start | bytes 3538948
  30.5 0.8 copy-start.12
  33.8 12.4 %copy-start.14 = (f32[128]{0:T(128)S(1)}, f32[128]{0:T(128)}, u32[]{:S(2)}) copy-start(f32[128]{0:T(128)} %param.17) | copy-start | bytes 1540
  33.8 12.5 %copy-start.5 = (bf16[1024,128]{1,0:T(8,128)(2,1)S(1)}, bf16[1024,128]{1,0:T(8,128)(2,1)}, u32[]{:S(2)}) copy-start(bf16[1024,128]{1,0:T(8,128)(2,1)} %grad.3) | copy-start | bytes 786436
  33.8 12.9 %copy-start.6 = (bf16[1,128,128]{2,1,0:T(8,128)(2,1)S(1)}, bf16[1,128,128]{2,1,0:T(8,128)(2,1)}, u32[]{:S(2)}) copy-start(bf16[1,128,128]{2,1,0:T(8,128)(2,1)} %param.15) | copy-start | bytes 98308
  33.8 12.9 %copy-start.7 = (f32[1024]{0:T(1024)S(1)}, f32[1024]{0:T(1024)}, u32[]{:S(2)}) copy-start(f32[1024]{0:T(1024)} %param.16) | copy-start | bytes 12292
  40.6 6.0 %collective-permute-start.3 = (bf16[16,32,1024]{2,1,0:T(8,128)(2,1)S(1)}, bf16[16,32,1024]{2,1,0:T(8,128)(2,1)S(1)}, u32[]{:S(2)}, u32[]{:S(2)}) collective-permute-start(bf16[16,32,1024]{2,1,0:T(8,128)(2,1)S(1)} %all-to-all-done.slabs.q_own), channel_id=1, source_target_pairs={{0,4},{4,0},{1,5},{5,1},{2,6},{6,2},{3,7},{7,3},{8,12},{12,8},{9,1... | collective-permute-start | bytes 3145736 | tf_op jit(solution)/shard_map/ppermute | solution.py:197
  42.4 21.5 %all-to-all-start.1 = ((bf16[16,32,1024]{2,1,0:T(8,128)(2,1)}), bf16[16,32,1024]{2,1,0:T(8,128)(2,1)S(1)}, u32[]{:S(2)}, u32[]{:S(2)}) async-start(bf16[16,32,1024]{2,1,0:T(8,128)(2,1)} %pack_in.1), calls=%async_computation.1 | async-start | bytes 2097152 | tf_op jit(solution)/shard_map/all_to_all | solution.py:237
  46.1 3.4 %collective-permute-start.2 = (bf16[16,144,128]{2,1,0:T(8,128)(2,1)}, bf16[16,144,128]{2,1,0:T(8,128)(2,1)}, u32[]{:S(2)}, u32[]{:S(2)}) collective-permute-start(bf16[16,144,128]{2,1,0:T(8,128)(2,1)} %copy-done.12), channel_id=1, source_target_pairs={{0,4},{4,0},{1,5},{5,1},{2,6},{6,2},{3,7},{7,3},{8,12},{12,8},{9,1... | collective-permute-start | bytes 1769480 | tf_op jit(solution)/shard_map/ppermute | solution.py:197
  46.7 2.8 %copy-start.4 = (f32[16,144,128]{2,1,0:T(8,128)S(1)}, f32[16,144,128]{2,1,0:T(8,128)}, u32[]{:S(2)}) copy-start(f32[16,144,128]{2,1,0:T(8,128)} %copy-done.3) | copy-start | bytes 3538948
  47.5 2.0 %collective-permute-start.4 = (f32[8,128]{1,0:T(8,128)S(1)}, f32[8,128]{1,0:T(8,128)S(1)}, u32[]{:S(2)}, u32[]{:S(2)}) collective-permute-start(f32[8,128]{1,0:T(8,128)S(1)} %get-tuple-element.35.inner), channel_id=1, source_target_pairs={{0,4},{4,0},{1,5},{5,1},{2,6},{6,2},{3,7},{7,3},{8,12},{12,8},{9,1... | collective-permute-start | bytes 12296 | tf_op jit(solution)/shard_map/ppermute | solution.py:197
  48.7 0.8 copy-start.1
  51.6 39.2 %copy-start.2 = (f32[1024,128]{1,0:T(8,128)S(1)}, f32[1024,128]{1,0:T(8,128)}, u32[]{:S(2)}) copy-start(f32[1024,128]{1,0:T(8,128)} %copy-done.1) | copy-start | bytes 1572868
  63.9 14.5 %all-to-all-start.2 = ((bf16[16,144,128]{2,1,0:T(8,128)(2,1)}), bf16[16,144,128]{2,1,0:T(8,128)(2,1)S(1)}, u32[]{:S(2)}, u32[]{:S(2)}) async-start(bf16[16,144,128]{2,1,0:T(8,128)(2,1)} %pack_out.1), calls=%async_computation.2 | async-start | bytes 1179648 | tf_op jit(solution)/shard_map/all_to_all | solution.py:263
  67.7 11.6 %collective-permute-start.5 = (f32[16,1024]{1,0:T(8,128)S(1)}, f32[16,1024]{1,0:T(8,128)S(1)}, u32[]{:S(2)}, u32[]{:S(2)}) collective-permute-start(f32[16,1024]{1,0:T(8,128)S(1)} %get-tuple-element.41), channel_id=1, source_target_pairs={{0,32},{32,0},{1,33},{33,1},{2,34},{34,2},{3,35},{35,3},{4,36},{36... | collective-permute-start | bytes 196616 | tf_op jit(solution)/shard_map/ppermute | solution.py:197
  79.2 11.6 %all-to-all-start.3 = ((f32[8,40,128]{2,1,0:T(8,128)}), f32[8,40,128]{2,1,0:T(8,128)S(1)}, u32[]{:S(2)}, u32[]{:S(2)}) async-start(f32[8,40,128]{2,1,0:T(8,128)} %unpack_out.1), calls=%async_computation.3 | async-start | bytes 327680 | tf_op jit(solution)/shard_map/all_to_all | solution.py:268
  (1 other events, 0.7 us)

commit v8 on v7

--- a/solution.py
+++ b/solution.py
@@ -58,12 +58,13 @@
     lax.fori_loop(0, 16, step, 0, unroll=2)
 
 
-def cov_in_kernel(counts, tokens, send, keep):
+def cov_in_rows(counts, tokens, send, keep, start):
     dp, core, _ = counted()
     first = core == 0
     live = lax.broadcasted_iota(jnp.int32, (tokens.shape[0], 256), 0) < counts[dp]
-    for x in range(4):
-        some = jnp.where(live, tokens[:, x * 256 : x * 256 + 256], jnp.zeros((), bf16))
+    for x in range(2):
+        cols = slice((start + x) * 256, (start + x) * 256 + 256)
+        some = jnp.where(live, tokens[:, cols], jnp.zeros((), bf16))
         part = dot(some, tokens[...], 0, 0)
         for zh in range(2):
             for y in range(4):
@@ -74,12 +75,21 @@
                 send[x * 4 + y, to] = jnp.where(first, high, low).astype(bf16)
 
 
-def pack_in_kernel(keep, recv, msg):
+def cov_in_first_kernel(*refs):
+    cov_in_rows(*refs, 0)
+
+
+def cov_in_second_kernel(*refs):
+    cov_in_rows(*refs, 2)
+
+
+def pack_in_kernel(keep_one, recv_one, keep_two, recv_two, msg):
     def step(s, _):
-        msg[s] = (keep[s] + recv[s].astype(f32)).astype(bf16)
+        msg[s] = (keep_one[s] + recv_one[s].astype(f32)).astype(bf16)
+        msg[8 + s] = (keep_two[s] + recv_two[s].astype(f32)).astype(bf16)
         return 0
 
-    lax.fori_loop(0, 16, step, 0)
+    lax.fori_loop(0, 8, step, 0)
 
 
 def pack_out_kernel(keep, recv, inner, other_inner, msg):
@@ -213,15 +223,15 @@
     shape = jax.ShapeDtypeStruct
     mine = basis_in[0]
     slabs = jnp.concatenate([mine, swap(mine, "zh")], axis=0)
-    rows = (16, 32, 1024)
-    send_in, keep_in = on_chip(
-        cov_in_kernel, [shape(rows, bf16), shape(rows, f32)], 2 << 30, token_counts, activations
-    )
-    slabs, send_in, counts = lax.optimization_barrier((slabs, send_in, token_counts))
-    recv_in = swap(send_in, "core")
+    half = [shape((8, 32, 1024), bf16), shape((8, 32, 1024), f32)]
+    send_one, keep_one = on_chip(cov_in_first_kernel, half, 1 << 30, token_counts, activations)
+    slabs, send_one, counts = lax.optimization_barrier((slabs, send_one, token_counts))
     q_own = lax.all_to_all(
         jnp.broadcast_to(slabs[None], (16,) + slabs.shape), PLANE, 0, 0, tiled=True
     )
+    recv_one = swap(send_one, "core")
+    send_two, keep_two = on_chip(cov_in_second_kernel, half, 1 << 30, counts, activations)
+    recv_two = swap(send_two, "core")
     folded = (16, ROWS_OUT + ROWS_EXTRA, 128)
     send_out, keep_out = on_chip(
         cov_out_kernel,
@@ -232,7 +242,15 @@
         output_grads,
     )
     recv_out = swap(send_out, "core")
-    (msg_in,) = on_chip(pack_in_kernel, [shape(rows, bf16)], 1024, keep_in, recv_in)
+    (msg_in,) = on_chip(
+        pack_in_kernel,
+        [shape((16, 32, 1024), bf16)],
+        1024,
+        keep_one,
+        recv_one,
+        keep_two,
+        recv_two,
+    )
     q_own, msg_in, keep_out = lax.optimization_barrier((q_own, msg_in, keep_out))
     got_in = lax.all_to_all(msg_in, PLANE, 0, 0, tiled=True)
     q_other = swap(q_own, "core")

time: 93.3 us -> 90.5 us (0.970)
  waiting for transfers between devices: 33.9 us -> 28.2 us
  starting transfers between devices: 30.2 us -> 32.5 us
  local copies, waits for them, and re-layouts: 8.33 us -> 9.93 us
  Pallas kernels: 16.3 us -> 14.9 us
    all_to_all x1, waiting for transfers between devices: 6.84 us -> 1.45 us  [local(): lax.all_to_all(jnp.broadcast_to(slabs[None], (16,) + slabs.shape), PLANE,...]
    ppermute x6 -> x7, starting transfers between devices: 12.8 us -> 15.1 us  [swap(): return lax.ppermute(array, axis, [(0, 1), (1, 0)])]
    unnamed x30 -> x32, local copies, waits for them, and re-layouts: 7.09 us -> 8.69 us
    pallas_call x10 -> x11, Pallas kernels: 16.3 us -> 14.9 us  [on_chip(): pl.pallas_call(kernel, in_specs=[whole if a.ndim > 1 else pl.BlockSpec(me...]
  transfers between devices with their start and end apart: 10 -> 11, of which waited for: 4 -> 4; matrix products, arithmetic and copies ran while one was open for 3% -> 2% of each run, Pallas kernels for 16% -> 15%
where the time goes in v8:
time: 90.5 us; the launch traced here: 88.9 us
  starting transfers between devices  32.5 us (36%)
  waiting for transfers between devices  28.2 us (31%)
  Pallas kernels  14.9 us (16%)
  local copies, waits for them, and re-layouts  9.93 us (11%)
  between operations  2.14 us (2%)
  other arithmetic  1.36 us (2%)
    ppermute x7, starting transfers between devices, swap(): return lax.ppermute(array, axis, [(0, 1), (1, 0)])  15.1 us
    pallas_call x11, Pallas kernels, on_chip(): pl.pallas_call(kernel, in_specs=[whole if a.ndim > 1 else pl.BlockSpec(me...  14.9 us
    all_to_all x1, waiting for transfers between devices, local(): got_in = lax.all_to_all(msg_in, PLANE, 0, 0, tiled=True)  12.3 us
    unnamed x32, local copies, waits for them, and re-layouts  8.69 us
    all_to_all x1, waiting for transfers between devices, local(): column = lax.all_to_all(column, COLUMN, 0, 0, tiled=True)  7.57 us
    all_to_all x1, waiting for transfers between devices, local(): got_out = lax.all_to_all(msg_out, PLANE, 0, 0, tiled=True)  6.79 us
    all_to_all x1, starting transfers between devices, local(): lax.all_to_all(jnp.broadcast_to(slabs[None], (16,) + slabs.shape), PLANE,...  6.76 us
    all_to_all x1, starting transfers between devices, local(): got_in = lax.all_to_all(msg_in, PLANE, 0, 0, tiled=True)  3.65 us
  transfers between devices with their start and end apart: 11, of which 4 were waited for; matrix products, arithmetic and copies ran while one was open for 2% of the time, Pallas kernels for 15%

profile of v8, /device:TPU:1, one launch (start us, length us, event | category | flops | bytes accessed | tf_op | source)
XLA Modules:
  0.0 88.9 jit_solution(15236842922107046510)
XLA Ops:
  0.6 7.8 %collective-permute-start = (bf16[16,1024]{1,0:T(8,128)(2,1)}, bf16[16,1024]{1,0:T(8,128)(2,1)S(1)}, u32[]{:S(2)}, u32[]{:S(2)}) collective-permute-start(bf16[16,1024]{1,0:T(8,128)(2,1)} %bitcast.9), channel_id=1, source_target_pairs={{0,32},{32,0},{1,33},{33,1},{2,34},{34,2},{3,35},{35,3},{4,36},{36... | collective-permute-start | bytes 98312 | tf_op jit(solution)/shard_map/ppermute | solution.py:207
  9.1 1.6 %copy-done.11 = bf16[1024,1024]{1,0:T(8,128)(2,1)S(1)} copy-done((bf16[1024,1024]{1,0:T(8,128)(2,1)S(1)}, bf16[1024,1024]{1,0:T(8,128)(2,1)}, u32[]{:S(2)}) %copy-start.11) | copy-done | bytes 2097176
  10.7 1.9 %cov_in_first.1 = (bf16[8,32,1024]{2,1,0:T(8,128)(2,1)S(1)}, f32[8,32,1024]{2,1,0:T(8,128)S(1)}) custom-call(s32[64]{0:T(128)S(1)} %copy-done.9, bf16[1024,1024]{1,0:T(8,128)(2,1)S(1)} %copy-done.11), custom_call_target="tpu_custom_call" | custom-call | flops 1073741824 | bytes 2097408 | tf_op jit(solution)/shard_map/cov_in_first/pallas_call | solution.py:164
  12.6 1.1 %broadcast_in_dim.15 = bf16[16,32,1024]{2,1,0:T(8,128)(2,1)} broadcast(bf16[32,1024]{1,0:T(8,128)(2,1)S(1)} %pad_maximum_fusion), dimensions={1,2} | broadcast | bytes 1114112 | tf_op jit(solution)/shard_map/broadcast_in_dim | solution.py:230
  13.7 6.8 %all-to-all-start = ((bf16[16,32,1024]{2,1,0:T(8,128)(2,1)}), bf16[16,32,1024]{2,1,0:T(8,128)(2,1)S(1)}, u32[]{:S(2)}, u32[]{:S(2)}) async-start(bf16[16,32,1024]{2,1,0:T(8,128)(2,1)} %broadcast_in_dim.15), calls=%async_computation | async-start | bytes 2097152 | tf_op jit(solution)/shard_map/all_to_all | solution.py:229
  20.5 1.3 %collective-permute-start.1 = (bf16[8,32,1024]{2,1,0:T(8,128)(2,1)S(1)}, bf16[8,32,1024]{2,1,0:T(8,128)(2,1)S(1)}, u32[]{:S(2)}, u32[]{:S(2)}) collective-permute-start(bf16[8,32,1024]{2,1,0:T(8,128)(2,1)S(1)} %get-tuple-element.30), channel_id=1, source_target_pairs={{0,4},{4,0},{1,5},{5,1},{2,6},{6,2},{3,7},{7,3},{8,12},{12,8},{9,1... | collective-permute-start | bytes 1572872 | tf_op jit(solution)/shard_map/ppermute | solution.py:207
  21.8 1.6 %copy-done.12 = bf16[1024,1024]{1,0:T(8,128)(2,1)S(1)} copy-done((bf16[1024,1024]{1,0:T(8,128)(2,1)S(1)}, bf16[1024,1024]{1,0:T(8,128)(2,1)}, u32[]{:S(2)}) %copy-start.12) | copy-done | bytes 2097176
  23.4 1.9 %cov_in_second.1 = (bf16[8,32,1024]{2,1,0:T(8,128)(2,1)S(1)}, f32[8,32,1024]{2,1,0:T(8,128)S(1)}) custom-call(s32[64]{0:T(128)S(1)} %copy-done.10, bf16[1024,1024]{1,0:T(8,128)(2,1)S(1)} %copy-done.12), custom_call_target="tpu_custom_call" | custom-call | flops 1073741824 | bytes 2097408 | tf_op jit(solution)/shard_map/cov_in_second/pallas_call | solution.py:164
  25.4 2.2 %copy-done = bf16[256,8192]{1,0:T(8,128)(2,1)S(1)} copy-done((bf16[256,8192]{1,0:T(8,128)(2,1)S(1)}, bf16[256,8192]{1,0:T(8,128)(2,1)}, u32[]{:S(2)}) %copy-start) | copy-done | bytes 4194328
  27.6 3.6 %cov_out.1 = (bf16[16,144,128]{2,1,0:T(8,128)(2,1)S(1)}, f32[16,144,128]{2,1,0:T(8,128)S(1)}) custom-call(s32[64]{0:T(128)S(1)} %copy-done.8, s32[64]{0:T(128)S(1)} %copy-done.10, bf16[256,8192]{1,0:T(8,128)(2,1)S(1)} %copy-done), custom_call_target="tpu_custom_call" | custom-call | flops 1073741824 | bytes 4194816 | tf_op jit(solution)/shard_map/cov_out/pallas_call | solution.py:164
  31.3 1.0 %copy-done.3 = f32[16,144,128]{2,1,0:T(8,128)} copy-done((f32[16,144,128]{2,1,0:T(8,128)}, f32[16,144,128]{2,1,0:T(8,128)S(1)}, u32[]{:S(2)}) %copy-start.3) | copy-done | bytes 1179672
  32.3 0.8 copy-done.13
  33.1 1.2 %pack_in.1 = bf16[16,32,1024]{2,1,0:T(8,128)(2,1)} custom-call(f32[8,32,1024]{2,1,0:T(8,128)S(1)} %get-tuple-element.29.keep_one, bf16[8,32,1024]{2,1,0:T(8,128)(2,1)S(1)} %collective-permute-done.1.recv_one, f32[8,32,1024]{2,1,0:T(8,128)S(1)} %get-tuple-element.32.keep_two, bf16[8,32,1024]{2,1,0:T(8,128)(2,1)S(1)} %collective-permute-done.2.recv_two), custom_call_target="tpu_custom_call" | custom-call | flops 1024 | bytes 3145728 | tf_op jit(solution)/shard_map/pack_in/pallas_call | solution.py:164
  34.3 1.4 %all-to-all-done.slabs.q_own = bf16[16,32,1024]{2,1,0:T(8,128)(2,1)S(1)} async-done(((bf16[16,32,1024]{2,1,0:T(8,128)(2,1)}), bf16[16,32,1024]{2,1,0:T(8,128)(2,1)S(1)}, u32[]{:S(2)}, u32[]{:S(2)}) %all-to-all-start) | async-done | bytes 1048608 | tf_op jit(solution)/shard_map/all_to_all | solution.py:229
  35.8 3.2 %collective-permute-start.4 = (bf16[16,32,1024]{2,1,0:T(8,128)(2,1)S(1)}, bf16[16,32,1024]{2,1,0:T(8,128)(2,1)S(1)}, u32[]{:S(2)}, u32[]{:S(2)}) collective-permute-start(bf16[16,32,1024]{2,1,0:T(8,128)(2,1)S(1)} %all-to-all-done.slabs.q_own), channel_id=1, source_target_pairs={{0,4},{4,0},{1,5},{5,1},{2,6},{6,2},{3,7},{7,3},{8,12},{12,8},{9,1... | collective-permute-start | bytes 3145736 | tf_op jit(solution)/shard_map/ppermute | solution.py:207
  39.0 3.7 %all-to-all-start.1 = ((bf16[16,32,1024]{2,1,0:T(8,128)(2,1)}), bf16[16,32,1024]{2,1,0:T(8,128)(2,1)S(1)}, u32[]{:S(2)}, u32[]{:S(2)}) async-start(bf16[16,32,1024]{2,1,0:T(8,128)(2,1)} %pack_in.1), calls=%async_computation.1 | async-start | bytes 2097152 | tf_op jit(solution)/shard_map/all_to_all | solution.py:255
  46.1 2.1 %pack_out.1 = bf16[16,144,128]{2,1,0:T(8,128)(2,1)} custom-call(f32[16,144,128]{2,1,0:T(8,128)S(1)} %copy-done.4, bf16[16,144,128]{2,1,0:T(8,128)(2,1)} %collective-permute-done.3.recv, f32[8,128]{1,0:T(8,128)S(1)} %get-tuple-element.39.inner, f32[8,128]{1,0:T(8,128)S(1)} %collective-permute-done.5.other_inner), custom_call_target="tpu_custom_call" | custom-call | flops 1024 | bytes 1777664 | tf_op jit(solution)/shard_map/pack_out/pallas_call | solution.py:164
  48.2 12.3 %all-to-all-done.1.msg = bf16[16,32,1024]{2,1,0:T(8,128)(2,1)S(1)} async-done(((bf16[16,32,1024]{2,1,0:T(8,128)(2,1)}), bf16[16,32,1024]{2,1,0:T(8,128)(2,1)S(1)}, u32[]{:S(2)}, u32[]{:S(2)}) %all-to-all-start.1) | async-done | bytes 1048608 | tf_op jit(solution)/shard_map/all_to_all | solution.py:255
  60.5 3.6 %all-to-all-start.2 = ((bf16[16,144,128]{2,1,0:T(8,128)(2,1)}), bf16[16,144,128]{2,1,0:T(8,128)(2,1)S(1)}, u32[]{:S(2)}, u32[]{:S(2)}) async-start(bf16[16,144,128]{2,1,0:T(8,128)(2,1)} %pack_out.1), calls=%async_computation.2 | async-start | bytes 1179648 | tf_op jit(solution)/shard_map/all_to_all | solution.py:281
  64.3 2.0 %collective-permute-start.6 = (f32[16,1024]{1,0:T(8,128)S(1)}, f32[16,1024]{1,0:T(8,128)S(1)}, u32[]{:S(2)}, u32[]{:S(2)}) collective-permute-start(f32[16,1024]{1,0:T(8,128)S(1)} %get-tuple-element.45), channel_id=1, source_target_pairs={{0,32},{32,0},{1,33},{33,1},{2,34},{34,2},{3,35},{35,3},{4,36},{36... | collective-permute-start | bytes 196616 | tf_op jit(solution)/shard_map/ppermute | solution.py:207
  68.2 6.8 %all-to-all-done.2.msg = bf16[16,144,128]{2,1,0:T(8,128)(2,1)S(1)} async-done(((bf16[16,144,128]{2,1,0:T(8,128)(2,1)}), bf16[16,144,128]{2,1,0:T(8,128)(2,1)S(1)}, u32[]{:S(2)}, u32[]{:S(2)}) %all-to-all-start.2) | async-done | bytes 589856 | tf_op jit(solution)/shard_map/all_to_all | solution.py:281
  75.8 3.4 %all-to-all-start.3 = ((f32[8,40,128]{2,1,0:T(8,128)}), f32[8,40,128]{2,1,0:T(8,128)S(1)}, u32[]{:S(2)}, u32[]{:S(2)}) async-start(f32[8,40,128]{2,1,0:T(8,128)} %unpack_out.1), calls=%async_computation.3 | async-start | bytes 327680 | tf_op jit(solution)/shard_map/all_to_all | solution.py:286
  79.9 7.6 %all-to-all-done.3.column = f32[8,40,128]{2,1,0:T(8,128)S(1)} async-done(((f32[8,40,128]{2,1,0:T(8,128)}), f32[8,40,128]{2,1,0:T(8,128)S(1)}, u32[]{:S(2)}, u32[]{:S(2)}) %all-to-all-start.3) | async-done | bytes 163872 | tf_op jit(solution)/shard_map/all_to_all | solution.py:286
  87.5 1.4 %clip.1 = (f32[1,32,128]{2,1,0:T(8,128)}, f32[1024,128]{1,0:T(8,128)}) custom-call(f32[2]{0:T(128)S(1)} %pad_maximum_fusion.1.scalars, f32[8,40,128]{2,1,0:T(8,128)S(1)} %all-to-all-done.3.column, f32[1024,128]{1,0:T(8,128)S(1)} %copy-done.2), custom_call_target="tpu_custom_call" | custom-call | flops 1048576 | bytes 688136 | tf_op jit(solution)/shard_map/clip/pallas_call | solution.py:164
  (47 shorter events, 6.5 us)
Async XLA Ops:
  0.6 12.0 %collective-permute-start = (bf16[16,1024]{1,0:T(8,128)(2,1)}, bf16[16,1024]{1,0:T(8,128)(2,1)S(1)}, u32[]{:S(2)}, u32[]{:S(2)}) collective-permute-start(bf16[16,1024]{1,0:T(8,128)(2,1)} %bitcast.9), channel_id=1, source_target_pairs={{0,32},{32,0},{1,33},{33,1},{2,34},{34,2},{3,35},{35,3},{4,36},{36... | collective-permute-start | bytes 98312 | tf_op jit(solution)/shard_map/ppermute | solution.py:207
  9.1 1.6 %copy-start.11 = (bf16[1024,1024]{1,0:T(8,128)(2,1)S(1)}, bf16[1024,1024]{1,0:T(8,128)(2,1)}, u32[]{:S(2)}) copy-start(bf16[1024,1024]{1,0:T(8,128)(2,1)} %refs_1_.3) | copy-start | bytes 6291460
  10.7 1.9 %copy-start.14 = (bf16[1,16,1024]{2,1,0:T(8,128)(2,1)S(1)}, bf16[1,16,1024]{2,1,0:T(8,128)(2,1)}, u32[]{:S(2)}) copy-start(bf16[1,16,1024]{2,1,0:T(8,128)(2,1)} %param.14) | copy-start | bytes 98308
  12.6 9.3 %copy-start.10 = (s32[64]{0:T(128)S(1)}, s32[64]{0:T(128)}, u32[]{:S(2)}) copy-start(s32[64]{0:T(128)} %counts) | copy-start | bytes 772
  13.7 22.0 %all-to-all-start = ((bf16[16,32,1024]{2,1,0:T(8,128)(2,1)}), bf16[16,32,1024]{2,1,0:T(8,128)(2,1)S(1)}, u32[]{:S(2)}, u32[]{:S(2)}) async-start(bf16[16,32,1024]{2,1,0:T(8,128)(2,1)} %broadcast_in_dim.15), calls=%async_computation | async-start | bytes 2097152 | tf_op jit(solution)/shard_map/all_to_all | solution.py:229
  20.5 4.9 %copy-start.8 = (s32[64]{0:T(128)S(1)}, s32[64]{0:T(128)}, u32[]{:S(2)}) copy-start(s32[64]{0:T(128)} %owners.1) | copy-start | bytes 772
  20.5 12.6 %collective-permute-start.1 = (bf16[8,32,1024]{2,1,0:T(8,128)(2,1)S(1)}, bf16[8,32,1024]{2,1,0:T(8,128)(2,1)S(1)}, u32[]{:S(2)}, u32[]{:S(2)}) collective-permute-start(bf16[8,32,1024]{2,1,0:T(8,128)(2,1)S(1)} %get-tuple-element.30), channel_id=1, source_target_pairs={{0,4},{4,0},{1,5},{5,1},{2,6},{6,2},{3,7},{7,3},{8,12},{12,8},{9,1... | collective-permute-start | bytes 1572872 | tf_op jit(solution)/shard_map/ppermute | solution.py:207
  21.8 1.6 %copy-start.12 = (bf16[1024,1024]{1,0:T(8,128)(2,1)S(1)}, bf16[1024,1024]{1,0:T(8,128)(2,1)}, u32[]{:S(2)}) copy-start(bf16[1024,1024]{1,0:T(8,128)(2,1)} %refs_1_.3) | copy-start | bytes 6291460
  25.3 7.8 %collective-permute-start.2 = (bf16[8,32,1024]{2,1,0:T(8,128)(2,1)S(1)}, bf16[8,32,1024]{2,1,0:T(8,128)(2,1)S(1)}, u32[]{:S(2)}, u32[]{:S(2)}) collective-permute-start(bf16[8,32,1024]{2,1,0:T(8,128)(2,1)S(1)} %get-tuple-element.33), channel_id=1, source_target_pairs={{0,4},{4,0},{1,5},{5,1},{2,6},{6,2},{3,7},{7,3},{8,12},{12,8},{9,1... | collective-permute-start | bytes 1572872 | tf_op jit(solution)/shard_map/ppermute | solution.py:207
  25.4 2.2 %copy-start = (bf16[256,8192]{1,0:T(8,128)(2,1)S(1)}, bf16[256,8192]{1,0:T(8,128)(2,1)}, u32[]{:S(2)}) copy-start(bf16[256,8192]{1,0:T(8,128)(2,1)} %tokens.1) | copy-start | bytes 12582916
  31.3 1.0 %copy-start.3 = (f32[16,144,128]{2,1,0:T(8,128)}, f32[16,144,128]{2,1,0:T(8,128)S(1)}, u32[]{:S(2)}) copy-start(f32[16,144,128]{2,1,0:T(8,128)S(1)} %get-tuple-element.36.keep) | copy-start | bytes 3538948
  34.3 8.5 %copy-start.15 = (f32[128]{0:T(128)S(1)}, f32[128]{0:T(128)}, u32[]{:S(2)}) copy-start(f32[128]{0:T(128)} %param.17) | copy-start | bytes 1540
  34.3 8.6 %copy-start.5 = (bf16[1024,128]{1,0:T(8,128)(2,1)S(1)}, bf16[1024,128]{1,0:T(8,128)(2,1)}, u32[]{:S(2)}) copy-start(bf16[1024,128]{1,0:T(8,128)(2,1)} %grad.3) | copy-start | bytes 786436
  34.3 8.9 %copy-start.6 = (bf16[1,128,128]{2,1,0:T(8,128)(2,1)S(1)}, bf16[1,128,128]{2,1,0:T(8,128)(2,1)}, u32[]{:S(2)}) copy-start(bf16[1,128,128]{2,1,0:T(8,128)(2,1)} %param.15) | copy-start | bytes 98308
  34.3 9.0 %copy-start.7 = (f32[1024]{0:T(1024)S(1)}, f32[1024]{0:T(1024)}, u32[]{:S(2)}) copy-start(f32[1024]{0:T(1024)} %param.16) | copy-start | bytes 12292
  35.8 7.5 %collective-permute-start.4 = (bf16[16,32,1024]{2,1,0:T(8,128)(2,1)S(1)}, bf16[16,32,1024]{2,1,0:T(8,128)(2,1)S(1)}, u32[]{:S(2)}, u32[]{:S(2)}) collective-permute-start(bf16[16,32,1024]{2,1,0:T(8,128)(2,1)S(1)} %all-to-all-done.slabs.q_own), channel_id=1, source_target_pairs={{0,4},{4,0},{1,5},{5,1},{2,6},{6,2},{3,7},{7,3},{8,12},{12,8},{9,1... | collective-permute-start | bytes 3145736 | tf_op jit(solution)/shard_map/ppermute | solution.py:207
  39.0 21.5 %all-to-all-start.1 = ((bf16[16,32,1024]{2,1,0:T(8,128)(2,1)}), bf16[16,32,1024]{2,1,0:T(8,128)(2,1)S(1)}, u32[]{:S(2)}, u32[]{:S(2)}) async-start(bf16[16,32,1024]{2,1,0:T(8,128)(2,1)} %pack_in.1), calls=%async_computation.1 | async-start | bytes 2097152 | tf_op jit(solution)/shard_map/all_to_all | solution.py:255
  42.7 3.4 %collective-permute-start.3 = (bf16[16,144,128]{2,1,0:T(8,128)(2,1)}, bf16[16,144,128]{2,1,0:T(8,128)(2,1)}, u32[]{:S(2)}, u32[]{:S(2)}) collective-permute-start(bf16[16,144,128]{2,1,0:T(8,128)(2,1)} %copy-done.13), channel_id=1, source_target_pairs={{0,4},{4,0},{1,5},{5,1},{2,6},{6,2},{3,7},{7,3},{8,12},{12,8},{9,1... | collective-permute-start | bytes 1769480 | tf_op jit(solution)/shard_map/ppermute | solution.py:207
  43.3 2.8 %copy-start.4 = (f32[16,144,128]{2,1,0:T(8,128)S(1)}, f32[16,144,128]{2,1,0:T(8,128)}, u32[]{:S(2)}) copy-start(f32[16,144,128]{2,1,0:T(8,128)} %copy-done.3) | copy-start | bytes 3538948
  44.1 2.0 %collective-permute-start.5 = (f32[8,128]{1,0:T(8,128)S(1)}, f32[8,128]{1,0:T(8,128)S(1)}, u32[]{:S(2)}, u32[]{:S(2)}) collective-permute-start(f32[8,128]{1,0:T(8,128)S(1)} %get-tuple-element.39.inner), channel_id=1, source_target_pairs={{0,4},{4,0},{1,5},{5,1},{2,6},{6,2},{3,7},{7,3},{8,12},{12,8},{9,1... | collective-permute-start | bytes 12296 | tf_op jit(solution)/shard_map/ppermute | solution.py:207
  48.2 39.3 %copy-start.2 = (f32[1024,128]{1,0:T(8,128)S(1)}, f32[1024,128]{1,0:T(8,128)}, u32[]{:S(2)}) copy-start(f32[1024,128]{1,0:T(8,128)} %copy-done.1) | copy-start | bytes 1572868
  60.5 14.5 %all-to-all-start.2 = ((bf16[16,144,128]{2,1,0:T(8,128)(2,1)}), bf16[16,144,128]{2,1,0:T(8,128)(2,1)S(1)}, u32[]{:S(2)}, u32[]{:S(2)}) async-start(bf16[16,144,128]{2,1,0:T(8,128)(2,1)} %pack_out.1), calls=%async_computation.2 | async-start | bytes 1179648 | tf_op jit(solution)/shard_map/all_to_all | solution.py:281
  64.3 11.5 %collective-permute-start.6 = (f32[16,1024]{1,0:T(8,128)S(1)}, f32[16,1024]{1,0:T(8,128)S(1)}, u32[]{:S(2)}, u32[]{:S(2)}) collective-permute-start(f32[16,1024]{1,0:T(8,128)S(1)} %get-tuple-element.45), channel_id=1, source_target_pairs={{0,32},{32,0},{1,33},{33,1},{2,34},{34,2},{3,35},{35,3},{4,36},{36... | collective-permute-start | bytes 196616 | tf_op jit(solution)/shard_map/ppermute | solution.py:207
  75.8 11.7 %all-to-all-start.3 = ((f32[8,40,128]{2,1,0:T(8,128)}), f32[8,40,128]{2,1,0:T(8,128)S(1)}, u32[]{:S(2)}, u32[]{:S(2)}) async-start(f32[8,40,128]{2,1,0:T(8,128)} %unpack_out.1), calls=%async_computation.3 | async-start | bytes 327680 | tf_op jit(solution)/shard_map/all_to_all | solution.py:286
  (3 other events, 2.3 us)

commit v9 on v8

--- a/solution.py
+++ b/solution.py
@@ -62,7 +62,7 @@
     dp, core, _ = counted()
     first = core == 0
     live = lax.broadcasted_iota(jnp.int32, (tokens.shape[0], 256), 0) < counts[dp]
-    for x in range(2):
+    for x in range(send.shape[0] // 4):
         cols = slice((start + x) * 256, (start + x) * 256 + 256)
         some = jnp.where(live, tokens[:, cols], jnp.zeros((), bf16))
         part = dot(some, tokens[...], 0, 0)
@@ -80,16 +80,18 @@
 
 
 def cov_in_second_kernel(*refs):
-    cov_in_rows(*refs, 2)
+    cov_in_rows(*refs, 3)
 
 
 def pack_in_kernel(keep_one, recv_one, keep_two, recv_two, msg):
     def step(s, _):
-        msg[s] = (keep_one[s] + recv_one[s].astype(f32)).astype(bf16)
-        msg[8 + s] = (keep_two[s] + recv_two[s].astype(f32)).astype(bf16)
+        for at in range(3):
+            to = at * 4 + s
+            msg[to] = (keep_one[to] + recv_one[to].astype(f32)).astype(bf16)
+        msg[12 + s] = (keep_two[s] + recv_two[s].astype(f32)).astype(bf16)
         return 0
 
-    lax.fori_loop(0, 8, step, 0)
+    lax.fori_loop(0, 4, step, 0)
 
 
 def pack_out_kernel(keep, recv, inner, other_inner, msg):
@@ -223,14 +225,15 @@
     shape = jax.ShapeDtypeStruct
     mine = basis_in[0]
     slabs = jnp.concatenate([mine, swap(mine, "zh")], axis=0)
-    half = [shape((8, 32, 1024), bf16), shape((8, 32, 1024), f32)]
-    send_one, keep_one = on_chip(cov_in_first_kernel, half, 1 << 30, token_counts, activations)
+    most = [shape((12, 32, 1024), bf16), shape((12, 32, 1024), f32)]
+    rest = [shape((4, 32, 1024), bf16), shape((4, 32, 1024), f32)]
+    send_one, keep_one = on_chip(cov_in_first_kernel, most, 1 << 30, token_counts, activations)
     slabs, send_one, counts = lax.optimization_barrier((slabs, send_one, token_counts))
     q_own = lax.all_to_all(
         jnp.broadcast_to(slabs[None], (16,) + slabs.shape), PLANE, 0, 0, tiled=True
     )
     recv_one = swap(send_one, "core")
-    send_two, keep_two = on_chip(cov_in_second_kernel, half, 1 << 30, counts, activations)
+    send_two, keep_two = on_chip(cov_in_second_kernel, rest, 1 << 30, counts, activations)
     recv_two = swap(send_two, "core")
     folded = (16, ROWS_OUT + ROWS_EXTRA, 128)
     send_out, keep_out = on_chip(

time: 90.5 us -> 90.9 us (level)
  no operation moved by 1% of the time
where the time goes in v9:
time: 90.9 us; the launch traced here: 89.7 us
  starting transfers between devices  32.9 us (36%)
  waiting for transfers between devices  28.5 us (31%)
  Pallas kernels  14.8 us (16%)
  local copies, waits for them, and re-layouts  9.93 us (11%)
  between operations  2.13 us (2%)
  other arithmetic  1.35 us (1%)
    ppermute x7, starting transfers between devices, swap(): return lax.ppermute(array, axis, [(0, 1), (1, 0)])  15.4 us
    pallas_call x11, Pallas kernels, on_chip(): pl.pallas_call(kernel, in_specs=[whole if a.ndim > 1 else pl.BlockSpec(me...  14.8 us
    all_to_all x1, waiting for transfers between devices, local(): got_in = lax.all_to_all(msg_in, PLANE, 0, 0, tiled=True)  12.3 us
    unnamed x32, local copies, waits for them, and re-layouts  8.69 us
    all_to_all x1, waiting for transfers between devices, local(): column = lax.all_to_all(column, COLUMN, 0, 0, tiled=True)  7.67 us
    all_to_all x1, starting transfers between devices, local(): lax.all_to_all(jnp.broadcast_to(slabs[None], (16,) + slabs.shape), PLANE,...  6.75 us
    all_to_all x1, waiting for transfers between devices, local(): got_out = lax.all_to_all(msg_out, PLANE, 0, 0, tiled=True)  6.5 us
    all_to_all x1, starting transfers between devices, local(): got_in = lax.all_to_all(msg_in, PLANE, 0, 0, tiled=True)  3.65 us
  transfers between devices with their start and end apart: 11, of which 4 were waited for; matrix products, arithmetic and copies ran while one was open for 2% of the time, Pallas kernels for 15%

profile of v9, /device:TPU:1, one launch (start us, length us, event | category | flops | bytes accessed | tf_op | source)
XLA Modules:
  0.0 89.7 jit_solution(5386861483148115987)
XLA Ops:
  0.6 7.8 %collective-permute-start = (bf16[16,1024]{1,0:T(8,128)(2,1)}, bf16[16,1024]{1,0:T(8,128)(2,1)S(1)}, u32[]{:S(2)}, u32[]{:S(2)}) collective-permute-start(bf16[16,1024]{1,0:T(8,128)(2,1)} %bitcast.9), channel_id=1, source_target_pairs={{0,32},{32,0},{1,33},{33,1},{2,34},{34,2},{3,35},{35,3},{4,36},{36... | collective-permute-start | bytes 98312 | tf_op jit(solution)/shard_map/ppermute | solution.py:209
  9.1 1.6 %copy-done.11 = bf16[1024,1024]{1,0:T(8,128)(2,1)S(1)} copy-done((bf16[1024,1024]{1,0:T(8,128)(2,1)S(1)}, bf16[1024,1024]{1,0:T(8,128)(2,1)}, u32[]{:S(2)}) %copy-start.11) | copy-done | bytes 2097176
  10.7 2.4 %cov_in_first.1 = (bf16[12,32,1024]{2,1,0:T(8,128)(2,1)S(1)}, f32[12,32,1024]{2,1,0:T(8,128)S(1)}) custom-call(s32[64]{0:T(128)S(1)} %copy-done.9, bf16[1024,1024]{1,0:T(8,128)(2,1)S(1)} %copy-done.11), custom_call_target="tpu_custom_call" | custom-call | flops 1073741824 | bytes 2097408 | tf_op jit(solution)/shard_map/cov_in_first/pallas_call | solution.py:166
  13.2 1.1 %broadcast_in_dim.15 = bf16[16,32,1024]{2,1,0:T(8,128)(2,1)} broadcast(bf16[32,1024]{1,0:T(8,128)(2,1)S(1)} %pad_maximum_fusion), dimensions={1,2} | broadcast | bytes 1114112 | tf_op jit(solution)/shard_map/broadcast_in_dim | solution.py:233
  14.3 6.8 %all-to-all-start = ((bf16[16,32,1024]{2,1,0:T(8,128)(2,1)}), bf16[16,32,1024]{2,1,0:T(8,128)(2,1)S(1)}, u32[]{:S(2)}, u32[]{:S(2)}) async-start(bf16[16,32,1024]{2,1,0:T(8,128)(2,1)} %broadcast_in_dim.15), calls=%async_computation | async-start | bytes 2097152 | tf_op jit(solution)/shard_map/all_to_all | solution.py:232
  21.1 1.3 %collective-permute-start.1 = (bf16[12,32,1024]{2,1,0:T(8,128)(2,1)S(1)}, bf16[12,32,1024]{2,1,0:T(8,128)(2,1)S(1)}, u32[]{:S(2)}, u32[]{:S(2)}) collective-permute-start(bf16[12,32,1024]{2,1,0:T(8,128)(2,1)S(1)} %get-tuple-element.30), channel_id=1, source_target_pairs={{0,4},{4,0},{1,5},{5,1},{2,6},{6,2},{3,7},{7,3},{8,12},{12,8},{9,1... | collective-permute-start | bytes 2359304 | tf_op jit(solution)/shard_map/ppermute | solution.py:209
  22.4 1.6 %copy-done.12 = bf16[1024,1024]{1,0:T(8,128)(2,1)S(1)} copy-done((bf16[1024,1024]{1,0:T(8,128)(2,1)S(1)}, bf16[1024,1024]{1,0:T(8,128)(2,1)}, u32[]{:S(2)}) %copy-start.12) | copy-done | bytes 2097176
  24.0 1.3 %cov_in_second.1 = (bf16[4,32,1024]{2,1,0:T(8,128)(2,1)S(1)}, f32[4,32,1024]{2,1,0:T(8,128)S(1)}) custom-call(s32[64]{0:T(128)S(1)} %copy-done.10, bf16[1024,1024]{1,0:T(8,128)(2,1)S(1)} %copy-done.12), custom_call_target="tpu_custom_call" | custom-call | flops 1073741824 | bytes 2097408 | tf_op jit(solution)/shard_map/cov_in_second/pallas_call | solution.py:166
  25.4 2.2 %copy-done = bf16[256,8192]{1,0:T(8,128)(2,1)S(1)} copy-done((bf16[256,8192]{1,0:T(8,128)(2,1)S(1)}, bf16[256,8192]{1,0:T(8,128)(2,1)}, u32[]{:S(2)}) %copy-start) | copy-done | bytes 4194328
  27.6 3.6 %cov_out.1 = (bf16[16,144,128]{2,1,0:T(8,128)(2,1)S(1)}, f32[16,144,128]{2,1,0:T(8,128)S(1)}) custom-call(s32[64]{0:T(128)S(1)} %copy-done.8, s32[64]{0:T(128)S(1)} %copy-done.10, bf16[256,8192]{1,0:T(8,128)(2,1)S(1)} %copy-done), custom_call_target="tpu_custom_call" | custom-call | flops 1073741824 | bytes 4194816 | tf_op jit(solution)/shard_map/cov_out/pallas_call | solution.py:166
  31.2 1.0 %copy-done.3 = f32[16,144,128]{2,1,0:T(8,128)} copy-done((f32[16,144,128]{2,1,0:T(8,128)}, f32[16,144,128]{2,1,0:T(8,128)S(1)}, u32[]{:S(2)}) %copy-start.3) | copy-done | bytes 1179672
  32.3 0.8 copy-done.13
  33.1 1.2 %pack_in.1 = bf16[16,32,1024]{2,1,0:T(8,128)(2,1)} custom-call(f32[12,32,1024]{2,1,0:T(8,128)S(1)} %get-tuple-element.29.keep_one, bf16[12,32,1024]{2,1,0:T(8,128)(2,1)S(1)} %collective-permute-done.1.recv_one, f32[4,32,1024]{2,1,0:T(8,128)S(1)} %get-tuple-element.32.keep_two, bf16[4,32,1024]{2,1,0:T(8,128)(2,1)S(1)} %collective-permute-done.2.recv_two), custom_call_target="tpu_custom_call" | custom-call | flops 1024 | bytes 3145728 | tf_op jit(solution)/shard_map/pack_in/pallas_call | solution.py:166
  34.3 2.0 %all-to-all-done.slabs.q_own = bf16[16,32,1024]{2,1,0:T(8,128)(2,1)S(1)} async-done(((bf16[16,32,1024]{2,1,0:T(8,128)(2,1)}), bf16[16,32,1024]{2,1,0:T(8,128)(2,1)S(1)}, u32[]{:S(2)}, u32[]{:S(2)}) %all-to-all-start) | async-done | bytes 1048608 | tf_op jit(solution)/shard_map/all_to_all | solution.py:232
  36.3 3.2 %collective-permute-start.4 = (bf16[16,32,1024]{2,1,0:T(8,128)(2,1)S(1)}, bf16[16,32,1024]{2,1,0:T(8,128)(2,1)S(1)}, u32[]{:S(2)}, u32[]{:S(2)}) collective-permute-start(bf16[16,32,1024]{2,1,0:T(8,128)(2,1)S(1)} %all-to-all-done.slabs.q_own), channel_id=1, source_target_pairs={{0,4},{4,0},{1,5},{5,1},{2,6},{6,2},{3,7},{7,3},{8,12},{12,8},{9,1... | collective-permute-start | bytes 3145736 | tf_op jit(solution)/shard_map/ppermute | solution.py:209
  39.5 3.7 %all-to-all-start.1 = ((bf16[16,32,1024]{2,1,0:T(8,128)(2,1)}), bf16[16,32,1024]{2,1,0:T(8,128)(2,1)S(1)}, u32[]{:S(2)}, u32[]{:S(2)}) async-start(bf16[16,32,1024]{2,1,0:T(8,128)(2,1)} %pack_in.1), calls=%async_computation.1 | async-start | bytes 2097152 | tf_op jit(solution)/shard_map/all_to_all | solution.py:258
  46.7 2.1 %pack_out.1 = bf16[16,144,128]{2,1,0:T(8,128)(2,1)} custom-call(f32[16,144,128]{2,1,0:T(8,128)S(1)} %copy-done.4, bf16[16,144,128]{2,1,0:T(8,128)(2,1)} %collective-permute-done.3.recv, f32[8,128]{1,0:T(8,128)S(1)} %get-tuple-element.39.inner, f32[8,128]{1,0:T(8,128)S(1)} %collective-permute-done.5.other_inner), custom_call_target="tpu_custom_call" | custom-call | flops 1024 | bytes 1777664 | tf_op jit(solution)/shard_map/pack_out/pallas_call | solution.py:166
  48.8 12.3 %all-to-all-done.1.msg = bf16[16,32,1024]{2,1,0:T(8,128)(2,1)S(1)} async-done(((bf16[16,32,1024]{2,1,0:T(8,128)(2,1)}), bf16[16,32,1024]{2,1,0:T(8,128)(2,1)S(1)}, u32[]{:S(2)}, u32[]{:S(2)}) %all-to-all-start.1) | async-done | bytes 1048608 | tf_op jit(solution)/shard_map/all_to_all | solution.py:258
  61.1 3.6 %all-to-all-start.2 = ((bf16[16,144,128]{2,1,0:T(8,128)(2,1)}), bf16[16,144,128]{2,1,0:T(8,128)(2,1)S(1)}, u32[]{:S(2)}, u32[]{:S(2)}) async-start(bf16[16,144,128]{2,1,0:T(8,128)(2,1)} %pack_out.1), calls=%async_computation.2 | async-start | bytes 1179648 | tf_op jit(solution)/shard_map/all_to_all | solution.py:284
  64.8 2.3 %collective-permute-start.6 = (f32[16,1024]{1,0:T(8,128)S(1)}, f32[16,1024]{1,0:T(8,128)S(1)}, u32[]{:S(2)}, u32[]{:S(2)}) collective-permute-start(f32[16,1024]{1,0:T(8,128)S(1)} %get-tuple-element.45), channel_id=1, source_target_pairs={{0,32},{32,0},{1,33},{33,1},{2,34},{34,2},{3,35},{35,3},{4,36},{36... | collective-permute-start | bytes 196616 | tf_op jit(solution)/shard_map/ppermute | solution.py:209
  69.1 6.5 %all-to-all-done.2.msg = bf16[16,144,128]{2,1,0:T(8,128)(2,1)S(1)} async-done(((bf16[16,144,128]{2,1,0:T(8,128)(2,1)}), bf16[16,144,128]{2,1,0:T(8,128)(2,1)S(1)}, u32[]{:S(2)}, u32[]{:S(2)}) %all-to-all-start.2) | async-done | bytes 589856 | tf_op jit(solution)/shard_map/all_to_all | solution.py:284
  76.4 3.5 %all-to-all-start.3 = ((f32[8,40,128]{2,1,0:T(8,128)}), f32[8,40,128]{2,1,0:T(8,128)S(1)}, u32[]{:S(2)}, u32[]{:S(2)}) async-start(f32[8,40,128]{2,1,0:T(8,128)} %unpack_out.1), calls=%async_computation.3 | async-start | bytes 327680 | tf_op jit(solution)/shard_map/all_to_all | solution.py:289
  80.6 7.7 %all-to-all-done.3.column = f32[8,40,128]{2,1,0:T(8,128)S(1)} async-done(((f32[8,40,128]{2,1,0:T(8,128)}), f32[8,40,128]{2,1,0:T(8,128)S(1)}, u32[]{:S(2)}, u32[]{:S(2)}) %all-to-all-start.3) | async-done | bytes 163872 | tf_op jit(solution)/shard_map/all_to_all | solution.py:289
  88.3 1.4 %clip.1 = (f32[1,32,128]{2,1,0:T(8,128)}, f32[1024,128]{1,0:T(8,128)}) custom-call(f32[2]{0:T(128)S(1)} %pad_maximum_fusion.1.scalars, f32[8,40,128]{2,1,0:T(8,128)S(1)} %all-to-all-done.3.column, f32[1024,128]{1,0:T(8,128)S(1)} %copy-done.2), custom_call_target="tpu_custom_call" | custom-call | flops 1048576 | bytes 688136 | tf_op jit(solution)/shard_map/clip/pallas_call | solution.py:166
  (47 shorter events, 6.5 us)
Async XLA Ops:
  0.6 12.5 %collective-permute-start = (bf16[16,1024]{1,0:T(8,128)(2,1)}, bf16[16,1024]{1,0:T(8,128)(2,1)S(1)}, u32[]{:S(2)}, u32[]{:S(2)}) collective-permute-start(bf16[16,1024]{1,0:T(8,128)(2,1)} %bitcast.9), channel_id=1, source_target_pairs={{0,32},{32,0},{1,33},{33,1},{2,34},{34,2},{3,35},{35,3},{4,36},{36... | collective-permute-start | bytes 98312 | tf_op jit(solution)/shard_map/ppermute | solution.py:209
  9.1 1.6 %copy-start.11 = (bf16[1024,1024]{1,0:T(8,128)(2,1)S(1)}, bf16[1024,1024]{1,0:T(8,128)(2,1)}, u32[]{:S(2)}) copy-start(bf16[1024,1024]{1,0:T(8,128)(2,1)} %refs_1_.3) | copy-start | bytes 6291460
  10.7 2.4 %copy-start.14 = (bf16[1,16,1024]{2,1,0:T(8,128)(2,1)S(1)}, bf16[1,16,1024]{2,1,0:T(8,128)(2,1)}, u32[]{:S(2)}) copy-start(bf16[1,16,1024]{2,1,0:T(8,128)(2,1)} %param.14) | copy-start | bytes 98308
  13.1 9.3 %copy-start.10 = (s32[64]{0:T(128)S(1)}, s32[64]{0:T(128)}, u32[]{:S(2)}) copy-start(s32[64]{0:T(128)} %counts) | copy-start | bytes 772
  14.3 22.0 %all-to-all-start = ((bf16[16,32,1024]{2,1,0:T(8,128)(2,1)}), bf16[16,32,1024]{2,1,0:T(8,128)(2,1)S(1)}, u32[]{:S(2)}, u32[]{:S(2)}) async-start(bf16[16,32,1024]{2,1,0:T(8,128)(2,1)} %broadcast_in_dim.15), calls=%async_computation | async-start | bytes 2097152 | tf_op jit(solution)/shard_map/all_to_all | solution.py:232
  21.0 4.4 %copy-start.8 = (s32[64]{0:T(128)S(1)}, s32[64]{0:T(128)}, u32[]{:S(2)}) copy-start(s32[64]{0:T(128)} %owners.1) | copy-start | bytes 772
  21.1 12.0 %collective-permute-start.1 = (bf16[12,32,1024]{2,1,0:T(8,128)(2,1)S(1)}, bf16[12,32,1024]{2,1,0:T(8,128)(2,1)S(1)}, u32[]{:S(2)}, u32[]{:S(2)}) collective-permute-start(bf16[12,32,1024]{2,1,0:T(8,128)(2,1)S(1)} %get-tuple-element.30), channel_id=1, source_target_pairs={{0,4},{4,0},{1,5},{5,1},{2,6},{6,2},{3,7},{7,3},{8,12},{12,8},{9,1... | collective-permute-start | bytes 2359304 | tf_op jit(solution)/shard_map/ppermute | solution.py:209
  22.4 1.6 %copy-start.12 = (bf16[1024,1024]{1,0:T(8,128)(2,1)S(1)}, bf16[1024,1024]{1,0:T(8,128)(2,1)}, u32[]{:S(2)}) copy-start(bf16[1024,1024]{1,0:T(8,128)(2,1)} %refs_1_.3) | copy-start | bytes 6291460
  25.3 7.8 %collective-permute-start.2 = (bf16[4,32,1024]{2,1,0:T(8,128)(2,1)S(1)}, bf16[4,32,1024]{2,1,0:T(8,128)(2,1)S(1)}, u32[]{:S(2)}, u32[]{:S(2)}) collective-permute-start(bf16[4,32,1024]{2,1,0:T(8,128)(2,1)S(1)} %get-tuple-element.33), channel_id=1, source_target_pairs={{0,4},{4,0},{1,5},{5,1},{2,6},{6,2},{3,7},{7,3},{8,12},{12,8},{9,1... | collective-permute-start | bytes 786440 | tf_op jit(solution)/shard_map/ppermute | solution.py:209
  25.4 2.2 %copy-start = (bf16[256,8192]{1,0:T(8,128)(2,1)S(1)}, bf16[256,8192]{1,0:T(8,128)(2,1)}, u32[]{:S(2)}) copy-start(bf16[256,8192]{1,0:T(8,128)(2,1)} %tokens.1) | copy-start | bytes 12582916
  31.2 1.0 %copy-start.3 = (f32[16,144,128]{2,1,0:T(8,128)}, f32[16,144,128]{2,1,0:T(8,128)S(1)}, u32[]{:S(2)}) copy-start(f32[16,144,128]{2,1,0:T(8,128)S(1)} %get-tuple-element.36.keep) | copy-start | bytes 3538948
  34.3 9.0 %copy-start.15 = (f32[128]{0:T(128)S(1)}, f32[128]{0:T(128)}, u32[]{:S(2)}) copy-start(f32[128]{0:T(128)} %param.17) | copy-start | bytes 1540
  34.3 9.2 %copy-start.5 = (bf16[1024,128]{1,0:T(8,128)(2,1)S(1)}, bf16[1024,128]{1,0:T(8,128)(2,1)}, u32[]{:S(2)}) copy-start(bf16[1024,128]{1,0:T(8,128)(2,1)} %grad.3) | copy-start | bytes 786436
  34.3 9.5 %copy-start.6 = (bf16[1,128,128]{2,1,0:T(8,128)(2,1)S(1)}, bf16[1,128,128]{2,1,0:T(8,128)(2,1)}, u32[]{:S(2)}) copy-start(bf16[1,128,128]{2,1,0:T(8,128)(2,1)} %param.15) | copy-start | bytes 98308
  34.3 9.5 %copy-start.7 = (f32[1024]{0:T(1024)S(1)}, f32[1024]{0:T(1024)}, u32[]{:S(2)}) copy-start(f32[1024]{0:T(1024)} %param.16) | copy-start | bytes 12292
  36.3 7.5 %collective-permute-start.4 = (bf16[16,32,1024]{2,1,0:T(8,128)(2,1)S(1)}, bf16[16,32,1024]{2,1,0:T(8,128)(2,1)S(1)}, u32[]{:S(2)}, u32[]{:S(2)}) collective-permute-start(bf16[16,32,1024]{2,1,0:T(8,128)(2,1)S(1)} %all-to-all-done.slabs.q_own), channel_id=1, source_target_pairs={{0,4},{4,0},{1,5},{5,1},{2,6},{6,2},{3,7},{7,3},{8,12},{12,8},{9,1... | collective-permute-start | bytes 3145736 | tf_op jit(solution)/shard_map/ppermute | solution.py:209
  39.5 21.5 %all-to-all-start.1 = ((bf16[16,32,1024]{2,1,0:T(8,128)(2,1)}), bf16[16,32,1024]{2,1,0:T(8,128)(2,1)S(1)}, u32[]{:S(2)}, u32[]{:S(2)}) async-start(bf16[16,32,1024]{2,1,0:T(8,128)(2,1)} %pack_in.1), calls=%async_computation.1 | async-start | bytes 2097152 | tf_op jit(solution)/shard_map/all_to_all | solution.py:258
  43.2 3.4 %collective-permute-start.3 = (bf16[16,144,128]{2,1,0:T(8,128)(2,1)}, bf16[16,144,128]{2,1,0:T(8,128)(2,1)}, u32[]{:S(2)}, u32[]{:S(2)}) collective-permute-start(bf16[16,144,128]{2,1,0:T(8,128)(2,1)} %copy-done.13), channel_id=1, source_target_pairs={{0,4},{4,0},{1,5},{5,1},{2,6},{6,2},{3,7},{7,3},{8,12},{12,8},{9,1... | collective-permute-start | bytes 1769480 | tf_op jit(solution)/shard_map/ppermute | solution.py:209
  43.8 2.8 %copy-start.4 = (f32[16,144,128]{2,1,0:T(8,128)S(1)}, f32[16,144,128]{2,1,0:T(8,128)}, u32[]{:S(2)}) copy-start(f32[16,144,128]{2,1,0:T(8,128)} %copy-done.3) | copy-start | bytes 3538948
  44.6 2.0 %collective-permute-start.5 = (f32[8,128]{1,0:T(8,128)S(1)}, f32[8,128]{1,0:T(8,128)S(1)}, u32[]{:S(2)}, u32[]{:S(2)}) collective-permute-start(f32[8,128]{1,0:T(8,128)S(1)} %get-tuple-element.39.inner), channel_id=1, source_target_pairs={{0,4},{4,0},{1,5},{5,1},{2,6},{6,2},{3,7},{7,3},{8,12},{12,8},{9,1... | collective-permute-start | bytes 12296 | tf_op jit(solution)/shard_map/ppermute | solution.py:209
  48.8 39.5 %copy-start.2 = (f32[1024,128]{1,0:T(8,128)S(1)}, f32[1024,128]{1,0:T(8,128)}, u32[]{:S(2)}) copy-start(f32[1024,128]{1,0:T(8,128)} %copy-done.1) | copy-start | bytes 1572868
  61.1 14.5 %all-to-all-start.2 = ((bf16[16,144,128]{2,1,0:T(8,128)(2,1)}), bf16[16,144,128]{2,1,0:T(8,128)(2,1)S(1)}, u32[]{:S(2)}, u32[]{:S(2)}) async-start(bf16[16,144,128]{2,1,0:T(8,128)(2,1)} %pack_out.1), calls=%async_computation.2 | async-start | bytes 1179648 | tf_op jit(solution)/shard_map/all_to_all | solution.py:284
  64.8 11.5 %collective-permute-start.6 = (f32[16,1024]{1,0:T(8,128)S(1)}, f32[16,1024]{1,0:T(8,128)S(1)}, u32[]{:S(2)}, u32[]{:S(2)}) collective-permute-start(f32[16,1024]{1,0:T(8,128)S(1)} %get-tuple-element.45), channel_id=1, source_target_pairs={{0,32},{32,0},{1,33},{33,1},{2,34},{34,2},{3,35},{35,3},{4,36},{36... | collective-permute-start | bytes 196616 | tf_op jit(solution)/shard_map/ppermute | solution.py:209
  76.4 11.9 %all-to-all-start.3 = ((f32[8,40,128]{2,1,0:T(8,128)}), f32[8,40,128]{2,1,0:T(8,128)S(1)}, u32[]{:S(2)}, u32[]{:S(2)}) async-start(f32[8,40,128]{2,1,0:T(8,128)} %unpack_out.1), calls=%async_computation.3 | async-start | bytes 327680 | tf_op jit(solution)/shard_map/all_to_all | solution.py:289
  (3 other events, 2.3 us)

commit v10 on v8

--- a/solution.py
+++ b/solution.py
@@ -151,11 +151,33 @@
             precond[rows, :] = result[s * 16 : s * 16 + 16]
 
 
-def clip_kernel(scalars, column, precond, cov_out, update):
+def clip_kernel(scalars, column, precond, cov_out, update, ready, sems):
     total = jnp.sum(column[...], axis=0)
+    rate = scalars[1]
+    factor = jnp.minimum(1.0, jnp.sqrt(kl_clip / (rate * rate * total[32:33])))
+    copies = []
+    for part in range(8):
+        rows = pl.ds(part * 128, 128)
+        ready[rows, :] = factor * precond[rows, :]
+        copies.append(pltpu.make_async_copy(ready.at[rows], update.at[rows], sems.at[part]))
+        copies[-1].start()
     cov_out[0] = total[0:32] / scalars[0]
-    rate = scalars[1]
-    update[...] = jnp.minimum(1.0, jnp.sqrt(kl_clip / (rate * rate * total[32:33]))) * precond[...]
+    for copy in copies:
+        copy.wait()
+
+
+def clip(scalars, column, precond):
+    whole = pl.BlockSpec(memory_space=pltpu.VMEM)
+    return pl.pallas_call(
+        clip_kernel,
+        in_specs=[pl.BlockSpec(memory_space=pltpu.SMEM), whole, whole],
+        out_specs=[whole, pl.BlockSpec(memory_space=pl.ANY)],
+        out_shape=[jax.ShapeDtypeStruct((1, 32, 128), f32), jax.ShapeDtypeStruct((1024, 128), f32)],
+        scratch_shapes=[pltpu.VMEM((1024, 128), f32), pltpu.SemaphoreType.DMA((8,))],
+        compiler_params=pltpu.CompilerParams(vmem_limit_bytes=VMEM),
+        cost_estimate=pl.CostEstimate(flops=1024, bytes_accessed=1024, transcendentals=0),
+        name="clip",
+    )(scalars, column, precond)
 
 
 def on_chip(kernel, outs, flops, *args):
@@ -285,14 +307,7 @@
     column, recv_slab = lax.optimization_barrier((column, recv_slab))
     column = lax.all_to_all(column, COLUMN, 0, 0, tiled=True)
     cov_in = ((keep_slab + recv_slab) / token_total)[None]
-    cov_out, update = on_chip(
-        clip_kernel,
-        [shape((1, 32, 128), f32), shape((1024, 128), f32)],
-        1 << 20,
-        jnp.stack([token_total, learning_rate[0]]),
-        column,
-        precond,
-    )
+    cov_out, update = clip(jnp.stack([token_total, learning_rate[0]]), column, precond)
     return (cov_in, cov_out, update)
 
 

time: 90.5 us -> 91.1 us (level)
    pallas_call x0 -> x1, Pallas kernels: none -> 2.02 us  [clip(): pl.pallas_call(clip_kernel, in_specs=[pl.BlockSpec(memory_space=pltpu.SME...]
    pallas_call x11 -> x10, Pallas kernels: 14.9 us -> 13.5 us  [on_chip(): pl.pallas_call(kernel, in_specs=[whole if a.ndim > 1 else pl.BlockSpec(me...]
where the time goes in v10:
time: 91.1 us; the launch traced here: 89.5 us
  starting transfers between devices  32.5 us (36%)
  waiting for transfers between devices  28.2 us (31%)
  Pallas kernels  15.5 us (17%)
  local copies, waits for them, and re-layouts  9.93 us (11%)
  between operations  2.14 us (2%)
  other arithmetic  1.36 us (1%)
    ppermute x7, starting transfers between devices, swap(): return lax.ppermute(array, axis, [(0, 1), (1, 0)])  15.1 us
    pallas_call x10, Pallas kernels, on_chip(): pl.pallas_call(kernel, in_specs=[whole if a.ndim > 1 else pl.BlockSpec(me...  13.5 us
    all_to_all x1, waiting for transfers between devices, local(): got_in = lax.all_to_all(msg_in, PLANE, 0, 0, tiled=True)  12.3 us
    unnamed x32, local copies, waits for them, and re-layouts  8.69 us
    all_to_all x1, waiting for transfers between devices, local(): column = lax.all_to_all(column, COLUMN, 0, 0, tiled=True)  7.57 us
    all_to_all x1, waiting for transfers between devices, local(): got_out = lax.all_to_all(msg_out, PLANE, 0, 0, tiled=True)  6.79 us
    all_to_all x1, starting transfers between devices, local(): lax.all_to_all(jnp.broadcast_to(slabs[None], (16,) + slabs.shape), PLANE,...  6.76 us
    all_to_all x1, starting transfers between devices, local(): got_in = lax.all_to_all(msg_in, PLANE, 0, 0, tiled=True)  3.65 us
  transfers between devices with their start and end apart: 11, of which 4 were waited for; matrix products, arithmetic and copies ran while one was open for 2% of the time, Pallas kernels for 15%

profile of v10, /device:TPU:1, one launch (start us, length us, event | category | flops | bytes accessed | tf_op | source)
XLA Modules:
  0.0 89.5 jit_solution(6710934969116885430)
XLA Ops:
  0.6 7.8 %collective-permute-start = (bf16[16,1024]{1,0:T(8,128)(2,1)}, bf16[16,1024]{1,0:T(8,128)(2,1)S(1)}, u32[]{:S(2)}, u32[]{:S(2)}) collective-permute-start(bf16[16,1024]{1,0:T(8,128)(2,1)} %bitcast.9), channel_id=1, source_target_pairs={{0,32},{32,0},{1,33},{33,1},{2,34},{34,2},{3,35},{35,3},{4,36},{36... | collective-permute-start | bytes 98312 | tf_op jit(solution)/shard_map/ppermute | solution.py:229
  9.1 1.6 %copy-done.11 = bf16[1024,1024]{1,0:T(8,128)(2,1)S(1)} copy-done((bf16[1024,1024]{1,0:T(8,128)(2,1)S(1)}, bf16[1024,1024]{1,0:T(8,128)(2,1)}, u32[]{:S(2)}) %copy-start.11) | copy-done | bytes 2097176
  10.7 1.9 %cov_in_first.1 = (bf16[8,32,1024]{2,1,0:T(8,128)(2,1)S(1)}, f32[8,32,1024]{2,1,0:T(8,128)S(1)}) custom-call(s32[64]{0:T(128)S(1)} %copy-done.9, bf16[1024,1024]{1,0:T(8,128)(2,1)S(1)} %copy-done.11), custom_call_target="tpu_custom_call" | custom-call | flops 1073741824 | bytes 2097408 | tf_op jit(solution)/shard_map/cov_in_first/pallas_call | solution.py:186
  12.6 1.1 %broadcast_in_dim.15 = bf16[16,32,1024]{2,1,0:T(8,128)(2,1)} broadcast(bf16[32,1024]{1,0:T(8,128)(2,1)S(1)} %pad_maximum_fusion), dimensions={1,2} | broadcast | bytes 1114112 | tf_op jit(solution)/shard_map/broadcast_in_dim | solution.py:252
  13.7 6.8 %all-to-all-start = ((bf16[16,32,1024]{2,1,0:T(8,128)(2,1)}), bf16[16,32,1024]{2,1,0:T(8,128)(2,1)S(1)}, u32[]{:S(2)}, u32[]{:S(2)}) async-start(bf16[16,32,1024]{2,1,0:T(8,128)(2,1)} %broadcast_in_dim.15), calls=%async_computation | async-start | bytes 2097152 | tf_op jit(solution)/shard_map/all_to_all | solution.py:251
  20.5 1.3 %collective-permute-start.1 = (bf16[8,32,1024]{2,1,0:T(8,128)(2,1)S(1)}, bf16[8,32,1024]{2,1,0:T(8,128)(2,1)S(1)}, u32[]{:S(2)}, u32[]{:S(2)}) collective-permute-start(bf16[8,32,1024]{2,1,0:T(8,128)(2,1)S(1)} %get-tuple-element.30), channel_id=1, source_target_pairs={{0,4},{4,0},{1,5},{5,1},{2,6},{6,2},{3,7},{7,3},{8,12},{12,8},{9,1... | collective-permute-start | bytes 1572872 | tf_op jit(solution)/shard_map/ppermute | solution.py:229
  21.8 1.6 %copy-done.12 = bf16[1024,1024]{1,0:T(8,128)(2,1)S(1)} copy-done((bf16[1024,1024]{1,0:T(8,128)(2,1)S(1)}, bf16[1024,1024]{1,0:T(8,128)(2,1)}, u32[]{:S(2)}) %copy-start.12) | copy-done | bytes 2097176
  23.4 1.9 %cov_in_second.1 = (bf16[8,32,1024]{2,1,0:T(8,128)(2,1)S(1)}, f32[8,32,1024]{2,1,0:T(8,128)S(1)}) custom-call(s32[64]{0:T(128)S(1)} %copy-done.10, bf16[1024,1024]{1,0:T(8,128)(2,1)S(1)} %copy-done.12), custom_call_target="tpu_custom_call" | custom-call | flops 1073741824 | bytes 2097408 | tf_op jit(solution)/shard_map/cov_in_second/pallas_call | solution.py:186
  25.4 2.2 %copy-done = bf16[256,8192]{1,0:T(8,128)(2,1)S(1)} copy-done((bf16[256,8192]{1,0:T(8,128)(2,1)S(1)}, bf16[256,8192]{1,0:T(8,128)(2,1)}, u32[]{:S(2)}) %copy-start) | copy-done | bytes 4194328
  27.6 3.6 %cov_out.1 = (bf16[16,144,128]{2,1,0:T(8,128)(2,1)S(1)}, f32[16,144,128]{2,1,0:T(8,128)S(1)}) custom-call(s32[64]{0:T(128)S(1)} %copy-done.8, s32[64]{0:T(128)S(1)} %copy-done.10, bf16[256,8192]{1,0:T(8,128)(2,1)S(1)} %copy-done), custom_call_target="tpu_custom_call" | custom-call | flops 1073741824 | bytes 4194816 | tf_op jit(solution)/shard_map/cov_out/pallas_call | solution.py:186
  31.3 1.0 %copy-done.3 = f32[16,144,128]{2,1,0:T(8,128)} copy-done((f32[16,144,128]{2,1,0:T(8,128)}, f32[16,144,128]{2,1,0:T(8,128)S(1)}, u32[]{:S(2)}) %copy-start.3) | copy-done | bytes 1179672
  32.3 0.8 copy-done.13
  33.1 1.2 %pack_in.1 = bf16[16,32,1024]{2,1,0:T(8,128)(2,1)} custom-call(f32[8,32,1024]{2,1,0:T(8,128)S(1)} %get-tuple-element.29.keep_one, bf16[8,32,1024]{2,1,0:T(8,128)(2,1)S(1)} %collective-permute-done.1.recv_one, f32[8,32,1024]{2,1,0:T(8,128)S(1)} %get-tuple-element.32.keep_two, bf16[8,32,1024]{2,1,0:T(8,128)(2,1)S(1)} %collective-permute-done.2.recv_two), custom_call_target="tpu_custom_call" | custom-call | flops 1024 | bytes 3145728 | tf_op jit(solution)/shard_map/pack_in/pallas_call | solution.py:186
  34.3 1.4 %all-to-all-done.slabs.q_own = bf16[16,32,1024]{2,1,0:T(8,128)(2,1)S(1)} async-done(((bf16[16,32,1024]{2,1,0:T(8,128)(2,1)}), bf16[16,32,1024]{2,1,0:T(8,128)(2,1)S(1)}, u32[]{:S(2)}, u32[]{:S(2)}) %all-to-all-start) | async-done | bytes 1048608 | tf_op jit(solution)/shard_map/all_to_all | solution.py:251
  35.8 3.2 %collective-permute-start.4 = (bf16[16,32,1024]{2,1,0:T(8,128)(2,1)S(1)}, bf16[16,32,1024]{2,1,0:T(8,128)(2,1)S(1)}, u32[]{:S(2)}, u32[]{:S(2)}) collective-permute-start(bf16[16,32,1024]{2,1,0:T(8,128)(2,1)S(1)} %all-to-all-done.slabs.q_own), channel_id=1, source_target_pairs={{0,4},{4,0},{1,5},{5,1},{2,6},{6,2},{3,7},{7,3},{8,12},{12,8},{9,1... | collective-permute-start | bytes 3145736 | tf_op jit(solution)/shard_map/ppermute | solution.py:229
  39.0 3.7 %all-to-all-start.1 = ((bf16[16,32,1024]{2,1,0:T(8,128)(2,1)}), bf16[16,32,1024]{2,1,0:T(8,128)(2,1)S(1)}, u32[]{:S(2)}, u32[]{:S(2)}) async-start(bf16[16,32,1024]{2,1,0:T(8,128)(2,1)} %pack_in.1), calls=%async_computation.1 | async-start | bytes 2097152 | tf_op jit(solution)/shard_map/all_to_all | solution.py:277
  46.1 2.1 %pack_out.1 = bf16[16,144,128]{2,1,0:T(8,128)(2,1)} custom-call(f32[16,144,128]{2,1,0:T(8,128)S(1)} %copy-done.4, bf16[16,144,128]{2,1,0:T(8,128)(2,1)} %collective-permute-done.3.recv, f32[8,128]{1,0:T(8,128)S(1)} %get-tuple-element.39.inner, f32[8,128]{1,0:T(8,128)S(1)} %collective-permute-done.5.other_inner), custom_call_target="tpu_custom_call" | custom-call | flops 1024 | bytes 1777664 | tf_op jit(solution)/shard_map/pack_out/pallas_call | solution.py:186
  48.2 12.3 %all-to-all-done.1.msg = bf16[16,32,1024]{2,1,0:T(8,128)(2,1)S(1)} async-done(((bf16[16,32,1024]{2,1,0:T(8,128)(2,1)}), bf16[16,32,1024]{2,1,0:T(8,128)(2,1)S(1)}, u32[]{:S(2)}, u32[]{:S(2)}) %all-to-all-start.1) | async-done | bytes 1048608 | tf_op jit(solution)/shard_map/all_to_all | solution.py:277
  60.5 3.6 %all-to-all-start.2 = ((bf16[16,144,128]{2,1,0:T(8,128)(2,1)}), bf16[16,144,128]{2,1,0:T(8,128)(2,1)S(1)}, u32[]{:S(2)}, u32[]{:S(2)}) async-start(bf16[16,144,128]{2,1,0:T(8,128)(2,1)} %pack_out.1), calls=%async_computation.2 | async-start | bytes 1179648 | tf_op jit(solution)/shard_map/all_to_all | solution.py:303
  64.3 2.0 %collective-permute-start.6 = (f32[16,1024]{1,0:T(8,128)S(1)}, f32[16,1024]{1,0:T(8,128)S(1)}, u32[]{:S(2)}, u32[]{:S(2)}) collective-permute-start(f32[16,1024]{1,0:T(8,128)S(1)} %get-tuple-element.45), channel_id=1, source_target_pairs={{0,32},{32,0},{1,33},{33,1},{2,34},{34,2},{3,35},{35,3},{4,36},{36... | collective-permute-start | bytes 196616 | tf_op jit(solution)/shard_map/ppermute | solution.py:229
  68.2 6.8 %all-to-all-done.2.msg = bf16[16,144,128]{2,1,0:T(8,128)(2,1)S(1)} async-done(((bf16[16,144,128]{2,1,0:T(8,128)(2,1)}), bf16[16,144,128]{2,1,0:T(8,128)(2,1)S(1)}, u32[]{:S(2)}, u32[]{:S(2)}) %all-to-all-start.2) | async-done | bytes 589856 | tf_op jit(solution)/shard_map/all_to_all | solution.py:303
  75.8 3.4 %all-to-all-start.3 = ((f32[8,40,128]{2,1,0:T(8,128)}), f32[8,40,128]{2,1,0:T(8,128)S(1)}, u32[]{:S(2)}, u32[]{:S(2)}) async-start(f32[8,40,128]{2,1,0:T(8,128)} %unpack_out.1), calls=%async_computation.3 | async-start | bytes 327680 | tf_op jit(solution)/shard_map/all_to_all | solution.py:308
  79.9 7.6 %all-to-all-done.3.column = f32[8,40,128]{2,1,0:T(8,128)S(1)} async-done(((f32[8,40,128]{2,1,0:T(8,128)}), f32[8,40,128]{2,1,0:T(8,128)S(1)}, u32[]{:S(2)}, u32[]{:S(2)}) %all-to-all-start.3) | async-done | bytes 163872 | tf_op jit(solution)/shard_map/all_to_all | solution.py:308
  87.5 2.0 %clip.1 = (f32[1,32,128]{2,1,0:T(8,128)}, f32[1024,128]{1,0:T(8,128)}) custom-call(f32[2]{0:T(128)S(1)} %pad_maximum_fusion.1.scalars, f32[8,40,128]{2,1,0:T(8,128)S(1)} %all-to-all-done.3.column, f32[1024,128]{1,0:T(8,128)S(1)} %copy-done.2), custom_call_target="tpu_custom_call" | custom-call | flops 1024 | bytes 1024 | tf_op jit(solution)/shard_map/clip/pallas_call | solution.py:171
  (47 shorter events, 6.5 us)
Async XLA Ops:
  0.6 12.0 %collective-permute-start = (bf16[16,1024]{1,0:T(8,128)(2,1)}, bf16[16,1024]{1,0:T(8,128)(2,1)S(1)}, u32[]{:S(2)}, u32[]{:S(2)}) collective-permute-start(bf16[16,1024]{1,0:T(8,128)(2,1)} %bitcast.9), channel_id=1, source_target_pairs={{0,32},{32,0},{1,33},{33,1},{2,34},{34,2},{3,35},{35,3},{4,36},{36... | collective-permute-start | bytes 98312 | tf_op jit(solution)/shard_map/ppermute | solution.py:229
  9.1 1.6 %copy-start.11 = (bf16[1024,1024]{1,0:T(8,128)(2,1)S(1)}, bf16[1024,1024]{1,0:T(8,128)(2,1)}, u32[]{:S(2)}) copy-start(bf16[1024,1024]{1,0:T(8,128)(2,1)} %refs_1_.3) | copy-start | bytes 6291460
  10.7 1.9 %copy-start.14 = (bf16[1,16,1024]{2,1,0:T(8,128)(2,1)S(1)}, bf16[1,16,1024]{2,1,0:T(8,128)(2,1)}, u32[]{:S(2)}) copy-start(bf16[1,16,1024]{2,1,0:T(8,128)(2,1)} %param.14) | copy-start | bytes 98308
  12.6 9.3 %copy-start.10 = (s32[64]{0:T(128)S(1)}, s32[64]{0:T(128)}, u32[]{:S(2)}) copy-start(s32[64]{0:T(128)} %counts) | copy-start | bytes 772
  13.7 22.0 %all-to-all-start = ((bf16[16,32,1024]{2,1,0:T(8,128)(2,1)}), bf16[16,32,1024]{2,1,0:T(8,128)(2,1)S(1)}, u32[]{:S(2)}, u32[]{:S(2)}) async-start(bf16[16,32,1024]{2,1,0:T(8,128)(2,1)} %broadcast_in_dim.15), calls=%async_computation | async-start | bytes 2097152 | tf_op jit(solution)/shard_map/all_to_all | solution.py:251
  20.5 4.9 %copy-start.8 = (s32[64]{0:T(128)S(1)}, s32[64]{0:T(128)}, u32[]{:S(2)}) copy-start(s32[64]{0:T(128)} %owners.1) | copy-start | bytes 772
  20.5 12.6 %collective-permute-start.1 = (bf16[8,32,1024]{2,1,0:T(8,128)(2,1)S(1)}, bf16[8,32,1024]{2,1,0:T(8,128)(2,1)S(1)}, u32[]{:S(2)}, u32[]{:S(2)}) collective-permute-start(bf16[8,32,1024]{2,1,0:T(8,128)(2,1)S(1)} %get-tuple-element.30), channel_id=1, source_target_pairs={{0,4},{4,0},{1,5},{5,1},{2,6},{6,2},{3,7},{7,3},{8,12},{12,8},{9,1... | collective-permute-start | bytes 1572872 | tf_op jit(solution)/shard_map/ppermute | solution.py:229
  21.8 1.6 %copy-start.12 = (bf16[1024,1024]{1,0:T(8,128)(2,1)S(1)}, bf16[1024,1024]{1,0:T(8,128)(2,1)}, u32[]{:S(2)}) copy-start(bf16[1024,1024]{1,0:T(8,128)(2,1)} %refs_1_.3) | copy-start | bytes 6291460
  25.3 7.8 %collective-permute-start.2 = (bf16[8,32,1024]{2,1,0:T(8,128)(2,1)S(1)}, bf16[8,32,1024]{2,1,0:T(8,128)(2,1)S(1)}, u32[]{:S(2)}, u32[]{:S(2)}) collective-permute-start(bf16[8,32,1024]{2,1,0:T(8,128)(2,1)S(1)} %get-tuple-element.33), channel_id=1, source_target_pairs={{0,4},{4,0},{1,5},{5,1},{2,6},{6,2},{3,7},{7,3},{8,12},{12,8},{9,1... | collective-permute-start | bytes 1572872 | tf_op jit(solution)/shard_map/ppermute | solution.py:229
  25.4 2.2 %copy-start = (bf16[256,8192]{1,0:T(8,128)(2,1)S(1)}, bf16[256,8192]{1,0:T(8,128)(2,1)}, u32[]{:S(2)}) copy-start(bf16[256,8192]{1,0:T(8,128)(2,1)} %tokens.1) | copy-start | bytes 12582916
  31.3 1.0 %copy-start.3 = (f32[16,144,128]{2,1,0:T(8,128)}, f32[16,144,128]{2,1,0:T(8,128)S(1)}, u32[]{:S(2)}) copy-start(f32[16,144,128]{2,1,0:T(8,128)S(1)} %get-tuple-element.36.keep) | copy-start | bytes 3538948
  34.3 8.4 %copy-start.15 = (f32[128]{0:T(128)S(1)}, f32[128]{0:T(128)}, u32[]{:S(2)}) copy-start(f32[128]{0:T(128)} %param.17) | copy-start | bytes 1540
  34.3 8.6 %copy-start.5 = (bf16[1024,128]{1,0:T(8,128)(2,1)S(1)}, bf16[1024,128]{1,0:T(8,128)(2,1)}, u32[]{:S(2)}) copy-start(bf16[1024,128]{1,0:T(8,128)(2,1)} %grad.3) | copy-start | bytes 786436
  34.3 8.9 %copy-start.6 = (bf16[1,128,128]{2,1,0:T(8,128)(2,1)S(1)}, bf16[1,128,128]{2,1,0:T(8,128)(2,1)}, u32[]{:S(2)}) copy-start(bf16[1,128,128]{2,1,0:T(8,128)(2,1)} %param.15) | copy-start | bytes 98308
  34.3 8.9 %copy-start.7 = (f32[1024]{0:T(1024)S(1)}, f32[1024]{0:T(1024)}, u32[]{:S(2)}) copy-start(f32[1024]{0:T(1024)} %param.16) | copy-start | bytes 12292
  35.8 7.5 %collective-permute-start.4 = (bf16[16,32,1024]{2,1,0:T(8,128)(2,1)S(1)}, bf16[16,32,1024]{2,1,0:T(8,128)(2,1)S(1)}, u32[]{:S(2)}, u32[]{:S(2)}) collective-permute-start(bf16[16,32,1024]{2,1,0:T(8,128)(2,1)S(1)} %all-to-all-done.slabs.q_own), channel_id=1, source_target_pairs={{0,4},{4,0},{1,5},{5,1},{2,6},{6,2},{3,7},{7,3},{8,12},{12,8},{9,1... | collective-permute-start | bytes 3145736 | tf_op jit(solution)/shard_map/ppermute | solution.py:229
  39.0 21.5 %all-to-all-start.1 = ((bf16[16,32,1024]{2,1,0:T(8,128)(2,1)}), bf16[16,32,1024]{2,1,0:T(8,128)(2,1)S(1)}, u32[]{:S(2)}, u32[]{:S(2)}) async-start(bf16[16,32,1024]{2,1,0:T(8,128)(2,1)} %pack_in.1), calls=%async_computation.1 | async-start | bytes 2097152 | tf_op jit(solution)/shard_map/all_to_all | solution.py:277
  42.7 3.4 %collective-permute-start.3 = (bf16[16,144,128]{2,1,0:T(8,128)(2,1)}, bf16[16,144,128]{2,1,0:T(8,128)(2,1)}, u32[]{:S(2)}, u32[]{:S(2)}) collective-permute-start(bf16[16,144,128]{2,1,0:T(8,128)(2,1)} %copy-done.13), channel_id=1, source_target_pairs={{0,4},{4,0},{1,5},{5,1},{2,6},{6,2},{3,7},{7,3},{8,12},{12,8},{9,1... | collective-permute-start | bytes 1769480 | tf_op jit(solution)/shard_map/ppermute | solution.py:229
  43.3 2.8 %copy-start.4 = (f32[16,144,128]{2,1,0:T(8,128)S(1)}, f32[16,144,128]{2,1,0:T(8,128)}, u32[]{:S(2)}) copy-start(f32[16,144,128]{2,1,0:T(8,128)} %copy-done.3) | copy-start | bytes 3538948
  44.1 2.0 %collective-permute-start.5 = (f32[8,128]{1,0:T(8,128)S(1)}, f32[8,128]{1,0:T(8,128)S(1)}, u32[]{:S(2)}, u32[]{:S(2)}) collective-permute-start(f32[8,128]{1,0:T(8,128)S(1)} %get-tuple-element.39.inner), channel_id=1, source_target_pairs={{0,4},{4,0},{1,5},{5,1},{2,6},{6,2},{3,7},{7,3},{8,12},{12,8},{9,1... | collective-permute-start | bytes 12296 | tf_op jit(solution)/shard_map/ppermute | solution.py:229
  48.2 39.3 %copy-start.2 = (f32[1024,128]{1,0:T(8,128)S(1)}, f32[1024,128]{1,0:T(8,128)}, u32[]{:S(2)}) copy-start(f32[1024,128]{1,0:T(8,128)} %copy-done.1) | copy-start | bytes 1572868
  60.5 14.5 %all-to-all-start.2 = ((bf16[16,144,128]{2,1,0:T(8,128)(2,1)}), bf16[16,144,128]{2,1,0:T(8,128)(2,1)S(1)}, u32[]{:S(2)}, u32[]{:S(2)}) async-start(bf16[16,144,128]{2,1,0:T(8,128)(2,1)} %pack_out.1), calls=%async_computation.2 | async-start | bytes 1179648 | tf_op jit(solution)/shard_map/all_to_all | solution.py:303
  64.3 11.5 %collective-permute-start.6 = (f32[16,1024]{1,0:T(8,128)S(1)}, f32[16,1024]{1,0:T(8,128)S(1)}, u32[]{:S(2)}, u32[]{:S(2)}) collective-permute-start(f32[16,1024]{1,0:T(8,128)S(1)} %get-tuple-element.45), channel_id=1, source_target_pairs={{0,32},{32,0},{1,33},{33,1},{2,34},{34,2},{3,35},{35,3},{4,36},{36... | collective-permute-start | bytes 196616 | tf_op jit(solution)/shard_map/ppermute | solution.py:229
  75.8 11.7 %all-to-all-start.3 = ((f32[8,40,128]{2,1,0:T(8,128)}), f32[8,40,128]{2,1,0:T(8,128)S(1)}, u32[]{:S(2)}, u32[]{:S(2)}) async-start(f32[8,40,128]{2,1,0:T(8,128)} %unpack_out.1), calls=%async_computation.3 | async-start | bytes 327680 | tf_op jit(solution)/shard_map/all_to_all | solution.py:308
  (3 other events, 2.3 us)
